TPU v7x, 256 devices: a whole 4x4x8 slice. The times are simulated.
256 devices in a mesh: clip: 4 (over y), band: 4 (over x_hi, core), chan: 16 (over x_lo, z).
Axes of the slice: x: 4 (x_hi: 2, x_lo: 2; x = x_hi * 2 + x_lo), y: 4, z: 8, core: 2. Of those that a mesh axis runs over, the one named last changes fastest.
Arguments:
- frames: bfloat16 [512, 4, 40960], P(None, 'clip', ('band', 'chan')), may hold values from -6 to 6
- weight: bfloat16 [512, 3, 3, 512], P('chan'), may hold values from -0.09375 to 0.09375
- bias: float32 [512], replicated, may hold values from -3 to 3
- cotangent: bfloat16 [512, 4, 40960], P(None, 'clip', ('band', 'chan')), may hold values from -6 to 6
Outputs:
- outputs: bfloat16 [512, 4, 40960], P(None, 'clip', ('band', 'chan'))
- grad_frames: bfloat16 [512, 4, 40960], P(None, 'clip', ('band', 'chan'))
- grad_weight: float32 [512, 3, 3, 512], P('chan')
- grad_bias: float32 [512], P('chan')
All inputs are finite; a program needn't handle non-finite values.
Results may differ from a plain program's by a relative error of at most 0.001.
Values may be sent and summed in bfloat16 or wider, within the bound.
No kernel may reach another device: no remote copies, remote signals or barrier semaphores. Data moves between devices by JAX's collectives and lax.ppermute only.
A program may use at most 128 MiB of HBM per device.

v0:
```python
import math

import jax
import jax.numpy as jnp
from jax import lax
from jax.sharding import PartitionSpec as P

W = 160


def padded(x, sides, width):
    for axis, dim in sides:
        peers, length = (lax.axis_size(axis), x.shape[dim])
        up = [(i, (i + 1) % peers) for i in range(peers - 1)]
        down = [(j, i) for i, j in up]
        last = lax.slice_in_dim(x, length - width, length, axis=dim)
        leading = lax.slice_in_dim(x, 0, width, axis=dim)
        before = lax.ppermute(last, axis, up)
        after = lax.ppermute(leading, axis, down)
        x = jnp.concatenate([before, x, after], axis=dim)
    return x


def shifted(source, start_at, cell_count, keep_mask):
    window = lax.slice_in_dim(source, start_at, start_at + cell_count, axis=2)
    return jnp.where(keep_mask[None, None, :], window, jnp.zeros_like(window))


def local(frames, weight, bias, cotangent):
    channels, frame_count, cell_count = frames.shape
    joined = lax.axis_size("band") * lax.axis_size("chan")
    scale = 1.0 / math.sqrt(frame_count * lax.axis_size("clip") * cell_count * joined)
    first_cell = lax.axis_index(("band", "chan")) * cell_count
    column = (first_cell + jnp.arange(cell_count, dtype=jnp.int32)) % W
    left_ok = column != 0
    right_ok = column != W - 1
    every_cell = column >= 0
    keep_masks = (left_ok, every_cell, right_ok)
    margin_cells = W + 1
    stacked = jnp.stack((frames, cotangent), axis=0)
    extended = padded(stacked, ((("band", "chan"), 3),), margin_cells)
    ext_input = extended[0]
    ext_upstream = extended[1]
    in_windows = []
    cot_windows = []
    for a in range(3):
        for b in range(3):
            offset = margin_cells + (a - 1) * W + (b - 1)
            in_windows.append(shifted(ext_input, offset, cell_count, keep_masks[b]))
            back_offset = margin_cells + (1 - a) * W + (1 - b)
            cot_windows.append(shifted(ext_upstream, back_offset, cell_count, keep_masks[2 - b]))
    tap_rows = []
    for a in range(3):
        tap_row = []
        for b in range(3):
            tap_row.append(
                jnp.einsum(
                    "ifs,ofs->oi",
                    in_windows[3 * a + b],
                    cotangent,
                    preferred_element_type=jnp.float32,
                )
            )
        tap_rows.append(jnp.stack(tap_row, axis=1))
    dw_local = jnp.stack(tap_rows, axis=1) * scale
    db_local = jnp.sum(cotangent.astype(jnp.float32), axis=(1, 2)) * scale
    start_out = jnp.zeros((channels, frame_count, cell_count), jnp.float32)
    start_grad = jnp.zeros((channels, frame_count, cell_count), jnp.float32)
    kernel = lax.all_gather(weight, "chan", axis=0, tiled=True)
    conv_sum = start_out
    grad_sum = start_grad
    for a in range(3):
        for b in range(3):
            conv_sum = conv_sum + jnp.einsum(
                "ifs,oi->ofs",
                in_windows[3 * a + b],
                kernel[:, a, b, :],
                preferred_element_type=jnp.float32,
            )
            grad_sum = grad_sum + jnp.einsum(
                "ofs,oi->ifs",
                cot_windows[3 * a + b],
                kernel[:, a, b, :],
                preferred_element_type=jnp.float32,
            )
    outputs = (conv_sum + bias[:, None, None]).astype(jnp.bfloat16)
    grad_frames = grad_sum.astype(jnp.bfloat16)
    dw_part, db_part = (
        lax.psum_scatter(dw_local, "chan", scatter_dimension=0, tiled=True),
        lax.psum_scatter(db_local, "chan", scatter_dimension=0, tiled=True),
    )
    grad_weight, grad_bias = lax.psum((dw_part, db_part), ("clip", "band"))
    return (outputs, grad_frames, grad_weight, grad_bias)


def solution(mesh):
    in_specs = (
        P(None, "clip", ("band", "chan")),
        P("chan", None, None, None),
        P(),
        P(None, "clip", ("band", "chan")),
    )
    out_specs = (
        P(None, "clip", ("band", "chan")),
        P(None, "clip", ("band", "chan")),
        P("chan", None, None, None),
        P("chan"),
    )
    return jax.shard_map(local, mesh=mesh, in_specs=in_specs, out_specs=out_specs, check_vma=False)
```

profile of v0, /device:TPU:1, one launch (start us, length us, event | category | flops | bytes accessed | tf_op | source)
XLA Modules:
  0.0 548.4 jit_solution(1162634151973713417)
XLA Ops:
  7.2 0.7 all-gather.2.cloned.1.call-update
  7.9 1.5 pad_maximum_fusion.2
  9.4 9.8 %collective-permute-start.1 = (bf16[2,512,1,161]{3,1,2,0:T(8,128)(2,1)S(1)}, bf16[2,512,1,161]{3,1,2,0:T(8,128)(2,1)S(1)}, u32[]{:S(2)}, u32[]{:S(2)}) collective-permute-start(bf16[2,512,1,161]{3,1,2,0:T(8,128)(2,1)S(1)} %get-tuple-element.15), channel_id=1, source_target_pairs={{1,0},{2,1},{3,2},{4,3},{5,4},{6,5},{7,6},{8,7},{9,8},{10,9},{11,1... | collective-permute-start | bytes 989192 | tf_op jit(solution)/shard_map/ppermute | solution.py:19
  19.2 1.9 collective-permute-start
  21.2 4.6 collective-permute-done.1
  25.8 19.1 %collective-permute-done = bf16[2,512,1,161]{3,1,2,0:T(8,128)(2,1)S(1)} collective-permute-done((bf16[2,512,1,161]{3,1,2,0:T(8,128)(2,1)S(1)}, bf16[2,512,1,161]{3,1,2,0:T(8,128)(2,1)S(1)}, u32[]{:S(2)}, u32[]{:S(2)}) %collective-permute-start) | collective-permute-done | bytes 329760 | tf_op jit(solution)/shard_map/ppermute | solution.py:18
  44.9 2.3 pad_maximum_fusion
  47.4 0.9 copy-done.1
  48.3 0.6 convolution_bitcast_fusion
  49.0 0.6 convolution_bitcast_fusion.1
  49.6 0.6 convolution_bitcast_fusion.2
  50.6 0.6 convolution_bitcast_fusion.3
  51.2 0.6 convolution_bitcast_fusion.4
  51.8 0.6 convolution_bitcast_fusion.5
  52.8 0.6 convolution_bitcast_fusion.6
  53.4 0.6 convolution_bitcast_fusion.7
  54.1 0.6 convolution_bitcast_fusion.8
  54.7 0.3 maximum_bitcast_fusion
  55.0 4.3 maximum_multiply_fusion
  59.3 13.9 %copy.11 = f32[512,3,3,512]{3,2,1,0:T(4,128)} copy(f32[512,3,3,512]{0,3,2,1:T(8,128)} %maximum_multiply_fusion) | data formatting | bytes 18874368 | tf_op jit(solution)/shard_map/mul | solution.py:65
  73.2 0.6 copy-done.3
  73.8 0.6 dynamic-slice
  75.2 25.5 %all-reduce.1 = f32[512]{0:T(512)S(1)} all-reduce(f32[512]{0:T(512)S(1)} %broadcast_multiply_fusion), channel_id=3, replica_groups=mesh['clip'=4,'band'=4,'chan'=16] {'chan'}, use_global_device_ids=true, to_apply=%region_3.4.clone | all-reduce | flops 512 | bytes 4096
  100.8 153.2 %psum.15 = f32[32]{0:T(128)} all-reduce(f32[32]{0:T(128)S(1)} %dynamic-slice.3), channel_id=1, replica_groups=mesh['clip'=4,'band'=4,'chan'=16] {'clip','band'}, use_global_device_ids=true, to_apply=%region_4.5 | all-reduce | flops 32 | bytes 256 | tf_op jit(solution)/shard_map/psum | solution.py:92
  254.1 1.7 fusion.52
  255.8 1.9 fusion.22
  257.7 0.9 convolution_add_fusion.15
  258.6 0.9 convolution_add_fusion.14
  259.5 0.9 convolution_add_fusion.13
  260.4 0.9 convolution_add_fusion.12
  261.3 0.9 convolution_add_fusion.11
  262.2 0.9 convolution_add_fusion.10
  263.1 2.0 convolution_add_fusion.9
  265.0 0.8 convolution_add_fusion.7
  265.9 0.8 convolution_add_fusion.6
  266.7 0.8 convolution_add_fusion.5
  267.6 0.8 convolution_add_fusion.4
  268.4 0.8 convolution_add_fusion.3
  269.3 0.8 convolution_add_fusion.2
  270.1 111.2 %all-reduce.7.cloned.1.call-done = f32[512,3,3,512]{3,2,1,0:T(4,128)} async-done(((f32[512,3,3,512]{3,2,1,0:T(4,128)}), f32[512,3,3,512]{3,2,1,0:T(4,128)}) %all-reduce.7.cloned.1.call-update) | async-done | bytes 9437200
  381.3 2.2 constant_dynamic-slice_fusion
  383.6 3.2 fusion.4
  386.8 2.2 copy.12
  388.9 1.9 convolution_add_fusion.1
  390.8 1.6 fusion.3
  392.4 1.1 copy.13
  393.5 146.3 %all-reduce.5.cloned.1.call-done = f32[32,3,3,512]{3,2,1,0:T(4,128)} async-done(((f32[32,3,3,512]{3,2,1,0:T(4,128)}), f32[32,3,3,512]{3,2,1,0:T(4,128)}) %all-reduce.5.cloned.1.call-update) | async-done | bytes 589840 | tf_op jit(solution)/shard_map/psum | solution.py:92
  539.8 2.1 copy.14
  (20 shorter events, 1.2 us)
Async XLA Ops:
  7.2 246.9 %all-gather.2.cloned.1.call-start = ((), (), s32[]{:S(2)}) async-start(), calls=%async_computation | async-start | bytes 5013504 | tf_op jit(solution)/shard_map/all_gather | solution.py:69
  7.9 373.4 %all-reduce.7.cloned.1.call-start = ((), (), s32[]{:S(2)}) async-start(), calls=%async_computation.2 | async-start | bytes 25165824
  9.4 16.4 %collective-permute-start.1 = (bf16[2,512,1,161]{3,1,2,0:T(8,128)(2,1)S(1)}, bf16[2,512,1,161]{3,1,2,0:T(8,128)(2,1)S(1)}, u32[]{:S(2)}, u32[]{:S(2)}) collective-permute-start(bf16[2,512,1,161]{3,1,2,0:T(8,128)(2,1)S(1)} %get-tuple-element.15), channel_id=1, source_target_pairs={{1,0},{2,1},{3,2},{4,3},{5,4},{6,5},{7,6},{8,7},{9,8},{10,9},{11,1... | collective-permute-start | bytes 989192 | tf_op jit(solution)/shard_map/ppermute | solution.py:19
  19.2 25.7 %collective-permute-start = (bf16[2,512,1,161]{3,1,2,0:T(8,128)(2,1)S(1)}, bf16[2,512,1,161]{3,1,2,0:T(8,128)(2,1)S(1)}, u32[]{:S(2)}, u32[]{:S(2)}) collective-permute-start(bf16[2,512,1,161]{3,1,2,0:T(8,128)(2,1)S(1)} %get-tuple-element.14), channel_id=1, source_target_pairs={{0,1},{1,2},{2,3},{3,4},{4,5},{5,6},{6,7},{7,8},{8,9},{9,10},{10,1... | collective-permute-start | bytes 989192 | tf_op jit(solution)/shard_map/ppermute | solution.py:18
  47.2 1.1 copy-start.1
  73.1 0.7 copy-start.3
  73.1 466.6 %all-reduce.5.cloned.1.call-start = ((), (), s32[]{:S(2)}) async-start(), calls=%async_computation.1 | async-start | bytes 1572864 | tf_op jit(solution)/shard_map/psum | solution.py:92
  254.1 3.6 copy-start
  269.2 114.3 %copy-start.2 = (f32[512]{0:T(512)S(1)}, f32[512]{0:T(512)}, u32[]{:S(2)}) copy-start(f32[512]{0:T(512)} %param.6) | copy-start | bytes 6148
Sparse Core Ops, SparseCore 0:
  9.8 79.0 all-gather.1
  91.5 289.7 all-reduce.6
  384.0 155.7 all-reduce.4
where the time goes:
time: 549 us; the launch traced here: 548 us
  waiting for transfers between devices  282 us (51%)
  blocking collectives  179 us (33%)
  matrix products  28.3 us (5%)
  local copies, waits for them, and re-layouts  23.8 us (4%)
  between operations  14.7 us (3%)
  starting transfers between devices  11.8 us (2%)
  other arithmetic  9.19 us (2%)
    psum x1, blocking collectives, local(): grad_weight, grad_bias = lax.psum((dw_part, db_part), ('clip', 'band'))  153 us
    psum x1, waiting for transfers between devices, local(): grad_weight, grad_bias = lax.psum((dw_part, db_part), ('clip', 'band'))  146 us
    unnamed x4, waiting for transfers between devices  112 us
    unnamed x1, blocking collectives  25.5 us
    ppermute x1, waiting for transfers between devices, padded(): before = lax.ppermute(last, axis, up)  19.1 us
    mul x1, local copies, waits for them, and re-layouts, local(): dw_local = jnp.stack(tap_rows, axis=1) * scale  13.9 us
    dot_general x9, matrix products, local(): jnp.einsum('ifs,oi->ofs', in_windows[3 * a + b], kernel[:, a, b, :], pref...  12.3 us
  transfers between devices with their start and end apart: 5, of which 4 were waited for; matrix products, arithmetic and copies ran while one was open for 10% of the time, Pallas kernels for 0%

commit v1 on v0

v1 whole, which is shorter than its diff:
```python
import functools
import math

import jax
import jax.numpy as jnp
from jax import lax
from jax.experimental import pallas as pl
from jax.experimental.pallas import tpu as pltpu
from jax.sharding import Mesh, PartitionSpec as P

C = 512
HALF = 256
W = 160
S = 640
TAPS = 9
AXES = ("y", "xh", "core", "xl", "z")
SIZES = (4, 2, 2, 2, 8)
CELLS = ("xh", "core", "xl", "z")
ROWS = 80
VMEM = 56 * 1024 * 1024

bf16 = jnp.bfloat16
f16 = jnp.float16
f32 = jnp.float32


def vmem():
    return pl.BlockSpec(memory_space=pltpu.VMEM)


def smem():
    return pl.BlockSpec(memory_space=pltpu.SMEM)


def params():
    return pltpu.CompilerParams(vmem_limit_bytes=VMEM)


def roll(x, shift):
    return pltpu.roll(x, shift % x.shape[-1], x.ndim - 1)


def pack_row(wide, tile, start):
    lane = lax.broadcasted_iota(jnp.int32, (128, 128), 1)
    tile = tile.astype(f32)
    total = jnp.zeros((128, 128), f32)
    for g in range(4):
        part = roll(tile[128 * g:128 * (g + 1)], 32 * g - start)
        total = jnp.where((lane >= 32 * g) & (lane < 32 * g + 32), part, total)
    return jnp.concatenate([wide, total.astype(bf16)], axis=0)


def pack_kernel(core_ref, f_ref, g_ref, fl_ref, ff_ref, gl_ref, gf_ref, swap_ref):
    for x, last, first in ((f_ref, fl_ref, ff_ref), (g_ref, gl_ref, gf_ref)):
        last[...] = pack_row(x[:, 512:640], x[:, 384:512], 96)
        first[...] = pack_row(x[:, 0:128], x[:, 128:256], 0)
    other = pl.multiple_of((1 - core_ref[0]) * HALF, HALF)
    swap_ref[:HALF, :] = f_ref[pl.ds(other, HALF), :]
    swap_ref[HALF:, :] = g_ref[...]


def pack(core, f, g):
    row = jax.ShapeDtypeStruct((640, 128), bf16)
    return pl.pallas_call(
        pack_kernel,
        out_shape=(row, row, row, row, jax.ShapeDtypeStruct((HALF + C, S), bf16)),
        in_specs=[smem(), vmem(), vmem()],
        out_specs=(vmem(),) * 5,
        compiler_params=params(),
        name="pack",
    )(core, f, g)


def column_masks(rows):
    column = lax.broadcasted_iota(jnp.int32, (rows, S), 1) % W
    return column != 0, None, column != W - 1


def fill(ext, rows, cells, before, after, groups):
    ext[:rows, 256:896] = cells
    ext[:rows, 128:256] = before[0]
    ext[:rows, 896:1024] = after[0]
    tail_before = before[1].astype(f32)
    tail_after = after[1].astype(f32)
    for k, g in enumerate(groups):
        ext[128 * k:128 * (k + 1), 0:128] = pltpu.roll(tail_before, (96 - 32 * g) % 128, 1).astype(bf16)
        ext[128 * k:128 * (k + 1), 1024:1152] = pltpu.roll(tail_after, (128 - 32 * g) % 128, 1).astype(bf16)


def window(ext, rows, da, db, masks):
    start = 256 + da * W + db
    x = ext[pl.ds(rows[0], rows[1]), :][:, start:start + S]
    mask = masks[db + 1]
    if mask is not None:
        x = jnp.where(mask, x, jnp.zeros_like(x))
    return x


def dw_kernel(core_ref, f_ref, g_ref, before_ref, after_ref, swap_ref, halo_ref, out_ref, peak_ref, ext, win, cot):
    core = core_ref[0]
    mine = pl.multiple_of(core * HALF, HALF)
    masks = column_masks(HALF)
    groups = (2 * core, 2 * core + 1)
    cot[:, :S] = g_ref[...]
    cot[:, S:] = swap_ref[HALF:, :]
    for seg in range(2):
        if seg == 0:
            cells = f_ref[pl.ds(mine, HALF), :]
            before = (before_ref[pl.ds(mine, HALF), :], before_ref[C:, :])
            after = (after_ref[pl.ds(mine, HALF), :], after_ref[C:, :])
        else:
            cells = swap_ref[:HALF, :]
            before = (halo_ref[0, pl.ds(mine, HALF), :], halo_ref[0, C:, :])
            after = (halo_ref[1, pl.ds(mine, HALF), :], halo_ref[1, C:, :])
        fill(ext, HALF, cells, before, after, groups)
        for a in range(3):
            for b in range(3):
                win[3 * a + b, :, S * seg:S * (seg + 1)] = window(ext, (0, HALF), a - 1, b - 1, masks)
    peak = jnp.zeros((8, 128), f32)
    for t in range(TAPS):
        part = lax.dot_general(cot[...], win[t], (((1,), (1,)), ((), ())), preferred_element_type=f32)
        for o in range(64):
            xl, z, y = o // 32, (o // 4) % 8, o % 4
            for xh in range(2):
                block = part[8 * o:8 * o + 8, 128 * xh:128 * xh + 128]
                out_ref[y, xh, xl, z, 8 * t:8 * t + 8, :] = block
                peak = jnp.maximum(peak, jnp.abs(block))
    peak_ref[0] = peak
    bias_peak = jnp.zeros((8, 128), f32)
    total = jnp.zeros((C, 128), f32)
    for k in range(2 * S // 128):
        total = total + cot[:, 128 * k:128 * (k + 1)].astype(f32)
    total = jnp.broadcast_to(jnp.sum(total, axis=1, keepdims=True), (C, 128))
    for o in range(64):
        xl, z, y = o // 32, (o // 4) % 8, o % 4
        block = total[8 * o:8 * o + 8, :]
        bias_peak = jnp.maximum(bias_peak, jnp.abs(block))
        for xh in range(2):
            out_ref[y, xh, xl, z, 72:80, :] = block
    peak_ref[1] = bias_peak


def kernel_gradient(core, f, g, before, after, swapped, halo):
    return pl.pallas_call(
        dw_kernel,
        out_shape=(
            jax.ShapeDtypeStruct((4, 2, 2, 8, ROWS, 128), f32),
            jax.ShapeDtypeStruct((2, 8, 128), f32),
        ),
        in_specs=[smem()] + [vmem()] * 6,
        out_specs=(vmem(), vmem()),
        scratch_shapes=[
            pltpu.VMEM((HALF, 1152), bf16),
            pltpu.VMEM((TAPS, HALF, 2 * S), bf16),
            pltpu.VMEM((C, 2 * S), bf16),
        ],
        compiler_params=params(),
        cost_estimate=pl.CostEstimate(flops=2 * TAPS * C * HALF * 2 * S, bytes_accessed=9_000_000, transcendentals=0),
        name="kernel_gradient",
    )(core, f, g, before, after, swapped, halo)


def conv_kernel(core_ref, f_ref, g_ref, fb_ref, fa_ref, gb_ref, ga_ref, own_ref, other_ref, bias_ref,
                out_ref, grad_ref, ext, win, kern):
    core = core_ref[0]
    for half, ref in ((core, own_ref), (1 - core, other_ref)):
        for t in range(TAPS):
            lanes = pl.ds(pl.multiple_of(t * C + half * HALF, HALF), HALF)
            for xl in range(2):
                for z in range(8):
                    o = 256 * xl + 32 * z
                    kern[o:o + 32, lanes] = ref[z, xl, t]
    masks = column_masks(C)
    groups = (0, 1, 2, 3)
    fill(ext, C, f_ref[...], (fb_ref[:C, :], fb_ref[C:, :]), (fa_ref[:C, :], fa_ref[C:, :]), groups)
    for a in range(3):
        for b in range(3):
            t = 3 * a + b
            win[C * t:C * (t + 1), :] = window(ext, (0, C), a - 1, b - 1, masks)
    for m in range(2):
        rows = slice(HALF * m, HALF * (m + 1))
        total = jnp.dot(kern[rows, :], win[...], preferred_element_type=f32)
        out_ref[rows, :] = (total + bias_ref[rows, :]).astype(bf16)
    fill(ext, C, g_ref[...], (gb_ref[:C, :], gb_ref[C:, :]), (ga_ref[:C, :], ga_ref[C:, :]), groups)
    for a in range(3):
        for b in range(3):
            t = 3 * a + b
            win[C * t:C * (t + 1), :] = window(ext, (0, C), 1 - a, 1 - b, masks)
    for m in range(2):
        rows = slice(HALF * m, HALF * (m + 1))
        total = jnp.zeros((HALF, S), f32)
        for t in range(TAPS):
            total = total + lax.dot_general(
                kern[:, C * t + HALF * m:C * t + HALF * (m + 1)],
                win[C * t:C * (t + 1), :],
                (((0,), (0,)), ((), ())),
                preferred_element_type=f32,
            )
        grad_ref[rows, :] = total.astype(bf16)


def convolve(core, f, g, fb, fa, gb, ga, own, other, bias):
    flat = jax.ShapeDtypeStruct((C, S), bf16)
    return pl.pallas_call(
        conv_kernel,
        out_shape=(flat, flat),
        in_specs=[smem()] + [vmem()] * 9,
        out_specs=(vmem(), vmem()),
        scratch_shapes=[
            pltpu.VMEM((C, 1152), bf16),
            pltpu.VMEM((TAPS * C, S), bf16),
            pltpu.VMEM((C, TAPS * C), bf16),
        ],
        compiler_params=params(),
        cost_estimate=pl.CostEstimate(flops=4 * TAPS * C * C * S, bytes_accessed=9_000_000, transcendentals=0),
        name="convolve",
    )(core, f, g, fb, fa, gb, ga, own, other, bias)


def swap_cores(x):
    return lax.ppermute(x, "core", [(0, 1), (1, 0)])


def local(frames, weight, bias, cotangent):
    f = frames.reshape(C, S)
    g = cotangent.reshape(C, S)
    core = lax.axis_index("core")
    core_ref = core.reshape(1).astype(jnp.int32)
    up = [(i, i + 1) for i in range(63)]
    down = [(i + 1, i) for i in range(63)]

    fl, ff, gl, gf, swap = pack(core_ref, f, g)
    swapped = swap_cores(swap)
    fb = lax.ppermute(fl, CELLS, up)
    fa = lax.ppermute(ff, CELLS, down)
    halo = swap_cores(jnp.stack((fb, fa)))
    gb = lax.ppermute(gl, CELLS, up)
    ga = lax.ppermute(gf, CELLS, down)

    taps = weight.transpose(1, 2, 0, 3).reshape(TAPS, 32, C)
    half = lax.dynamic_slice_in_dim(taps, core * HALF, HALF, axis=2)
    beside = lax.ppermute(half, "xl", [(0, 1), (1, 0)])
    low = lax.axis_index("xl") == 0
    pair = jnp.stack((jnp.where(low, half, beside), jnp.where(low, beside, half)))
    own = lax.all_gather(pair, "z", axis=0, tiled=False)
    other = swap_cores(own)

    part, peak = kernel_gradient(core_ref, f, g, fb, fa, swapped, halo)
    peaks = jnp.maximum(jnp.max(peak, axis=(1, 2)), 1e-30)
    power = 14.0 - jnp.floor(jnp.log2(peaks))
    row = lax.broadcasted_iota(jnp.int32, (ROWS, 128), 0)
    lane = lax.broadcasted_iota(jnp.int32, (ROWS, 128), 1)
    factor = jnp.where(row < 72, jnp.exp2(power[0]), jnp.exp2(power[1]))
    scaled = part * factor
    scaled = jnp.where((row >= 72) & (lane == 126), power[0], scaled)
    scaled = jnp.where((row >= 72) & (lane == 127), power[1], scaled)
    sent = scaled.astype(f16).reshape(16, 8 * ROWS, 128)
    got = lax.all_to_all(sent, ("y", "xh", "xl"), 0, 0, tiled=True)
    got = got.reshape(16, 8, ROWS, 128).astype(f32)
    back_w = jnp.exp2(-got[:, 0, 72, 126])
    back_b = jnp.exp2(-got[:, 0, 72, 127])
    factors = jnp.where(row < 72, back_w[:, None, None], back_b[:, None, None])
    plane = jnp.sum(got * factors[:, None], axis=0)
    lines = lax.all_to_all(plane, "z", 0, 0, tiled=True)
    scale = 1.0 / math.sqrt(4 * 256 * 160)
    done = jnp.sum(lines, axis=0) * scale
    whole = lax.all_gather(done, ("y", "xh", "core"), axis=0, tiled=False)
    whole = whole.reshape(4, 2, 2, ROWS, 128)
    grad_weight = whole[:, :, :, :72].reshape(4, 2, 2, 3, 3, 8, 128)
    grad_weight = grad_weight.transpose(0, 5, 3, 4, 2, 1, 6).reshape(32, 3, 3, C)
    grad_bias = whole[:, 0, 0, 72:80, 0].reshape(32)

    outputs, grad_frames = convolve(core_ref, f, g, fb, fa, gb, ga, own, other, bias.reshape(C, 1))
    return (outputs.reshape(C, 1, S), grad_frames.reshape(C, 1, S), grad_weight, grad_bias)


def solution(mesh):
    fine = Mesh(mesh.devices.reshape(SIZES), AXES)
    cells = P(None, "y", CELLS)
    rows = ("xl", "z")
    in_specs = (cells, P(rows, None, None, None), P(), cells)
    out_specs = (cells, cells, P(rows, None, None, None), P(rows))
    return jax.shard_map(local, mesh=fine, in_specs=in_specs, out_specs=out_specs, check_vma=False)
```

time: 549 us -> 197 us (0.36)
  waiting for transfers between devices: 282 us -> 51.2 us
  blocking collectives: 179 us -> 27.2 us
  matrix products: 28.3 us -> 0 us
  starting transfers between devices: 11.8 us -> 36.9 us
  Pallas kernels: 0 us -> 23.4 us
    psum x1 -> x0, blocking collectives: 153 us -> none  [local(): grad_weight, grad_bias = lax.psum((dw_part, db_part), ('clip', 'band'))]
    psum x1 -> x0, waiting for transfers between devices: 146 us -> none  [local(): grad_weight, grad_bias = lax.psum((dw_part, db_part), ('clip', 'band'))]
    unnamed x4 -> x1, waiting for transfers between devices: 112 us -> 0.02 us
    all_to_all x0 -> x2, waiting for transfers between devices: none -> 41.6 us  [the longest x1 39 us: local(): got = lax.all_to_all(sent, ('y', 'xh', 'xl'), 0, 0, tiled=True)]
    dot_general x27 -> x0, matrix products: 28.3 us -> none  [the longest x9 12.3 us: local(): jnp.einsum('ifs,oi->ofs', in_windows[3 * a + b], kernel[:, a, b, :], pref...]
    all_gather x0 -> x1, blocking collectives: none -> 27.2 us  [local(): whole = lax.all_gather(done, ('y', 'xh', 'core'), axis=0, tiled=False)]
    unnamed x1 -> x0, blocking collectives: 25.5 us -> none
    pallas_call x0 -> x3, Pallas kernels: none -> 23.4 us  [the longest x1 12.9 us: convolve(): pl.pallas_call(conv_kernel, out_shape=(flat, flat), in_specs=[smem()] + [...]
  transfers between devices with their start and end apart: 5 -> 11, of which waited for: 4 -> 6; matrix products, arithmetic and copies ran while one was open for 10% -> 19% of each run, Pallas kernels for 0% -> 5%
where the time goes in v1:
time: 197 us; the launch traced here: 196 us
  waiting for transfers between devices  51.2 us (26%)
  starting transfers between devices  36.9 us (19%)
  local copies, waits for them, and re-layouts  27.8 us (14%)
  blocking collectives  27.2 us (14%)
  Pallas kernels  23.4 us (12%)
  between operations  15.6 us (8%)
  other arithmetic  14.2 us (7%)
    all_to_all x1, waiting for transfers between devices, local(): got = lax.all_to_all(sent, ('y', 'xh', 'xl'), 0, 0, tiled=True)  39 us
    all_gather x1, blocking collectives, local(): whole = lax.all_gather(done, ('y', 'xh', 'core'), axis=0, tiled=False)  27.2 us
    convert_element_type x1, local copies, waits for them, and re-layouts, local(): got = got.reshape(16, 8, ROWS, 128).astype(f32)  20.6 us
    pallas_call x1, Pallas kernels, convolve(): pl.pallas_call(conv_kernel, out_shape=(flat, flat), in_specs=[smem()] + [...  12.9 us
    all_to_all x1, starting transfers between devices, local(): got = lax.all_to_all(sent, ('y', 'xh', 'xl'), 0, 0, tiled=True)  8.5 us
    pallas_call x1, Pallas kernels, kernel_gradient(): pl.pallas_call(dw_kernel, out_shape=(jax.ShapeDtypeStruct((4, 2, 2, 8, RO...  7.96 us
    ppermute x1, starting transfers between devices, local(): fa = lax.ppermute(ff, CELLS, down)  6.67 us
    convert_element_type x1, other arithmetic, local(): sent = scaled.astype(f16).reshape(16, 8 * ROWS, 128)  6.25 us
  transfers between devices with their start and end apart: 11, of which 6 were waited for; matrix products, arithmetic and copies ran while one was open for 19% of the time, Pallas kernels for 5%

profile of v1, /device:TPU:1, one launch (start us, length us, event | category | flops | bytes accessed | tf_op | source)
XLA Modules:
  0.0 196.2 jit_solution(10996926395567135867)
XLA Ops:
  7.2 0.0 all-gather.4.cloned.1.call-start
  7.2 0.9 constant_dynamic-slice_fusion
  8.1 2.1 %collective-permute-start.4 = (bf16[9,32,256]{2,1,0:T(8,128)(2,1)S(1)}, bf16[9,32,256]{2,1,0:T(8,128)(2,1)S(1)}, u32[]{:S(2)}, u32[]{:S(2)}) collective-permute-start(bf16[9,32,256]{2,1,0:T(8,128)(2,1)S(1)} %constant_dynamic-slice_fusion), channel_id=1, source_target_pairs={{0,8},{8,0},{1,9},{9,1},{2,10},{10,2},{3,11},{11,3},{4,12},{12,4},... | collective-permute-start | bytes 442376 | tf_op jit(solution)/shard_map/ppermute | solution.py:242
  10.3 2.5 %collective-permute-done.4 = bf16[9,32,256]{2,1,0:T(8,128)(2,1)S(1)} collective-permute-done((bf16[9,32,256]{2,1,0:T(8,128)(2,1)S(1)}, bf16[9,32,256]{2,1,0:T(8,128)(2,1)S(1)}, u32[]{:S(2)}, u32[]{:S(2)}) %collective-permute-start.4) | collective-permute-done | bytes 147488 | tf_op jit(solution)/shard_map/ppermute | solution.py:242
  12.8 1.0 select_bitcast_fusion.1
  13.8 0.7 pad_maximum_fusion.1
  14.5 0.0 all-gather.4.cloned.1.call-update
  14.6 2.6 %pack.1 = (bf16[640,128]{1,0:T(8,128)(2,1)}, bf16[640,128]{1,0:T(8,128)(2,1)}, bf16[640,128]{1,0:T(8,128)(2,1)}, bf16[640,128]{1,0:T(8,128)(2,1)}, bf16[768,640]{1,0:T(8,128)(2,1)}) custom-call(s32[1]{0:T(128)} %bitcast.core_ref, bf16[512,640]{1,0:T(8,128)(2,1)} %bitcast.40, bf16[512,640]{1,0:T(8,128)(2,1)} %bitcast.43), custom_call_target="tpu_custom_call" | custom-call | tf_op jit(solution)/shard_map/pack/pallas_call | solution.py:64
  17.1 3.8 %collective-permute-start.6 = (bf16[768,640]{1,0:T(8,128)(2,1)}, bf16[768,640]{1,0:T(8,128)(2,1)S(1)}, u32[]{:S(2)}, u32[]{:S(2)}) collective-permute-start(bf16[768,640]{1,0:T(8,128)(2,1)} %get-tuple-element.19), channel_id=1, source_target_pairs={{0,16},{16,0},{1,17},{17,1},{2,18},{18,2},{3,19},{19,3},{4,20},{20... | collective-permute-start | bytes 2949128 | tf_op jit(solution)/shard_map/ppermute | solution.py:221
  21.0 2.2 %collective-permute-start = (bf16[640,128]{1,0:T(8,128)(2,1)}, bf16[640,128]{1,0:T(8,128)(2,1)S(1)}, u32[]{:S(2)}, u32[]{:S(2)}) collective-permute-start(bf16[640,128]{1,0:T(8,128)(2,1)} %get-tuple-element.13), channel_id=1, source_target_pairs={{0,1},{1,2},{2,3},{3,4},{4,5},{5,6},{6,7},{7,8},{8,9},{9,10},{10,1... | collective-permute-start | bytes 491528 | tf_op jit(solution)/shard_map/ppermute | solution.py:234
  23.2 6.7 %collective-permute-start.1 = (bf16[640,128]{1,0:T(8,128)(2,1)}, bf16[640,128]{1,0:T(8,128)(2,1)S(1)}, u32[]{:S(2)}, u32[]{:S(2)}) collective-permute-start(bf16[640,128]{1,0:T(8,128)(2,1)} %get-tuple-element.14), channel_id=1, source_target_pairs={{1,0},{2,1},{3,2},{4,3},{5,4},{6,5},{7,6},{8,7},{9,8},{10,9},{11,1... | collective-permute-start | bytes 491528 | tf_op jit(solution)/shard_map/ppermute | solution.py:235
  29.9 2.8 %collective-permute-done.fb_ref.before_ref = bf16[640,128]{1,0:T(8,128)(2,1)S(1)} collective-permute-done((bf16[640,128]{1,0:T(8,128)(2,1)}, bf16[640,128]{1,0:T(8,128)(2,1)S(1)}, u32[]{:S(2)}, u32[]{:S(2)}) %collective-permute-start) | collective-permute-done | bytes 163872 | tf_op jit(solution)/shard_map/ppermute | solution.py:234
  32.7 2.6 %collective-permute-done.1.fa_ref.after_ref = bf16[640,128]{1,0:T(8,128)(2,1)S(1)} collective-permute-done((bf16[640,128]{1,0:T(8,128)(2,1)}, bf16[640,128]{1,0:T(8,128)(2,1)S(1)}, u32[]{:S(2)}, u32[]{:S(2)}) %collective-permute-start.1) | collective-permute-done | bytes 163872 | tf_op jit(solution)/shard_map/ppermute | solution.py:235
  35.4 0.1 collective-permute-start.7
  35.5 0.1 broadcast_and_fusion.1
  35.6 1.5 collective-permute-done.7.halo_ref
  37.1 0.0 collective-permute-done.6.swap_ref
  37.1 0.7 copy-done.4
  37.8 1.0 copy-done.3
  38.8 8.0 %kernel_gradient.1 = (f32[4,2,2,8,80,128]{5,4,3,2,1,0:T(8,128)}, f32[2,8,128]{2,1,0:T(8,128)}) custom-call(s32[1]{0:T(128)} %bitcast.core_ref, bf16[512,640]{1,0:T(8,128)(2,1)} %bitcast.41, bf16[512,640]{1,0:T(8,128)(2,1)} %bitcast.44, bf16[640,128]{1,0:T(8,128)(2,1)} %copy-done, bf16[640,128]{1,0:T(8,128)(2,1)} %copy-done.1, bf16[768,640]{1,0:T(8,128)(2,1)} %copy-done.3, ...), custom_call_target="tpu_custom_call" | custom-call | flops 3019898880 | bytes 9000000 | tf_op jit(solution)/shard_map/kernel_gradient/pallas_call | solution.py:144
  46.8 0.8 reduce_max.9
  47.6 0.6 fusion.7
  49.6 6.2 %select_convert_fusion = f16[4,2,2,8,80,128]{5,4,3,2,1,0:T(8,128)(2,1)} fusion(f32[4,2,2,8,80,128]{5,4,3,2,1,0:T(8,128)} %get-tuple-element.21, f32[80]{0:T(128)S(1)} %broadcast_select_fusion.1, f32[]{:T(128)} %bitcast.14, f32[]{:T(128)} %bitcast.13, pred[80,128]{1,0:T(8,128)(4,1)S(1)} %get-tuple-element.27, pred[80,128]{1,0:T(8,128)(4,1)S(1)} %get-tuple-element.26), kind=kLoop, calls=%fused_computation.2 | loop fusion | flops 5242880 | bytes 7885128 | tf_op jit(solution)/shard_map/convert_element_type | solution.py:257
  55.8 8.5 %all-to-all-start = ((f16[16,640,128]{2,1,0:T(8,128)(2,1)}), f16[16,640,128]{2,1,0:T(8,128)(2,1)S(1)}, u32[]{:S(2)}, u32[]{:S(2)}) async-start(f16[16,640,128]{2,1,0:T(8,128)(2,1)} %bitcast.36), calls=%async_computation | async-start | bytes 5242880 | tf_op jit(solution)/shard_map/all_to_all | solution.py:258
  64.3 0.0 all-gather.4.cloned.1.call-done
  64.4 0.7 collective-permute-start.5
  65.1 39.0 %all-to-all-done = f16[16,640,128]{2,1,0:T(8,128)(2,1)S(1)} async-done(((f16[16,640,128]{2,1,0:T(8,128)(2,1)}), f16[16,640,128]{2,1,0:T(8,128)(2,1)S(1)}, u32[]{:S(2)}, u32[]{:S(2)}) %all-to-all-start) | async-done | bytes 2621472 | tf_op jit(solution)/shard_map/all_to_all | solution.py:258
  104.1 2.8 %convert_element_type.13 = f32[16,640,128]{2,1,0:T(8,128)} convert(f16[16,640,128]{2,1,0:T(8,128)(2,1)S(1)} %all-to-all-done) | non-fusion elementwise | flops 1310720 | bytes 7864320 | tf_op jit(solution)/shard_map/convert_element_type | solution.py:259
  106.9 20.6 %copy.19 = f32[16,640,128]{0,2,1:T(8,128)} copy(f32[16,640,128]{2,1,0:T(8,128)} %convert_element_type.13) | data formatting | bytes 10485760 | tf_op jit(solution)/shard_map/convert_element_type | solution.py:259
  127.5 0.8 fusion.6
  128.3 0.1 broadcast_select_fusion
  128.4 1.6 fusion
  130.0 5.0 %all-to-all-start.1 = ((f32[8,80,128]{2,1,0:T(8,128)}), f32[8,80,128]{2,1,0:T(8,128)S(1)}, u32[]{:S(2)}, u32[]{:S(2)}) async-start(f32[8,80,128]{2,1,0:T(8,128)} %bitcast.20), calls=%async_computation.1 | async-start | bytes 655360 | tf_op jit(solution)/shard_map/all_to_all | solution.py:264
  135.0 3.4 %collective-permute-start.2 = (bf16[640,128]{1,0:T(8,128)(2,1)S(1)}, bf16[640,128]{1,0:T(8,128)(2,1)S(1)}, u32[]{:S(2)}, u32[]{:S(2)}) collective-permute-start(bf16[640,128]{1,0:T(8,128)(2,1)S(1)} %copy-done.6), channel_id=1, source_target_pairs={{0,1},{1,2},{2,3},{3,4},{4,5},{5,6},{6,7},{7,8},{8,9},{9,10},{10,1... | collective-permute-start | bytes 491528 | tf_op jit(solution)/shard_map/ppermute | solution.py:237
  138.4 4.3 %collective-permute-start.3 = (bf16[640,128]{1,0:T(8,128)(2,1)S(1)}, bf16[640,128]{1,0:T(8,128)(2,1)S(1)}, u32[]{:S(2)}, u32[]{:S(2)}) collective-permute-start(bf16[640,128]{1,0:T(8,128)(2,1)S(1)} %copy-done.5), channel_id=1, source_target_pairs={{1,0},{2,1},{3,2},{4,3},{5,4},{6,5},{7,6},{8,7},{9,8},{10,9},{11,1... | collective-permute-start | bytes 491528 | tf_op jit(solution)/shard_map/ppermute | solution.py:238
  142.7 0.9 copy.18.bias_ref
  143.6 2.6 %all-to-all-done.1 = f32[8,80,128]{2,1,0:T(8,128)S(1)} async-done(((f32[8,80,128]{2,1,0:T(8,128)}), f32[8,80,128]{2,1,0:T(8,128)S(1)}, u32[]{:S(2)}, u32[]{:S(2)}) %all-to-all-start.1) | async-done | bytes 327712 | tf_op jit(solution)/shard_map/all_to_all | solution.py:264
  146.2 27.2 %all-gather.1 = f32[1280,128]{1,0:T(8,128)S(1)} all-gather(f32[80,128]{1,0:T(8,128)S(1)} %broadcast_multiply_fusion), channel_id=3, replica_groups=mesh['y'=4,'xh'=2,'core'=2,'xl'=2,'z'=8] {'y','xh','core'}, dimensions={0}, use_global_device_ids=true | all-gather | bytes 696320 | tf_op jit(solution)/shard_map/all_gather | solution.py:267
  173.5 0.3 copy.20
  173.8 1.3 reshape.88
  175.1 0.1 slice_reduce_fusion
  175.2 0.6 reshape_squeeze.3
  175.8 0.0 collective-permute-done.2.gb_ref
  175.8 0.0 collective-permute-done.3.ga_ref
  175.8 0.0 collective-permute-done.5.other_ref
  175.8 0.6 copy-done.7
  176.5 0.1 copy-done.8
  176.5 12.9 %convolve.1 = (bf16[512,640]{1,0:T(8,128)(2,1)}, bf16[512,640]{1,0:T(8,128)(2,1)}) custom-call(s32[1]{0:T(128)} %bitcast.core_ref, bf16[512,640]{1,0:T(8,128)(2,1)} %bitcast.42, bf16[512,640]{1,0:T(8,128)(2,1)} %bitcast.45, bf16[640,128]{1,0:T(8,128)(2,1)} %copy-done, bf16[640,128]{1,0:T(8,128)(2,1)} %copy-done.1, bf16[640,128]{1,0:T(8,128)(2,1)} %copy-done.7, ...), custom_call_target="tpu_custom_call" | custom-call | flops 6039797760 | bytes 9000000 | tf_op jit(solution)/shard_map/convolve/pallas_call | solution.py:204
  (23 shorter events, 0.2 us)
Async XLA Ops:
  7.2 57.2 %all-gather.4.cloned.1.call-start = ((), (), s32[]{:S(2)}) async-start(), calls=%async_computation.2 | async-start | bytes 2654208 | tf_op jit(solution)/shard_map/all_gather | solution.py:245
  8.1 4.7 %collective-permute-start.4 = (bf16[9,32,256]{2,1,0:T(8,128)(2,1)S(1)}, bf16[9,32,256]{2,1,0:T(8,128)(2,1)S(1)}, u32[]{:S(2)}, u32[]{:S(2)}) collective-permute-start(bf16[9,32,256]{2,1,0:T(8,128)(2,1)S(1)} %constant_dynamic-slice_fusion), channel_id=1, source_target_pairs={{0,8},{8,0},{1,9},{9,1},{2,10},{10,2},{3,11},{11,3},{4,12},{12,4},... | collective-permute-start | bytes 442376 | tf_op jit(solution)/shard_map/ppermute | solution.py:242
  17.1 20.0 %collective-permute-start.6 = (bf16[768,640]{1,0:T(8,128)(2,1)}, bf16[768,640]{1,0:T(8,128)(2,1)S(1)}, u32[]{:S(2)}, u32[]{:S(2)}) collective-permute-start(bf16[768,640]{1,0:T(8,128)(2,1)} %get-tuple-element.19), channel_id=1, source_target_pairs={{0,16},{16,0},{1,17},{17,1},{2,18},{18,2},{3,19},{19,3},{4,20},{20... | collective-permute-start | bytes 2949128 | tf_op jit(solution)/shard_map/ppermute | solution.py:221
  21.0 11.8 %collective-permute-start = (bf16[640,128]{1,0:T(8,128)(2,1)}, bf16[640,128]{1,0:T(8,128)(2,1)S(1)}, u32[]{:S(2)}, u32[]{:S(2)}) collective-permute-start(bf16[640,128]{1,0:T(8,128)(2,1)} %get-tuple-element.13), channel_id=1, source_target_pairs={{0,1},{1,2},{2,3},{3,4},{4,5},{5,6},{6,7},{7,8},{8,9},{9,10},{10,1... | collective-permute-start | bytes 491528 | tf_op jit(solution)/shard_map/ppermute | solution.py:234
  23.2 12.1 %collective-permute-start.1 = (bf16[640,128]{1,0:T(8,128)(2,1)}, bf16[640,128]{1,0:T(8,128)(2,1)S(1)}, u32[]{:S(2)}, u32[]{:S(2)}) collective-permute-start(bf16[640,128]{1,0:T(8,128)(2,1)} %get-tuple-element.14), channel_id=1, source_target_pairs={{1,0},{2,1},{3,2},{4,3},{5,4},{6,5},{7,6},{8,7},{9,8},{10,9},{11,1... | collective-permute-start | bytes 491528 | tf_op jit(solution)/shard_map/ppermute | solution.py:235
  32.7 4.4 %copy-start = (bf16[640,128]{1,0:T(8,128)(2,1)}, bf16[640,128]{1,0:T(8,128)(2,1)S(1)}, u32[]{:S(2)}) copy-start(bf16[640,128]{1,0:T(8,128)(2,1)S(1)} %collective-permute-done.fb_ref.before_ref) | copy-start | bytes 491524
  35.4 1.8 copy-start.1
  35.4 1.7 collective-permute-start.7
  37.1 0.7 copy-start.4
  37.8 1.0 copy-start.3
  55.8 48.3 %all-to-all-start = ((f16[16,640,128]{2,1,0:T(8,128)(2,1)}), f16[16,640,128]{2,1,0:T(8,128)(2,1)S(1)}, u32[]{:S(2)}, u32[]{:S(2)}) async-start(f16[16,640,128]{2,1,0:T(8,128)(2,1)} %bitcast.36), calls=%async_computation | async-start | bytes 5242880 | tf_op jit(solution)/shard_map/all_to_all | solution.py:258
  64.4 111.5 %collective-permute-start.5 = (bf16[8,2,9,32,256]{4,3,2,1,0:T(8,128)(2,1)}, bf16[8,2,9,32,256]{4,3,2,1,0:T(8,128)(2,1)}, u32[]{:S(2)}, u32[]{:S(2)}) collective-permute-start(bf16[8,2,9,32,256]{4,3,2,1,0:T(8,128)(2,1)} %bitcast.51), channel_id=1, source_target_pairs={{0,16},{16,0},{1,17},{17,1},{2,18},{18,2},{3,19},{19,3},{4,20},{20... | collective-permute-start | bytes 7077896 | tf_op jit(solution)/shard_map/ppermute | solution.py:221
  106.9 28.1 %copy-start.6 = (bf16[640,128]{1,0:T(8,128)(2,1)S(1)}, bf16[640,128]{1,0:T(8,128)(2,1)}, u32[]{:S(2)}) copy-start(bf16[640,128]{1,0:T(8,128)(2,1)} %get-tuple-element.15) | copy-start | bytes 491524
  106.9 31.5 %copy-start.5 = (bf16[640,128]{1,0:T(8,128)(2,1)S(1)}, bf16[640,128]{1,0:T(8,128)(2,1)}, u32[]{:S(2)}) copy-start(bf16[640,128]{1,0:T(8,128)(2,1)} %get-tuple-element.16) | copy-start | bytes 491524
  106.9 35.8 %copy-start.2 = (f32[512]{0:T(512)S(1)}, f32[512]{0:T(512)}, u32[]{:S(2)}) copy-start(f32[512]{0:T(512)} %param.6) | copy-start | bytes 6148
  130.0 16.2 %all-to-all-start.1 = ((f32[8,80,128]{2,1,0:T(8,128)}), f32[8,80,128]{2,1,0:T(8,128)S(1)}, u32[]{:S(2)}, u32[]{:S(2)}) async-start(f32[8,80,128]{2,1,0:T(8,128)} %bitcast.20), calls=%async_computation.1 | async-start | bytes 655360 | tf_op jit(solution)/shard_map/all_to_all | solution.py:264
  135.0 40.8 %collective-permute-start.2 = (bf16[640,128]{1,0:T(8,128)(2,1)S(1)}, bf16[640,128]{1,0:T(8,128)(2,1)S(1)}, u32[]{:S(2)}, u32[]{:S(2)}) collective-permute-start(bf16[640,128]{1,0:T(8,128)(2,1)S(1)} %copy-done.6), channel_id=1, source_target_pairs={{0,1},{1,2},{2,3},{3,4},{4,5},{5,6},{6,7},{7,8},{8,9},{9,10},{10,1... | collective-permute-start | bytes 491528 | tf_op jit(solution)/shard_map/ppermute | solution.py:237
  138.4 37.4 %collective-permute-start.3 = (bf16[640,128]{1,0:T(8,128)(2,1)S(1)}, bf16[640,128]{1,0:T(8,128)(2,1)S(1)}, u32[]{:S(2)}, u32[]{:S(2)}) collective-permute-start(bf16[640,128]{1,0:T(8,128)(2,1)S(1)} %copy-done.5), channel_id=1, source_target_pairs={{1,0},{2,1},{3,2},{4,3},{5,4},{6,5},{7,6},{8,7},{9,8},{10,9},{11,1... | collective-permute-start | bytes 491528 | tf_op jit(solution)/shard_map/ppermute | solution.py:238
  175.8 0.7 copy-start.7
  175.8 0.7 copy-start.8
Sparse Core Ops, SparseCore 0:
  14.7 44.2 all-gather.3

commit v2 on v1

v2 whole, which is shorter than its diff:
```python
import functools
import math

import jax
import jax.numpy as jnp
from jax import lax
from jax.experimental import pallas as pl
from jax.experimental.pallas import tpu as pltpu
from jax.sharding import Mesh, PartitionSpec as P

C = 512
HALF = 256
W = 160
S = 640
TAPS = 9
AXES = ("y", "xh", "core", "xl", "z")
SIZES = (4, 2, 2, 2, 8)
CELLS = ("xh", "core", "xl", "z")

bf16 = jnp.bfloat16
f16 = jnp.float16
f32 = jnp.float32


def vmem():
    return pl.BlockSpec(memory_space=pltpu.VMEM)


def smem():
    return pl.BlockSpec(memory_space=pltpu.SMEM)


def params(mib):
    return pltpu.CompilerParams(vmem_limit_bytes=mib * 1024 * 1024)


def roll(x, shift):
    return pltpu.roll(x, shift % x.shape[-1], x.ndim - 1)


def pack_row(wide, tile, start):
    lane = lax.broadcasted_iota(jnp.int32, (128, 128), 1)
    tile = tile.astype(f32)
    total = jnp.zeros((128, 128), f32)
    for g in range(4):
        part = roll(tile[128 * g:128 * (g + 1)], 32 * g - start)
        total = jnp.where((lane >= 32 * g) & (lane < 32 * g + 32), part, total)
    return jnp.concatenate([wide, total.astype(bf16)], axis=0)


def pack_kernel(core_ref, f_ref, g_ref, fl_ref, ff_ref, gl_ref, gf_ref, swap_ref):
    for x, last, first in ((f_ref, fl_ref, ff_ref), (g_ref, gl_ref, gf_ref)):
        last[...] = pack_row(x[:, 512:640], x[:, 384:512], 96)
        first[...] = pack_row(x[:, 0:128], x[:, 128:256], 0)
    other = pl.multiple_of((1 - core_ref[0]) * HALF, HALF)
    swap_ref[:HALF, :] = f_ref[pl.ds(other, HALF), :]
    swap_ref[HALF:, :] = g_ref[...]


def pack(core, f, g):
    row = jax.ShapeDtypeStruct((640, 128), bf16)
    return pl.pallas_call(
        pack_kernel,
        out_shape=(row, row, row, row, jax.ShapeDtypeStruct((HALF + C, S), bf16)),
        in_specs=[smem(), vmem(), vmem()],
        out_specs=(vmem(),) * 5,
        compiler_params=params(12),
        name="pack",
    )(core, f, g)


def column_masks(rows):
    column = lax.broadcasted_iota(jnp.int32, (rows, S), 1) % W
    return column != 0, None, column != W - 1


def fill(ext, rows, cells, before, after, groups):
    ext[:rows, 256:896] = cells
    ext[:rows, 128:256] = before[0]
    ext[:rows, 896:1024] = after[0]
    tail_before = before[1].astype(f32)
    tail_after = after[1].astype(f32)
    for k, g in enumerate(groups):
        ext[128 * k:128 * (k + 1), 0:128] = pltpu.roll(tail_before, (96 - 32 * g) % 128, 1).astype(bf16)
        ext[128 * k:128 * (k + 1), 1024:1152] = pltpu.roll(tail_after, (128 - 32 * g) % 128, 1).astype(bf16)


def window(ext, rows, da, db, masks):
    start = 256 + da * W + db
    x = ext[pl.ds(rows[0], rows[1]), :][:, start:start + S]
    mask = masks[db + 1]
    if mask is not None:
        x = jnp.where(mask, x, jnp.zeros_like(x))
    return x


def pair_rows(part, y, xh, xl, k):
    lanes = slice(128 * xh, 128 * xh + 128)
    o = 256 * xl + 64 * k + 8 * y
    return jnp.concatenate([part[o:o + 8, lanes], part[o + 32:o + 40, lanes]], axis=0)


def store_tap(out_ref, part, position, peak):
    for y in range(4):
        for xh in range(2):
            for xl in range(2):
                for k in range(4):
                    block = pair_rows(part, y, xh, xl, k)
                    row = 64 * position + 16 * k
                    out_ref[4 * y + 2 * xh + xl, row:row + 16, :] = block
                    peak = jnp.maximum(peak, jnp.abs(block))
    return peak


def power_of(peak):
    top = jnp.max(jnp.max(peak, axis=1, keepdims=True), axis=0, keepdims=True)
    return 14.0 - jnp.floor(jnp.log2(jnp.maximum(top, 1e-30)))


def contract(cot, win):
    return lax.dot_general(cot, win, (((1,), (1,)), ((), ())), preferred_element_type=f32)


def middle_kernel(core_ref, f_ref, g_ref, swap_ref, out_ref, ext, win, cot):
    core = core_ref[0]
    mine = pl.multiple_of(core * HALF, HALF)
    masks = column_masks(HALF)
    cot[:, :S] = g_ref[...]
    cot[:, S:] = swap_ref[HALF:, :]
    ext[...] = jnp.zeros_like(ext)
    for seg in range(2):
        ext[:, 256:896] = f_ref[pl.ds(mine, HALF), :] if seg == 0 else swap_ref[:HALF, :]
        for b in range(3):
            win[b, :, S * seg:S * (seg + 1)] = window(ext, (0, HALF), 0, b - 1, masks)
    peak = jnp.zeros((16, 128), f32)
    for b in range(3):
        peak = store_tap(out_ref, contract(cot[...], win[b]), b, peak)
    power = power_of(peak)
    factor = jnp.exp2(power)
    total = jnp.zeros((C, 128), f32)
    for k in range(2 * S // 128):
        total = total + cot[:, 128 * k:128 * (k + 1)].astype(f32)
    total = jnp.sum(total, axis=1, keepdims=True)
    bias_power = power_of(jnp.abs(total))
    total = jnp.broadcast_to(total * jnp.exp2(bias_power), (C, 128))
    lane = lax.broadcasted_iota(jnp.int32, (8, 128), 1)
    for y in range(4):
        for xl in range(2):
            extra = jnp.where(lane == 8, jnp.broadcast_to(power, (8, 128)), jnp.broadcast_to(bias_power, (8, 128)))
            for z in range(8):
                o = 256 * xl + 32 * z + 8 * y
                extra = jnp.where(lane == z, total[o:o + 8, :], extra)
            for xh in range(2):
                d = 4 * y + 2 * xh + xl
                out_ref[d, 192:208, :] = jnp.concatenate([extra, extra], axis=0)
    for d in range(16):
        out_ref[d, :192, :] = out_ref[d, :192, :] * factor


def middle_taps(core, f, g, swapped):
    return pl.pallas_call(
        middle_kernel,
        out_shape=jax.ShapeDtypeStruct((16, 208, 128), f32),
        in_specs=[smem()] + [vmem()] * 3,
        out_specs=vmem(),
        scratch_shapes=[
            pltpu.VMEM((HALF, 1152), bf16),
            pltpu.VMEM((3, HALF, 2 * S), bf16),
            pltpu.VMEM((C, 2 * S), bf16),
        ],
        compiler_params=params(20),
        cost_estimate=pl.CostEstimate(flops=2 * 3 * C * HALF * 2 * S, bytes_accessed=5_000_000, transcendentals=0),
        name="middle_taps",
    )(core, f, g, swapped)


def outer_kernel(core_ref, f_ref, g_ref, before_ref, after_ref, swap_ref, halo_ref, out_ref, ext, win, cot):
    core = core_ref[0]
    mine = pl.multiple_of(core * HALF, HALF)
    masks = column_masks(HALF)
    groups = (2 * core, 2 * core + 1)
    cot[:, :S] = g_ref[...]
    cot[:, S:] = swap_ref[HALF:, :]
    for seg in range(2):
        if seg == 0:
            cells = f_ref[pl.ds(mine, HALF), :]
            before = (before_ref[pl.ds(mine, HALF), :], before_ref[C:, :])
            after = (after_ref[pl.ds(mine, HALF), :], after_ref[C:, :])
        else:
            cells = swap_ref[:HALF, :]
            before = (halo_ref[0, pl.ds(mine, HALF), :], halo_ref[0, C:, :])
            after = (halo_ref[1, pl.ds(mine, HALF), :], halo_ref[1, C:, :])
        fill(ext, HALF, cells, before, after, groups)
        for a in range(2):
            for b in range(3):
                win[3 * a + b, :, S * seg:S * (seg + 1)] = window(ext, (0, HALF), 2 * a - 1, b - 1, masks)
    peak = jnp.zeros((16, 128), f32)
    for t in range(6):
        peak = store_tap(out_ref, contract(cot[...], win[t]), t, peak)
    power = power_of(peak)
    factor = jnp.exp2(power)
    for d in range(16):
        out_ref[d, :384, :] = out_ref[d, :384, :] * factor
        out_ref[d, 384:400, :] = jnp.broadcast_to(power, (16, 128))


def outer_taps(core, f, g, before, after, swapped, halo):
    return pl.pallas_call(
        outer_kernel,
        out_shape=jax.ShapeDtypeStruct((16, 400, 128), f32),
        in_specs=[smem()] + [vmem()] * 6,
        out_specs=vmem(),
        scratch_shapes=[
            pltpu.VMEM((HALF, 1152), bf16),
            pltpu.VMEM((6, HALF, 2 * S), bf16),
            pltpu.VMEM((C, 2 * S), bf16),
        ],
        compiler_params=params(24),
        cost_estimate=pl.CostEstimate(flops=2 * 6 * C * HALF * 2 * S, bytes_accessed=7_000_000, transcendentals=0),
        name="outer_taps",
    )(core, f, g, before, after, swapped, halo)


def load_kernel(place_ref, own_ref, other_ref, kern):
    core, low = place_ref[0], place_ref[1]
    for half, ref in ((core, own_ref), (1 - core, other_ref)):
        for t in range(TAPS):
            lanes = pl.ds(pl.multiple_of(t * C + half * HALF, HALF), HALF)
            for k in range(2):
                first = pl.multiple_of(HALF * (low if k == 0 else 1 - low), HALF)
                kern[pl.ds(first, HALF), lanes] = ref[:, k, t].reshape(HALF, HALF)


def forward_kernel(core_ref, f_ref, fb_ref, fa_ref, own_ref, other_ref, bias_ref, out_ref, ext, win, kern):
    load_kernel(core_ref, own_ref, other_ref, kern)
    masks = column_masks(C)
    fill(ext, C, f_ref[...], (fb_ref[:C, :], fb_ref[C:, :]), (fa_ref[:C, :], fa_ref[C:, :]), (0, 1, 2, 3))
    for a in range(3):
        for b in range(3):
            t = 3 * a + b
            win[C * t:C * (t + 1), :] = window(ext, (0, C), a - 1, b - 1, masks)
    for m in range(2):
        rows = slice(HALF * m, HALF * (m + 1))
        total = jnp.dot(kern[rows, :], win[...], preferred_element_type=f32)
        out_ref[rows, :] = (total + bias_ref[rows, :]).astype(bf16)


def backward_kernel(core_ref, g_ref, gb_ref, ga_ref, own_ref, other_ref, grad_ref, ext, win, kern):
    load_kernel(core_ref, own_ref, other_ref, kern)
    masks = column_masks(C)
    fill(ext, C, g_ref[...], (gb_ref[:C, :], gb_ref[C:, :]), (ga_ref[:C, :], ga_ref[C:, :]), (0, 1, 2, 3))
    for a in range(3):
        for b in range(3):
            t = 3 * a + b
            win[C * t:C * (t + 1), :] = window(ext, (0, C), 1 - a, 1 - b, masks)
    for m in range(2):
        total = jnp.zeros((HALF, S), f32)
        for t in range(TAPS):
            total = total + lax.dot_general(
                kern[:, C * t + HALF * m:C * t + HALF * (m + 1)],
                win[C * t:C * (t + 1), :],
                (((0,), (0,)), ((), ())),
                preferred_element_type=f32,
            )
        grad_ref[HALF * m:HALF * (m + 1), :] = total.astype(bf16)


def convolve(body, name, *args):
    return pl.pallas_call(
        body,
        out_shape=jax.ShapeDtypeStruct((C, S), bf16),
        in_specs=[smem()] + [vmem()] * (len(args) - 1),
        out_specs=vmem(),
        scratch_shapes=[
            pltpu.VMEM((C, 1152), bf16),
            pltpu.VMEM((TAPS * C, S), bf16),
            pltpu.VMEM((C, TAPS * C), bf16),
        ],
        compiler_params=params(32),
        cost_estimate=pl.CostEstimate(flops=2 * TAPS * C * C * S, bytes_accessed=7_000_000, transcendentals=0),
        name=name,
    )(*args)


def swap_cores(x):
    return lax.ppermute(x, "core", [(0, 1), (1, 0)])


def sum_sources(got, rows, power):
    factor = jnp.exp2(-power)[:, None, None]
    return jnp.sum(got[:, :rows].astype(f32) * factor, axis=0)


def after(values, *first):
    return lax.optimization_barrier((tuple(values), first))[0]


def local(frames, weight, bias, cotangent):
    f = frames.reshape(C, S)
    g = cotangent.reshape(C, S)
    core = lax.axis_index("core")
    place = jnp.stack((core, lax.axis_index("xl"))).astype(jnp.int32)
    up = [(i, i + 1) for i in range(63)]
    down = [(i + 1, i) for i in range(63)]
    plane = ("y", "xh", "xl")

    fl, ff, gl, gf, swap = pack(place, f, g)
    swapped = swap_cores(swap)
    taps = weight.transpose(1, 2, 0, 3).reshape(TAPS, 32, C)
    half = lax.dynamic_slice_in_dim(taps, core * HALF, HALF, axis=2)
    (half,) = after((half,), fl)
    beside = lax.ppermute(half, "xl", [(0, 1), (1, 0)])
    fl, ff = after((fl, ff), swapped)
    fb = lax.ppermute(fl, CELLS, up)
    fa = lax.ppermute(ff, CELLS, down)

    part = middle_taps(place, f, g, swapped)
    part, fb, fa = lax.optimization_barrier((part, fb, fa))
    got = lax.all_to_all(part.astype(f16), plane, 0, 0, tiled=True)
    halo = swap_cores(jnp.stack((fb, fa)))

    half, beside = after((half, beside), fb, fa)
    own = lax.all_gather(jnp.stack((half, beside)), "z", axis=0, tiled=False)
    other = swap_cores(own)

    part2 = outer_taps(place, f, g, fb, fa, swapped, halo)
    got2 = lax.all_to_all(part2.astype(f16), plane, 0, 0, tiled=True)
    gl, gf = after((gl, gf), part2)
    gb = lax.ppermute(gl, CELLS, up)
    ga = lax.ppermute(gf, CELLS, down)

    extra, extra2 = lax.optimization_barrier((got[:, 192:200], got2[:, 384:392]))
    extra = extra.astype(f32)
    extra2 = extra2.astype(f32)
    middle = sum_sources(got, 192, extra[:, 0, 8]).reshape(3, 8, 8, 128)
    outer = sum_sources(got2, 384, extra2[:, 0, 8]).reshape(6, 8, 8, 128)
    ends = jnp.sum(extra * jnp.exp2(-extra[:, 0, 9])[:, None, None], axis=0)
    ends = jnp.broadcast_to(ends[:, :8].T[:, :, None], (8, 8, 128))[None]
    line = jnp.concatenate((outer[:3], middle, outer[3:], ends), axis=0).transpose(1, 0, 2, 3)
    lines = lax.all_to_all(line, "z", 0, 0, tiled=True)
    (f,) = after((f,), line, gb, ga)
    outputs = convolve(forward_kernel, "forward", place, f, fb, fa, own, other, bias.reshape(C, 1))
    lines, outputs = lax.optimization_barrier((lines, outputs))
    scale = 1.0 / math.sqrt(4 * 256 * 160)
    done = jnp.sum(lines, axis=0) * scale
    whole = jnp.broadcast_to(done, (16, 10, 8, 128))
    whole, g = lax.optimization_barrier((whole, g))
    whole = lax.all_to_all(whole, ("y", "xh", "core"), 0, 0, tiled=True)
    grad_frames = convolve(backward_kernel, "backward", place, g, gb, ga, own, other)
    whole, grad_frames = lax.optimization_barrier((whole, grad_frames))
    whole = whole.reshape(4, 2, 2, 10, 8, 128)
    grad_weight = whole[:, :, :, :9].reshape(4, 2, 2, 3, 3, 8, 128)
    grad_weight = grad_weight.transpose(0, 5, 3, 4, 2, 1, 6).reshape(32, 3, 3, C)
    grad_bias = whole[:, 0, 0, 9, :, 0].reshape(32)
    return (outputs.reshape(C, 1, S), grad_frames.reshape(C, 1, S), grad_weight, grad_bias)


def solution(mesh):
    fine = Mesh(mesh.devices.reshape(SIZES), AXES)
    cells = P(None, "y", CELLS)
    rows = ("xl", "z")
    in_specs = (cells, P(rows, None, None, None), P(), cells)
    out_specs = (cells, cells, P(rows, None, None, None), P(rows))
    return jax.shard_map(local, mesh=fine, in_specs=in_specs, out_specs=out_specs, check_vma=False)
```

time: 197 us -> 145 us (0.74)
  blocking collectives: 27.2 us -> 0 us
  waiting for transfers between devices: 51.2 us -> 36.5 us
  local copies, waits for them, and re-layouts: 27.8 us -> 13.7 us
  starting transfers between devices: 36.9 us -> 47.3 us
  other arithmetic: 14.2 us -> 8.32 us
    all_to_all x2 -> x4, waiting for transfers between devices: 41.6 us -> 13.1 us  [the longest x1 5.85 us: local(): got = lax.all_to_all(part.astype(f16), plane, 0, 0, tiled=True)]
    all_gather x1 -> x0, blocking collectives: 27.2 us -> none  [local(): whole = lax.all_gather(done, ('y', 'xh', 'core'), axis=0, tiled=False)]
    convert_element_type x1 -> x0, local copies, waits for them, and re-layouts: 20.6 us -> none  [local(): got = got.reshape(16, 8, ROWS, 128).astype(f32)]
    all_gather x1, waiting for transfers between devices: 0.02 us -> 12.9 us  [local(): own = lax.all_gather(jnp.stack((half, beside)), 'z', axis=0, tiled=False)]
    all_to_all x2 -> x4, starting transfers between devices: 13.5 us -> 20.5 us  [the longest x1 6.74 us: local(): got = lax.all_to_all(part.astype(f16), plane, 0, 0, tiled=True)]
    unnamed x18 -> x32, local copies, waits for them, and re-layouts: 2.41 us -> 9.36 us
    convert_element_type x2 -> x3, other arithmetic: 9.03 us -> 2.47 us  [the longest x1 1.44 us: local(): got2 = lax.all_to_all(part2.astype(f16), plane, 0, 0, tiled=True)]
    ppermute x1, waiting for transfers between devices: 0.01 us -> 4.73 us  [local(): gb = lax.ppermute(gl, CELLS, up)]
  transfers between devices with their start and end apart: 11 -> 13, of which waited for: 6 -> 8; matrix products, arithmetic and copies ran while one was open for 19% -> 6% of each run, Pallas kernels for 5% -> 15%
where the time goes in v2:
time: 145 us; the launch traced here: 144 us
  starting transfers between devices  47.3 us (33%)
  waiting for transfers between devices  36.5 us (25%)
  Pallas kernels  23.7 us (16%)
  between operations  14.3 us (10%)
  local copies, waits for them, and re-layouts  13.7 us (9%)
  other arithmetic  8.32 us (6%)
    pallas_call x2, Pallas kernels, convolve(): pl.pallas_call(body, out_shape=jax.ShapeDtypeStruct((C, S), bf16), in_spe...  15.7 us
    all_gather x1, waiting for transfers between devices, local(): own = lax.all_gather(jnp.stack((half, beside)), 'z', axis=0, tiled=False)  12.9 us
    unnamed x32, local copies, waits for them, and re-layouts  9.36 us
    ppermute x3, starting transfers between devices, swap_cores(): return lax.ppermute(x, 'core', [(0, 1), (1, 0)])  7.63 us
    ppermute x1, starting transfers between devices, local(): fa = lax.ppermute(ff, CELLS, down)  6.94 us
    ppermute x1, starting transfers between devices, local(): ga = lax.ppermute(gf, CELLS, down)  6.84 us
    all_to_all x1, starting transfers between devices, local(): got = lax.all_to_all(part.astype(f16), plane, 0, 0, tiled=True)  6.74 us
    all_to_all x1, waiting for transfers between devices, local(): got = lax.all_to_all(part.astype(f16), plane, 0, 0, tiled=True)  5.85 us
  transfers between devices with their start and end apart: 13, of which 8 were waited for; matrix products, arithmetic and copies ran while one was open for 6% of the time, Pallas kernels for 15%

profile of v2, /device:TPU:1, one launch (start us, length us, event | category | flops | bytes accessed | tf_op | source)
XLA Modules:
  0.0 143.9 jit_solution(4205456625625920184)
XLA Ops:
  7.3 1.1 copy-done.1
  8.4 1.1 copy-done.3
  9.5 1.8 %pack.1 = (bf16[640,128]{1,0:T(8,128)(2,1)}, bf16[640,128]{1,0:T(8,128)(2,1)}, bf16[640,128]{1,0:T(8,128)(2,1)S(1)}, bf16[640,128]{1,0:T(8,128)(2,1)S(1)}, bf16[768,640]{1,0:T(8,128)(2,1)}) custom-call(s32[2]{0:T(128)S(1)} %pad_add_fusion.core_ref, bf16[512,640]{1,0:T(8,128)(2,1)S(1)} %bitcast.28, bf16[512,640]{1,0:T(8,128)(2,1)S(1)} %bitcast.32), custom_call_target="tpu_custom_call" | custom-call | tf_op jit(solution)/shard_map/pack/pallas_call | solution.py:62
  11.3 0.7 copy-done.10
  11.9 0.7 copy-done.12
  12.6 3.2 %collective-permute-start = (bf16[768,640]{1,0:T(8,128)(2,1)}, bf16[768,640]{1,0:T(8,128)(2,1)S(1)}, u32[]{:S(2)}, u32[]{:S(2)}) collective-permute-start(bf16[768,640]{1,0:T(8,128)(2,1)} %get-tuple-element.28), channel_id=1, source_target_pairs={{0,16},{16,0},{1,17},{17,1},{2,18},{18,2},{3,19},{19,3},{4,20},{20... | collective-permute-start | bytes 2949128 | tf_op jit(solution)/shard_map/ppermute | solution.py:286
  15.8 2.4 %collective-permute-done.swap_ref = bf16[768,640]{1,0:T(8,128)(2,1)S(1)} collective-permute-done((bf16[768,640]{1,0:T(8,128)(2,1)}, bf16[768,640]{1,0:T(8,128)(2,1)S(1)}, u32[]{:S(2)}, u32[]{:S(2)}) %collective-permute-start) | collective-permute-done | bytes 983072 | tf_op jit(solution)/shard_map/ppermute | solution.py:286
  18.2 1.0 copy-done.5
  19.2 1.9 %collective-permute-start.1 = (bf16[640,128]{1,0:T(8,128)(2,1)}, bf16[640,128]{1,0:T(8,128)(2,1)S(1)}, u32[]{:S(2)}, u32[]{:S(2)}) collective-permute-start(bf16[640,128]{1,0:T(8,128)(2,1)} %get-tuple-element.31), channel_id=1, source_target_pairs={{0,1},{1,2},{2,3},{3,4},{4,5},{5,6},{6,7},{7,8},{8,9},{9,10},{10,1... | collective-permute-start | bytes 491528 | tf_op jit(solution)/shard_map/ppermute | solution.py:314
  21.1 6.9 %collective-permute-start.2 = (bf16[640,128]{1,0:T(8,128)(2,1)}, bf16[640,128]{1,0:T(8,128)(2,1)}, u32[]{:S(2)}, u32[]{:S(2)}) collective-permute-start(bf16[640,128]{1,0:T(8,128)(2,1)} %get-tuple-element.32), channel_id=1, source_target_pairs={{1,0},{2,1},{3,2},{4,3},{5,4},{6,5},{7,6},{8,7},{9,8},{10,9},{11,1... | collective-permute-start | bytes 491528 | tf_op jit(solution)/shard_map/ppermute | solution.py:315
  28.1 0.1 collective-permute-start.6
  28.2 1.2 copy-done.6
  29.4 2.2 %middle_taps.1 = f32[16,208,128]{2,1,0:T(8,128)S(1)} custom-call(s32[2]{0:T(128)S(1)} %pad_add_fusion.core_ref, bf16[512,640]{1,0:T(8,128)(2,1)S(1)} %bitcast.29, bf16[512,640]{1,0:T(8,128)(2,1)S(1)} %bitcast.33, bf16[768,640]{1,0:T(8,128)(2,1)S(1)} %copy-done.6), custom_call_target="tpu_custom_call" | custom-call | flops 1006632960 | bytes 5000000 | tf_op jit(solution)/shard_map/middle_taps/pallas_call | solution.py:161
  31.7 2.1 %collective-permute-done.6 = bf16[9,32,256]{2,1,0:T(8,128)(2,1)S(1)} collective-permute-done((bf16[9,32,256]{2,1,0:T(8,128)(2,1)S(1)}, bf16[9,32,256]{2,1,0:T(8,128)(2,1)S(1)}, u32[]{:S(2)}, u32[]{:S(2)}) %collective-permute-start.6) | collective-permute-done | bytes 147488 | tf_op jit(solution)/shard_map/ppermute | solution.py:312
  33.8 0.7 pad_maximum_fusion.1
  34.6 1.0 convert_element_type.18
  35.6 6.7 %all-to-all-start.1 = ((f16[16,208,128]{2,1,0:T(8,128)(2,1)}), f16[16,208,128]{2,1,0:T(8,128)(2,1)}, u32[]{:S(2)}, u32[]{:S(2)}) async-start(f16[16,208,128]{2,1,0:T(8,128)(2,1)} %convert_element_type.18), calls=%async_computation.1 | async-start | bytes 1703936 | tf_op jit(solution)/shard_map/all_to_all | solution.py:319
  42.3 0.9 pad_maximum_fusion
  43.3 0.8 collective-permute-start.3
  44.0 1.3 collective-permute-done.3.halo_ref
  45.3 4.0 %outer_taps.1 = f32[16,400,128]{2,1,0:T(8,128)S(1)} custom-call(s32[2]{0:T(128)S(1)} %pad_add_fusion.core_ref, bf16[512,640]{1,0:T(8,128)(2,1)S(1)} %bitcast.30, bf16[512,640]{1,0:T(8,128)(2,1)S(1)} %bitcast.34, bf16[640,128]{1,0:T(8,128)(2,1)S(1)} %collective-permute-done.1.before_ref.fb_ref, bf16[640,128]{1,0:T(8,128)(2,1)} %collective-permute-done.2.after_ref.fa_ref, ...), custom_call_target="tpu_custom_call" | custom-call | flops 2013265920 | bytes 7000000 | tf_op jit(solution)/shard_map/outer_taps/pallas_call | solution.py:208
  49.3 1.4 %convert_element_type.16 = f16[16,400,128]{2,1,0:T(8,128)(2,1)} convert(f32[16,400,128]{2,1,0:T(8,128)S(1)} %outer_taps.1) | non-fusion elementwise | flops 819200 | bytes 4915200 | tf_op jit(solution)/shard_map/convert_element_type | solution.py:327
  50.7 5.9 %all-to-all-done.1 = f16[16,208,128]{2,1,0:T(8,128)(2,1)} async-done(((f16[16,208,128]{2,1,0:T(8,128)(2,1)}), f16[16,208,128]{2,1,0:T(8,128)(2,1)}, u32[]{:S(2)}, u32[]{:S(2)}) %all-to-all-start.1) | async-done | bytes 852000 | tf_op jit(solution)/shard_map/all_to_all | solution.py:319
  56.6 3.8 %all-to-all-start = ((f16[16,400,128]{2,1,0:T(8,128)(2,1)}), f16[16,400,128]{2,1,0:T(8,128)(2,1)S(1)}, u32[]{:S(2)}, u32[]{:S(2)}) async-start(f16[16,400,128]{2,1,0:T(8,128)(2,1)} %convert_element_type.16), calls=%async_computation | async-start | bytes 3276800 | tf_op jit(solution)/shard_map/all_to_all | solution.py:327
  60.4 12.9 %all-gather.3.cloned.1.call-done = bf16[16,9,32,256]{3,2,1,0:T(8,128)(2,1)} async-done(((bf16[2,9,32,256]{3,2,1,0:T(8,128)(2,1)}), bf16[16,9,32,256]{3,2,1,0:T(8,128)(2,1)}) %all-gather.3.cloned.1.call-update) | async-done | bytes 2359312 | tf_op jit(solution)/shard_map/all_gather | solution.py:323
  73.2 3.6 %collective-permute-start.7 = (bf16[8,2,9,32,256]{4,3,2,1,0:T(8,128)(2,1)}, bf16[8,2,9,32,256]{4,3,2,1,0:T(8,128)(2,1)}, u32[]{:S(2)}, u32[]{:S(2)}) collective-permute-start(bf16[8,2,9,32,256]{4,3,2,1,0:T(8,128)(2,1)} %bitcast.37), channel_id=1, source_target_pairs={{0,16},{16,0},{1,17},{17,1},{2,18},{18,2},{3,19},{19,3},{4,20},{20... | collective-permute-start | bytes 7077896 | tf_op jit(solution)/shard_map/ppermute | solution.py:286
  76.9 0.8 slice.61
  77.6 4.2 %all-to-all-done = f16[16,400,128]{2,1,0:T(8,128)(2,1)S(1)} async-done(((f16[16,400,128]{2,1,0:T(8,128)(2,1)}), f16[16,400,128]{2,1,0:T(8,128)(2,1)S(1)}, u32[]{:S(2)}, u32[]{:S(2)}) %all-to-all-start) | async-done | bytes 1638432 | tf_op jit(solution)/shard_map/all_to_all | solution.py:327
  81.8 0.4 fusion.4
  82.4 0.3 exponential_reduce_fusion
  82.7 0.3 copy-done.14
  83.0 1.4 multiply_reduce_fusion.1
  84.5 1.9 %multiply_reduce_fusion = f32[384,128]{1,0:T(8,128)S(1)} fusion(f16[16,400,128]{2,1,0:T(8,128)(2,1)} %copy-done.14, f32[16]{0:T(128)S(1)} %exponential_reduce_fusion), kind=kLoop, calls=%fused_computation | loop fusion | flops 2310144 | bytes 1769536 | tf_op jit(solution)/shard_map/reduce_sum | solution.py:291
  86.5 0.7 copy.21
  87.2 4.8 %all-to-all-start.2 = ((f32[8,10,8,128]{3,2,1,0:T(8,128)}), f32[8,10,8,128]{3,2,1,0:T(8,128)S(1)}, u32[]{:S(2)}, u32[]{:S(2)}) async-start(f32[8,10,8,128]{3,2,1,0:T(8,128)} %copy.21), calls=%async_computation.2 | async-start | bytes 655360 | tf_op jit(solution)/shard_map/all_to_all | solution.py:340
  92.0 3.4 %collective-permute-start.4 = (bf16[640,128]{1,0:T(8,128)(2,1)S(1)}, bf16[640,128]{1,0:T(8,128)(2,1)S(1)}, u32[]{:S(2)}, u32[]{:S(2)}) collective-permute-start(bf16[640,128]{1,0:T(8,128)(2,1)S(1)} %copy-done.13), channel_id=1, source_target_pairs={{0,1},{1,2},{2,3},{3,4},{4,5},{5,6},{6,7},{7,8},{8,9},{9,10},{10,1... | collective-permute-start | bytes 491528 | tf_op jit(solution)/shard_map/ppermute | solution.py:329
  95.4 6.8 %collective-permute-start.5 = (bf16[640,128]{1,0:T(8,128)(2,1)S(1)}, bf16[640,128]{1,0:T(8,128)(2,1)S(1)}, u32[]{:S(2)}, u32[]{:S(2)}) collective-permute-start(bf16[640,128]{1,0:T(8,128)(2,1)S(1)} %copy-done.11), channel_id=1, source_target_pairs={{1,0},{2,1},{3,2},{4,3},{5,4},{6,5},{7,6},{8,7},{9,8},{10,9},{11,1... | collective-permute-start | bytes 491528 | tf_op jit(solution)/shard_map/ppermute | solution.py:330
  102.2 0.1 copy.22.bias_ref
  102.4 4.7 %collective-permute-done.4.gb_ref = bf16[640,128]{1,0:T(8,128)(2,1)S(1)} collective-permute-done((bf16[640,128]{1,0:T(8,128)(2,1)S(1)}, bf16[640,128]{1,0:T(8,128)(2,1)S(1)}, u32[]{:S(2)}, u32[]{:S(2)}) %collective-permute-start.4) | collective-permute-done | bytes 163872 | tf_op jit(solution)/shard_map/ppermute | solution.py:329
  107.1 1.7 %copy-done.8 = bf16[16,9,32,256]{3,2,1,0:T(8,128)(2,1)S(1)} copy-done((bf16[16,9,32,256]{3,2,1,0:T(8,128)(2,1)S(1)}, bf16[16,9,32,256]{3,2,1,0:T(8,128)(2,1)}, u32[]{:S(2)}) %copy-start.8) | copy-done | bytes 2359320
  108.8 7.7 %forward.1 = bf16[512,640]{1,0:T(8,128)(2,1)} custom-call(s32[2]{0:T(128)S(1)} %pad_add_fusion.core_ref, bf16[512,640]{1,0:T(8,128)(2,1)S(1)} %bitcast.31, bf16[640,128]{1,0:T(8,128)(2,1)S(1)} %collective-permute-done.1.before_ref.fb_ref, bf16[640,128]{1,0:T(8,128)(2,1)} %collective-permute-done.2.after_ref.fa_ref, bf16[8,2,9,32,256]{4,3,2,1,0:T(8,128)(2,1)S(1)} %bitcast.38, ...), custom_call_target="tpu_custom_call" | custom-call | flops 3019898880 | bytes 7000000 | tf_op jit(solution)/shard_map/forward/pallas_call | solution.py:269
  116.6 0.9 broadcast_in_dim.2
  117.5 5.3 %all-to-all-start.3 = ((f32[16,10,8,128]{3,2,1,0:T(8,128)}), f32[16,10,8,128]{3,2,1,0:T(8,128)S(1)}, u32[]{:S(2)}, u32[]{:S(2)}) async-start(f32[16,10,8,128]{3,2,1,0:T(8,128)} %broadcast_in_dim.2), calls=%async_computation.3 | async-start | bytes 1310720 | tf_op jit(solution)/shard_map/all_to_all | solution.py:348
  122.7 1.7 %copy-done.9 = bf16[16,9,32,256]{3,2,1,0:T(8,128)(2,1)S(1)} copy-done((bf16[16,9,32,256]{3,2,1,0:T(8,128)(2,1)S(1)}, bf16[16,9,32,256]{3,2,1,0:T(8,128)(2,1)}, u32[]{:S(2)}) %copy-start.9) | copy-done | bytes 2359320
  124.4 8.0 %backward.1 = bf16[512,640]{1,0:T(8,128)(2,1)} custom-call(s32[2]{0:T(128)S(1)} %pad_add_fusion.core_ref, bf16[512,640]{1,0:T(8,128)(2,1)S(1)} %bitcast.35, bf16[640,128]{1,0:T(8,128)(2,1)S(1)} %collective-permute-done.4.gb_ref, bf16[640,128]{1,0:T(8,128)(2,1)S(1)} %collective-permute-done.5.ga_ref, bf16[8,2,9,32,256]{4,3,2,1,0:T(8,128)(2,1)S(1)} %bitcast.39, ...), custom_call_target="tpu_custom_call" | custom-call | flops 3019898880 | bytes 7000000 | tf_op jit(solution)/shard_map/backward/pallas_call | solution.py:269
  132.4 3.0 %all-to-all-done.3 = f32[16,10,8,128]{3,2,1,0:T(8,128)S(1)} async-done(((f32[16,10,8,128]{3,2,1,0:T(8,128)}), f32[16,10,8,128]{3,2,1,0:T(8,128)S(1)}, u32[]{:S(2)}, u32[]{:S(2)}) %all-to-all-start.3) | async-done | bytes 655392 | tf_op jit(solution)/shard_map/all_to_all | solution.py:348
  135.5 0.9 copy.23
  136.4 0.6 reshape_squeeze.3
  (44 shorter events, 0.7 us)
Async XLA Ops:
  7.2 20.9 %copy-start = (bf16[32,3,3,512]{3,0,2,1:T(8,128)(2,1)S(1)}, bf16[32,3,3,512]{3,0,2,1:T(8,128)(2,1)}, u32[]{:S(2)}) copy-start(bf16[32,3,3,512]{3,0,2,1:T(8,128)(2,1)} %param.5) | copy-start | bytes 884740
  7.2 66.1 %all-gather.3.cloned.1.call-start = ((), (), s32[]{:S(2)}) async-start(), calls=%async_computation.4 | async-start | bytes 2654208 | tf_op jit(solution)/shard_map/all_gather | solution.py:323
  7.3 1.1 copy-start.1
  8.4 1.1 copy-start.3
  9.5 18.7 %copy-start.2 = (bf16[512,1,640]{2,0,1:T(8,128)(2,1)S(1)}, bf16[512,1,640]{2,0,1:T(8,128)(2,1)}, u32[]{:S(2)}) copy-start(bf16[512,1,640]{2,0,1:T(8,128)(2,1)} %param.4) | copy-start | bytes 1966084
  9.5 18.7 %copy-start.4 = (bf16[512,1,640]{2,0,1:T(8,128)(2,1)S(1)}, bf16[512,1,640]{2,0,1:T(8,128)(2,1)}, u32[]{:S(2)}) copy-start(bf16[512,1,640]{2,0,1:T(8,128)(2,1)} %param.7) | copy-start | bytes 1966084
  11.3 0.7 copy-start.10
  11.9 0.7 copy-start.12
  12.6 5.6 %collective-permute-start = (bf16[768,640]{1,0:T(8,128)(2,1)}, bf16[768,640]{1,0:T(8,128)(2,1)S(1)}, u32[]{:S(2)}, u32[]{:S(2)}) collective-permute-start(bf16[768,640]{1,0:T(8,128)(2,1)} %get-tuple-element.28), channel_id=1, source_target_pairs={{0,16},{16,0},{1,17},{17,1},{2,18},{18,2},{3,19},{19,3},{4,20},{20... | collective-permute-start | bytes 2949128 | tf_op jit(solution)/shard_map/ppermute | solution.py:286
  18.2 1.0 copy-start.5
  19.2 12.5 %collective-permute-start.1 = (bf16[640,128]{1,0:T(8,128)(2,1)}, bf16[640,128]{1,0:T(8,128)(2,1)S(1)}, u32[]{:S(2)}, u32[]{:S(2)}) collective-permute-start(bf16[640,128]{1,0:T(8,128)(2,1)} %get-tuple-element.31), channel_id=1, source_target_pairs={{0,1},{1,2},{2,3},{3,4},{4,5},{5,6},{6,7},{7,8},{8,9},{9,10},{10,1... | collective-permute-start | bytes 491528 | tf_op jit(solution)/shard_map/ppermute | solution.py:314
  21.1 10.6 %collective-permute-start.2 = (bf16[640,128]{1,0:T(8,128)(2,1)}, bf16[640,128]{1,0:T(8,128)(2,1)}, u32[]{:S(2)}, u32[]{:S(2)}) collective-permute-start(bf16[640,128]{1,0:T(8,128)(2,1)} %get-tuple-element.32), channel_id=1, source_target_pairs={{1,0},{2,1},{3,2},{4,3},{5,4},{6,5},{7,6},{8,7},{9,8},{10,9},{11,1... | collective-permute-start | bytes 491528 | tf_op jit(solution)/shard_map/ppermute | solution.py:315
  28.1 5.7 %collective-permute-start.6 = (bf16[9,32,256]{2,1,0:T(8,128)(2,1)S(1)}, bf16[9,32,256]{2,1,0:T(8,128)(2,1)S(1)}, u32[]{:S(2)}, u32[]{:S(2)}) collective-permute-start(bf16[9,32,256]{2,1,0:T(8,128)(2,1)S(1)} %constant_dynamic-slice_fusion), channel_id=1, source_target_pairs={{0,8},{8,0},{1,9},{9,1},{2,10},{10,2},{3,11},{11,3},{4,12},{12,4},... | collective-permute-start | bytes 442376 | tf_op jit(solution)/shard_map/ppermute | solution.py:312
  28.2 1.2 copy-start.6
  35.6 9.7 %copy-start.7 = (bf16[768,640]{1,0:T(8,128)(2,1)S(1)}, bf16[768,640]{1,0:T(8,128)(2,1)}, u32[]{:S(2)}) copy-start(bf16[768,640]{1,0:T(8,128)(2,1)} %copy-done.5) | copy-start | bytes 2949124
  35.6 21.0 %all-to-all-start.1 = ((f16[16,208,128]{2,1,0:T(8,128)(2,1)}), f16[16,208,128]{2,1,0:T(8,128)(2,1)}, u32[]{:S(2)}, u32[]{:S(2)}) async-start(f16[16,208,128]{2,1,0:T(8,128)(2,1)} %convert_element_type.18), calls=%async_computation.1 | async-start | bytes 1703936 | tf_op jit(solution)/shard_map/all_to_all | solution.py:319
  43.3 2.0 %collective-permute-start.3 = (bf16[2,640,128]{2,1,0:T(8,128)(2,1)S(1)}, bf16[2,640,128]{2,1,0:T(8,128)(2,1)S(1)}, u32[]{:S(2)}, u32[]{:S(2)}) collective-permute-start(bf16[2,640,128]{2,1,0:T(8,128)(2,1)S(1)} %pad_maximum_fusion), channel_id=1, source_target_pairs={{0,16},{16,0},{1,17},{17,1},{2,18},{18,2},{3,19},{19,3},{4,20},{20... | collective-permute-start | bytes 983048 | tf_op jit(solution)/shard_map/ppermute | solution.py:286
  56.6 25.2 %all-to-all-start = ((f16[16,400,128]{2,1,0:T(8,128)(2,1)}), f16[16,400,128]{2,1,0:T(8,128)(2,1)S(1)}, u32[]{:S(2)}, u32[]{:S(2)}) async-start(f16[16,400,128]{2,1,0:T(8,128)(2,1)} %convert_element_type.16), calls=%async_computation | async-start | bytes 3276800 | tf_op jit(solution)/shard_map/all_to_all | solution.py:327
  73.2 33.9 %collective-permute-start.7 = (bf16[8,2,9,32,256]{4,3,2,1,0:T(8,128)(2,1)}, bf16[8,2,9,32,256]{4,3,2,1,0:T(8,128)(2,1)}, u32[]{:S(2)}, u32[]{:S(2)}) collective-permute-start(bf16[8,2,9,32,256]{4,3,2,1,0:T(8,128)(2,1)} %bitcast.37), channel_id=1, source_target_pairs={{0,16},{16,0},{1,17},{17,1},{2,18},{18,2},{3,19},{19,3},{4,20},{20... | collective-permute-start | bytes 7077896 | tf_op jit(solution)/shard_map/ppermute | solution.py:286
  81.8 1.2 copy-start.14
  84.4 7.6 %copy-start.13 = (bf16[640,128]{1,0:T(8,128)(2,1)S(1)}, bf16[640,128]{1,0:T(8,128)(2,1)}, u32[]{:S(2)}) copy-start(bf16[640,128]{1,0:T(8,128)(2,1)} %copy-done.12) | copy-start | bytes 491524
  84.4 10.9 %copy-start.11 = (bf16[640,128]{1,0:T(8,128)(2,1)S(1)}, bf16[640,128]{1,0:T(8,128)(2,1)}, u32[]{:S(2)}) copy-start(bf16[640,128]{1,0:T(8,128)(2,1)} %copy-done.10) | copy-start | bytes 491524
  84.5 17.8 %copy-start.15 = (f32[512]{0:T(512)S(1)}, f32[512]{0:T(512)}, u32[]{:S(2)}) copy-start(f32[512]{0:T(512)} %param.6) | copy-start | bytes 6148
  87.2 29.3 %all-to-all-start.2 = ((f32[8,10,8,128]{3,2,1,0:T(8,128)}), f32[8,10,8,128]{3,2,1,0:T(8,128)S(1)}, u32[]{:S(2)}, u32[]{:S(2)}) async-start(f32[8,10,8,128]{3,2,1,0:T(8,128)} %copy.21), calls=%async_computation.2 | async-start | bytes 655360 | tf_op jit(solution)/shard_map/all_to_all | solution.py:340
  92.0 15.1 %collective-permute-start.4 = (bf16[640,128]{1,0:T(8,128)(2,1)S(1)}, bf16[640,128]{1,0:T(8,128)(2,1)S(1)}, u32[]{:S(2)}, u32[]{:S(2)}) collective-permute-start(bf16[640,128]{1,0:T(8,128)(2,1)S(1)} %copy-done.13), channel_id=1, source_target_pairs={{0,1},{1,2},{2,3},{3,4},{4,5},{5,6},{6,7},{7,8},{8,9},{9,10},{10,1... | collective-permute-start | bytes 491528 | tf_op jit(solution)/shard_map/ppermute | solution.py:329
  95.4 11.7 %collective-permute-start.5 = (bf16[640,128]{1,0:T(8,128)(2,1)S(1)}, bf16[640,128]{1,0:T(8,128)(2,1)S(1)}, u32[]{:S(2)}, u32[]{:S(2)}) collective-permute-start(bf16[640,128]{1,0:T(8,128)(2,1)S(1)} %copy-done.11), channel_id=1, source_target_pairs={{1,0},{2,1},{3,2},{4,3},{5,4},{6,5},{7,6},{8,7},{9,8},{10,9},{11,1... | collective-permute-start | bytes 491528 | tf_op jit(solution)/shard_map/ppermute | solution.py:330
  107.1 1.7 %copy-start.8 = (bf16[16,9,32,256]{3,2,1,0:T(8,128)(2,1)S(1)}, bf16[16,9,32,256]{3,2,1,0:T(8,128)(2,1)}, u32[]{:S(2)}) copy-start(bf16[16,9,32,256]{3,2,1,0:T(8,128)(2,1)} %all-gather.3.cloned.1.call-done) | copy-start | bytes 7077892
  117.5 18.0 %all-to-all-start.3 = ((f32[16,10,8,128]{3,2,1,0:T(8,128)}), f32[16,10,8,128]{3,2,1,0:T(8,128)S(1)}, u32[]{:S(2)}, u32[]{:S(2)}) async-start(f32[16,10,8,128]{3,2,1,0:T(8,128)} %broadcast_in_dim.2), calls=%async_computation.3 | async-start | bytes 1310720 | tf_op jit(solution)/shard_map/all_to_all | solution.py:348
  122.7 1.7 %copy-start.9 = (bf16[16,9,32,256]{3,2,1,0:T(8,128)(2,1)S(1)}, bf16[16,9,32,256]{3,2,1,0:T(8,128)(2,1)}, u32[]{:S(2)}) copy-start(bf16[16,9,32,256]{3,2,1,0:T(8,128)(2,1)} %all-gather.3.cloned.1.call-done) | copy-start | bytes 7077892
Sparse Core Ops, SparseCore 0:
  34.7 38.5 all-gather.2

commit v3 on v2

--- a/solution.py
+++ b/solution.py
@@ -13,6 +13,7 @@
 W = 160
 S = 640
 TAPS = 9
+GROUPS = (0, 1, 2, 3)
 AXES = ("y", "xh", "core", "xl", "z")
 SIZES = (4, 2, 2, 2, 8)
 CELLS = ("xh", "core", "xl", "z")
@@ -48,25 +49,22 @@
     return jnp.concatenate([wide, total.astype(bf16)], axis=0)
 
 
-def pack_kernel(core_ref, f_ref, g_ref, fl_ref, ff_ref, gl_ref, gf_ref, swap_ref):
-    for x, last, first in ((f_ref, fl_ref, ff_ref), (g_ref, gl_ref, gf_ref)):
-        last[...] = pack_row(x[:, 512:640], x[:, 384:512], 96)
-        first[...] = pack_row(x[:, 0:128], x[:, 128:256], 0)
-    other = pl.multiple_of((1 - core_ref[0]) * HALF, HALF)
-    swap_ref[:HALF, :] = f_ref[pl.ds(other, HALF), :]
-    swap_ref[HALF:, :] = g_ref[...]
-
-
-def pack(core, f, g):
-    row = jax.ShapeDtypeStruct((640, 128), bf16)
+def pack_kernel(f_ref, g_ref, last_ref, first_ref):
+    for k, x in enumerate((f_ref, g_ref)):
+        last_ref[k] = pack_row(x[:, 512:640], x[:, 384:512], 96)
+        first_ref[k] = pack_row(x[:, 0:128], x[:, 128:256], 0)
+
+
+def pack(f, g):
+    rows = jax.ShapeDtypeStruct((2, 640, 128), bf16)
     return pl.pallas_call(
         pack_kernel,
-        out_shape=(row, row, row, row, jax.ShapeDtypeStruct((HALF + C, S), bf16)),
-        in_specs=[smem(), vmem(), vmem()],
-        out_specs=(vmem(),) * 5,
+        out_shape=(rows, rows),
+        in_specs=[vmem(), vmem()],
+        out_specs=(vmem(), vmem()),
         compiler_params=params(12),
         name="pack",
-    )(core, f, g)
+    )(f, g)
 
 
 def column_masks(rows):
@@ -121,15 +119,15 @@
     return lax.dot_general(cot, win, (((1,), (1,)), ((), ())), preferred_element_type=f32)
 
 
-def middle_kernel(core_ref, f_ref, g_ref, swap_ref, out_ref, ext, win, cot):
+def middle_kernel(core_ref, f_ref, g_ref, fx_ref, gx_ref, out_ref, ext, win, cot):
     core = core_ref[0]
     mine = pl.multiple_of(core * HALF, HALF)
     masks = column_masks(HALF)
     cot[:, :S] = g_ref[...]
-    cot[:, S:] = swap_ref[HALF:, :]
+    cot[:, S:] = gx_ref[...]
     ext[...] = jnp.zeros_like(ext)
     for seg in range(2):
-        ext[:, 256:896] = f_ref[pl.ds(mine, HALF), :] if seg == 0 else swap_ref[:HALF, :]
+        ext[:, 256:896] = (f_ref, fx_ref)[seg][pl.ds(mine, HALF), :]
         for b in range(3):
             win[b, :, S * seg:S * (seg + 1)] = window(ext, (0, HALF), 0, b - 1, masks)
     peak = jnp.zeros((16, 128), f32)
@@ -157,11 +155,11 @@
         out_ref[d, :192, :] = out_ref[d, :192, :] * factor
 
 
-def middle_taps(core, f, g, swapped):
+def middle_taps(core, f, g, fx, gx):
     return pl.pallas_call(
         middle_kernel,
         out_shape=jax.ShapeDtypeStruct((16, 208, 128), f32),
-        in_specs=[smem()] + [vmem()] * 3,
+        in_specs=[smem()] + [vmem()] * 4,
         out_specs=vmem(),
         scratch_shapes=[
             pltpu.VMEM((HALF, 1152), bf16),
@@ -171,23 +169,23 @@
         compiler_params=params(20),
         cost_estimate=pl.CostEstimate(flops=2 * 3 * C * HALF * 2 * S, bytes_accessed=5_000_000, transcendentals=0),
         name="middle_taps",
-    )(core, f, g, swapped)
-
-
-def outer_kernel(core_ref, f_ref, g_ref, before_ref, after_ref, swap_ref, halo_ref, out_ref, ext, win, cot):
+    )(core, f, g, fx, gx)
+
+
+def outer_kernel(core_ref, f_ref, g_ref, before_ref, after_ref, fx_ref, gx_ref, halo_ref, out_ref, ext, win, cot):
     core = core_ref[0]
     mine = pl.multiple_of(core * HALF, HALF)
     masks = column_masks(HALF)
     groups = (2 * core, 2 * core + 1)
     cot[:, :S] = g_ref[...]
-    cot[:, S:] = swap_ref[HALF:, :]
+    cot[:, S:] = gx_ref[...]
     for seg in range(2):
         if seg == 0:
             cells = f_ref[pl.ds(mine, HALF), :]
-            before = (before_ref[pl.ds(mine, HALF), :], before_ref[C:, :])
-            after = (after_ref[pl.ds(mine, HALF), :], after_ref[C:, :])
+            before = (before_ref[0, pl.ds(mine, HALF), :], before_ref[0, C:, :])
+            after = (after_ref[0, pl.ds(mine, HALF), :], after_ref[0, C:, :])
         else:
-            cells = swap_ref[:HALF, :]
+            cells = fx_ref[pl.ds(mine, HALF), :]
             before = (halo_ref[0, pl.ds(mine, HALF), :], halo_ref[0, C:, :])
             after = (halo_ref[1, pl.ds(mine, HALF), :], halo_ref[1, C:, :])
         fill(ext, HALF, cells, before, after, groups)
@@ -204,11 +202,11 @@
         out_ref[d, 384:400, :] = jnp.broadcast_to(power, (16, 128))
 
 
-def outer_taps(core, f, g, before, after, swapped, halo):
+def outer_taps(core, f, g, before, after, fx, gx, halo):
     return pl.pallas_call(
         outer_kernel,
         out_shape=jax.ShapeDtypeStruct((16, 400, 128), f32),
-        in_specs=[smem()] + [vmem()] * 6,
+        in_specs=[smem()] + [vmem()] * 7,
         out_specs=vmem(),
         scratch_shapes=[
             pltpu.VMEM((HALF, 1152), bf16),
@@ -218,7 +216,7 @@
         compiler_params=params(24),
         cost_estimate=pl.CostEstimate(flops=2 * 6 * C * HALF * 2 * S, bytes_accessed=7_000_000, transcendentals=0),
         name="outer_taps",
-    )(core, f, g, before, after, swapped, halo)
+    )(core, f, g, before, after, fx, gx, halo)
 
 
 def load_kernel(place_ref, own_ref, other_ref, kern):
@@ -231,10 +229,10 @@
                 kern[pl.ds(first, HALF), lanes] = ref[:, k, t].reshape(HALF, HALF)
 
 
-def forward_kernel(core_ref, f_ref, fb_ref, fa_ref, own_ref, other_ref, bias_ref, out_ref, ext, win, kern):
+def forward_kernel(core_ref, f_ref, before_ref, after_ref, own_ref, other_ref, bias_ref, out_ref, ext, win, kern):
     load_kernel(core_ref, own_ref, other_ref, kern)
     masks = column_masks(C)
-    fill(ext, C, f_ref[...], (fb_ref[:C, :], fb_ref[C:, :]), (fa_ref[:C, :], fa_ref[C:, :]), (0, 1, 2, 3))
+    fill(ext, C, f_ref[...], (before_ref[0, :C, :], before_ref[0, C:, :]), (after_ref[0, :C, :], after_ref[0, C:, :]), GROUPS)
     for a in range(3):
         for b in range(3):
             t = 3 * a + b
@@ -245,10 +243,10 @@
         out_ref[rows, :] = (total + bias_ref[rows, :]).astype(bf16)
 
 
-def backward_kernel(core_ref, g_ref, gb_ref, ga_ref, own_ref, other_ref, grad_ref, ext, win, kern):
+def backward_kernel(core_ref, g_ref, before_ref, after_ref, own_ref, other_ref, grad_ref, ext, win, kern):
     load_kernel(core_ref, own_ref, other_ref, kern)
     masks = column_masks(C)
-    fill(ext, C, g_ref[...], (gb_ref[:C, :], gb_ref[C:, :]), (ga_ref[:C, :], ga_ref[C:, :]), (0, 1, 2, 3))
+    fill(ext, C, g_ref[...], (before_ref[1, :C, :], before_ref[1, C:, :]), (after_ref[1, :C, :], after_ref[1, C:, :]), GROUPS)
     for a in range(3):
         for b in range(3):
             t = 3 * a + b
@@ -304,49 +302,45 @@
     down = [(i + 1, i) for i in range(63)]
     plane = ("y", "xh", "xl")
 
-    fl, ff, gl, gf, swap = pack(place, f, g)
-    swapped = swap_cores(swap)
+    fx = swap_cores(f)
+    gx = swap_cores(g)
+    last, first = pack(f, g)
+    above = lax.ppermute(last, CELLS, up)
+    below = lax.ppermute(first, CELLS, down)
+
+    part = middle_taps(place, f, g, fx, gx)
+    sent = part.astype(f16)
+    got = lax.all_to_all(sent, plane, 0, 0, tiled=True)
+    near = after((above[0], below[0]), sent)
+    halo = swap_cores(jnp.stack(near))
+
     taps = weight.transpose(1, 2, 0, 3).reshape(TAPS, 32, C)
     half = lax.dynamic_slice_in_dim(taps, core * HALF, HALF, axis=2)
-    (half,) = after((half,), fl)
     beside = lax.ppermute(half, "xl", [(0, 1), (1, 0)])
-    fl, ff = after((fl, ff), swapped)
-    fb = lax.ppermute(fl, CELLS, up)
-    fa = lax.ppermute(ff, CELLS, down)
-
-    part = middle_taps(place, f, g, swapped)
-    part, fb, fa = lax.optimization_barrier((part, fb, fa))
-    got = lax.all_to_all(part.astype(f16), plane, 0, 0, tiled=True)
-    halo = swap_cores(jnp.stack((fb, fa)))
-
-    half, beside = after((half, beside), fb, fa)
+    half, beside = after((half, beside), above, below, sent)
     own = lax.all_gather(jnp.stack((half, beside)), "z", axis=0, tiled=False)
+
+    part2 = outer_taps(place, f, g, above, below, fx, gx, halo)
+    got2 = lax.all_to_all(part2.astype(f16), plane, 0, 0, tiled=True)
     other = swap_cores(own)
 
-    part2 = outer_taps(place, f, g, fb, fa, swapped, halo)
-    got2 = lax.all_to_all(part2.astype(f16), plane, 0, 0, tiled=True)
-    gl, gf = after((gl, gf), part2)
-    gb = lax.ppermute(gl, CELLS, up)
-    ga = lax.ppermute(gf, CELLS, down)
-
-    extra, extra2 = lax.optimization_barrier((got[:, 192:200], got2[:, 384:392]))
-    extra = extra.astype(f32)
-    extra2 = extra2.astype(f32)
+    extra = lax.optimization_barrier(got[:, 192:200]).astype(f32)
+    extra2 = lax.optimization_barrier(got2[:, 384:392]).astype(f32)
     middle = sum_sources(got, 192, extra[:, 0, 8]).reshape(3, 8, 8, 128)
     outer = sum_sources(got2, 384, extra2[:, 0, 8]).reshape(6, 8, 8, 128)
     ends = jnp.sum(extra * jnp.exp2(-extra[:, 0, 9])[:, None, None], axis=0)
     ends = jnp.broadcast_to(ends[:, :8].T[:, :, None], (8, 8, 128))[None]
     line = jnp.concatenate((outer[:3], middle, outer[3:], ends), axis=0).transpose(1, 0, 2, 3)
     lines = lax.all_to_all(line, "z", 0, 0, tiled=True)
-    (f,) = after((f,), line, gb, ga)
-    outputs = convolve(forward_kernel, "forward", place, f, fb, fa, own, other, bias.reshape(C, 1))
+    (f,) = after((f,), line)
+    outputs = convolve(forward_kernel, "forward", place, f, above, below, own, other, bias.reshape(C, 1))
     lines, outputs = lax.optimization_barrier((lines, outputs))
     scale = 1.0 / math.sqrt(4 * 256 * 160)
     done = jnp.sum(lines, axis=0) * scale
     whole = jnp.broadcast_to(done, (16, 10, 8, 128))
     whole, g = lax.optimization_barrier((whole, g))
     whole = lax.all_to_all(whole, ("y", "xh", "core"), 0, 0, tiled=True)
-    grad_frames = convolve(backward_kernel, "backward", place, g, gb, ga, own, other)
+    grad_frames = convolve(backward_kernel, "backward", place, g, above, below, own, other)
     whole, grad_frames = lax.optimization_barrier((whole, grad_frames))
     whole = whole.reshape(4, 2, 2, 10, 8, 128)
     grad_weight = whole[:, :, :, :9].reshape(4, 2, 2, 3, 3, 8, 128)

time: 145 us -> 130 us (0.90)
  waiting for transfers between devices: 36.5 us -> 29 us
  starting transfers between devices: 47.3 us -> 44 us
  local copies, waits for them, and re-layouts: 13.7 us -> 11.6 us
    ppermute x4 -> x2, starting transfers between devices: 19 us -> 8.88 us  [the longest x1 6.97 us: local(): below = lax.ppermute(first, CELLS, down)]
    ppermute x4 -> x2, waiting for transfers between devices: 4.74 us -> 0.01 us  [the longest x1 0.01 us: local(): above = lax.ppermute(last, CELLS, up)]
    all_to_all x1, starting transfers between devices: 5.25 us -> 9.89 us  [local(): whole = lax.all_to_all(whole, ('y', 'xh', 'core'), 0, 0, tiled=True)]
    unnamed x32 -> x16, local copies, waits for them, and re-layouts: 9.36 us -> 5.51 us
    all_to_all x1, waiting for transfers between devices: 4.18 us -> 0.6 us  [local(): got2 = lax.all_to_all(part2.astype(f16), plane, 0, 0, tiled=True)]
    ppermute x3 -> x4, waiting for transfers between devices: 3.66 us -> 1.26 us  [swap_cores(): return lax.ppermute(x, 'core', [(0, 1), (1, 0)])]
    ppermute x1, waiting for transfers between devices: 2.12 us -> 3.83 us  [local(): beside = lax.ppermute(half, 'xl', [(0, 1), (1, 0)])]
    ppermute x3 -> x4, starting transfers between devices: 7.63 us -> 7.9 us  [swap_cores(): return lax.ppermute(x, 'core', [(0, 1), (1, 0)])]
  transfers between devices with their start and end apart: 13 -> 12, of which waited for: 8 -> 7; matrix products, arithmetic and copies ran while one was open for 6% -> 8% of each run, Pallas kernels for 15% -> 18%
where the time goes in v3:
time: 130 us; the launch traced here: 129 us
  starting transfers between devices  44 us (34%)
  waiting for transfers between devices  29 us (22%)
  Pallas kernels  23.1 us (18%)
  between operations  14.3 us (11%)
  local copies, waits for them, and re-layouts  11.6 us (9%)
  other arithmetic  7.33 us (6%)
    pallas_call x2, Pallas kernels, convolve(): pl.pallas_call(body, out_shape=jax.ShapeDtypeStruct((C, S), bf16), in_spe...  15.8 us
    all_gather x1, waiting for transfers between devices, local(): own = lax.all_gather(jnp.stack((half, beside)), 'z', axis=0, tiled=False)  14.2 us
    all_to_all x1, starting transfers between devices, local(): whole = lax.all_to_all(whole, ('y', 'xh', 'core'), 0, 0, tiled=True)  9.89 us
    ppermute x4, starting transfers between devices, swap_cores(): return lax.ppermute(x, 'core', [(0, 1), (1, 0)])  7.9 us
    all_to_all x1, starting transfers between devices, local(): got = lax.all_to_all(sent, plane, 0, 0, tiled=True)  7.83 us
    ppermute x1, starting transfers between devices, local(): below = lax.ppermute(first, CELLS, down)  6.97 us
    all_to_all x1, waiting for transfers between devices, local(): got = lax.all_to_all(sent, plane, 0, 0, tiled=True)  5.66 us
    unnamed x16, local copies, waits for them, and re-layouts  5.51 us
  transfers between devices with their start and end apart: 12, of which 7 were waited for; matrix products, arithmetic and copies ran while one was open for 8% of the time, Pallas kernels for 18%

profile of v3, /device:TPU:1, one launch (start us, length us, event | category | flops | bytes accessed | tf_op | source)
XLA Modules:
  0.0 129.2 jit_solution(16643033559074300244)
XLA Ops:
  7.2 0.0 all-gather.3.cloned.1.call-start
  7.2 3.3 %collective-permute-start.2 = (bf16[512,640]{1,0:T(8,128)(2,1)}, bf16[512,640]{1,0:T(8,128)(2,1)S(1)}, u32[]{:S(2)}, u32[]{:S(2)}) collective-permute-start(bf16[512,640]{1,0:T(8,128)(2,1)} %bitcast.32), channel_id=1, source_target_pairs={{0,16},{16,0},{1,17},{17,1},{2,18},{18,2},{3,19},{19,3},{4,20},{20... | collective-permute-start | bytes 1966088 | tf_op jit(solution)/shard_map/ppermute | solution.py:284
  10.6 0.1 collective-permute-start.3
  10.7 1.1 copy-done.1
  11.7 1.1 copy-done.3
  12.8 1.0 pack.1
  13.9 1.9 %collective-permute-start = (bf16[2,640,128]{2,1,0:T(8,128)(2,1)}, bf16[2,640,128]{2,1,0:T(8,128)(2,1)S(1)}, u32[]{:S(2)}, u32[]{:S(2)}) collective-permute-start(bf16[2,640,128]{2,1,0:T(8,128)(2,1)} %get-tuple-element.17), channel_id=1, source_target_pairs={{0,1},{1,2},{2,3},{3,4},{4,5},{5,6},{6,7},{7,8},{8,9},{9,10},{10,1... | collective-permute-start | bytes 983048 | tf_op jit(solution)/shard_map/ppermute | solution.py:308
  15.8 7.0 %collective-permute-start.1 = (bf16[2,640,128]{2,1,0:T(8,128)(2,1)}, bf16[2,640,128]{2,1,0:T(8,128)(2,1)}, u32[]{:S(2)}, u32[]{:S(2)}) collective-permute-start(bf16[2,640,128]{2,1,0:T(8,128)(2,1)} %get-tuple-element.18), channel_id=1, source_target_pairs={{1,0},{2,1},{3,2},{4,3},{5,4},{6,5},{7,6},{8,7},{9,8},{10,9},{11,1... | collective-permute-start | bytes 983048 | tf_op jit(solution)/shard_map/ppermute | solution.py:309
  22.8 0.1 collective-permute-start.5
  22.9 0.1 pad_add_fusion.core_ref
  23.0 2.2 %middle_taps.1 = f32[16,208,128]{2,1,0:T(8,128)S(1)} custom-call(s32[2]{0:T(128)S(1)} %pad_add_fusion.core_ref, bf16[512,640]{1,0:T(8,128)(2,1)S(1)} %bitcast.34, bf16[512,640]{1,0:T(8,128)(2,1)S(1)} %bitcast.39, bf16[512,640]{1,0:T(8,128)(2,1)S(1)} %collective-permute-done.2.fx_ref, bf16[512,640]{1,0:T(8,128)(2,1)S(1)} %collective-permute-done.3.gx_ref), custom_call_target="tpu_custom_call" | custom-call | flops 1006632960 | bytes 5000000 | tf_op jit(solution)/shard_map/middle_taps/pallas_call | solution.py:159
  25.2 1.0 convert_element_type.16
  26.3 3.8 %collective-permute-done.5 = bf16[9,32,256]{2,1,0:T(8,128)(2,1)S(1)} collective-permute-done((bf16[9,32,256]{2,1,0:T(8,128)(2,1)S(1)}, bf16[9,32,256]{2,1,0:T(8,128)(2,1)S(1)}, u32[]{:S(2)}, u32[]{:S(2)}) %collective-permute-start.5) | collective-permute-done | bytes 147488 | tf_op jit(solution)/shard_map/ppermute | solution.py:319
  30.1 0.7 pad_maximum_fusion.1
  30.9 7.8 %all-to-all-start.1 = ((f16[16,208,128]{2,1,0:T(8,128)(2,1)}), f16[16,208,128]{2,1,0:T(8,128)(2,1)}, u32[]{:S(2)}, u32[]{:S(2)}) async-start(f16[16,208,128]{2,1,0:T(8,128)(2,1)} %convert_element_type.16), calls=%async_computation.1 | async-start | bytes 1703936 | tf_op jit(solution)/shard_map/all_to_all | solution.py:313
  38.7 0.9 slice_bitcast_fusion
  39.7 0.9 collective-permute-start.4
  40.6 1.3 collective-permute-done.4.halo_ref
  41.8 4.0 %outer_taps.1 = f32[16,400,128]{2,1,0:T(8,128)S(1)} custom-call(s32[2]{0:T(128)S(1)} %pad_add_fusion.core_ref, bf16[512,640]{1,0:T(8,128)(2,1)S(1)} %bitcast.35, bf16[512,640]{1,0:T(8,128)(2,1)S(1)} %bitcast.40, bf16[2,640,128]{2,1,0:T(8,128)(2,1)S(1)} %collective-permute-done.before_ref, bf16[2,640,128]{2,1,0:T(8,128)(2,1)} %collective-permute-done.1.after_ref, ...), custom_call_target="tpu_custom_call" | custom-call | flops 2013265920 | bytes 7000000 | tf_op jit(solution)/shard_map/outer_taps/pallas_call | solution.py:206
  45.8 1.4 %convert_element_type.17 = f16[16,400,128]{2,1,0:T(8,128)(2,1)} convert(f32[16,400,128]{2,1,0:T(8,128)S(1)} %outer_taps.1) | non-fusion elementwise | flops 819200 | bytes 4915200 | tf_op jit(solution)/shard_map/convert_element_type | solution.py:324
  47.2 5.7 %all-to-all-done.1 = f16[16,208,128]{2,1,0:T(8,128)(2,1)} async-done(((f16[16,208,128]{2,1,0:T(8,128)(2,1)}), f16[16,208,128]{2,1,0:T(8,128)(2,1)}, u32[]{:S(2)}, u32[]{:S(2)}) %all-to-all-start.1) | async-done | bytes 852000 | tf_op jit(solution)/shard_map/all_to_all | solution.py:313
  52.9 4.4 %all-to-all-start = ((f16[16,400,128]{2,1,0:T(8,128)(2,1)}), f16[16,400,128]{2,1,0:T(8,128)(2,1)}, u32[]{:S(2)}, u32[]{:S(2)}) async-start(f16[16,400,128]{2,1,0:T(8,128)(2,1)} %convert_element_type.17), calls=%async_computation | async-start | bytes 3276800 | tf_op jit(solution)/shard_map/all_to_all | solution.py:324
  57.3 14.2 %all-gather.3.cloned.1.call-done = bf16[16,9,32,256]{3,2,1,0:T(8,128)(2,1)} async-done(((bf16[2,9,32,256]{3,2,1,0:T(8,128)(2,1)}), bf16[16,9,32,256]{3,2,1,0:T(8,128)(2,1)}) %all-gather.3.cloned.1.call-update) | async-done | bytes 2359312 | tf_op jit(solution)/shard_map/all_gather | solution.py:321
  71.5 3.6 %collective-permute-start.6 = (bf16[8,2,9,32,256]{4,3,2,1,0:T(8,128)(2,1)}, bf16[8,2,9,32,256]{4,3,2,1,0:T(8,128)(2,1)}, u32[]{:S(2)}, u32[]{:S(2)}) collective-permute-start(bf16[8,2,9,32,256]{4,3,2,1,0:T(8,128)(2,1)} %bitcast.42), channel_id=1, source_target_pairs={{0,16},{16,0},{1,17},{17,1},{2,18},{18,2},{3,19},{19,3},{4,20},{20... | collective-permute-start | bytes 7077896 | tf_op jit(solution)/shard_map/ppermute | solution.py:284
  75.1 0.8 slice.75
  75.9 0.4 fusion.8
  76.3 0.1 multiply_reduce_fusion.2
  76.4 0.1 copy.20
  76.5 1.4 %multiply_reduce_fusion.1 = f32[192,128]{1,0:T(8,128)S(1)} fusion(f16[16,208,128]{2,1,0:T(8,128)(2,1)} %all-to-all-done.1, f32[16]{0:T(128)S(1)} %get-tuple-element.30), kind=kLoop, calls=%fused_computation.1 | loop fusion | flops 1155072 | bytes 884800 | tf_op jit(solution)/shard_map/reduce_sum | solution.py:289
  77.9 0.6 all-to-all-done
  78.5 0.8 slice.71
  79.2 0.3 fusion.7
  79.5 1.8 %multiply_reduce_fusion = f32[384,128]{1,0:T(8,128)S(1)} fusion(f16[16,400,128]{2,1,0:T(8,128)(2,1)} %all-to-all-done, f32[16]{0:T(128)S(1)} %fusion.7), kind=kLoop, calls=%fused_computation | loop fusion | flops 2310144 | bytes 1769536 | tf_op jit(solution)/shard_map/reduce_sum | solution.py:289
  81.4 0.1 broadcast_in_dim_broadcast_in_dim.2
  81.5 0.7 copy.21
  82.2 4.9 %all-to-all-start.2 = ((f32[8,10,8,128]{3,2,1,0:T(8,128)}), f32[8,10,8,128]{3,2,1,0:T(8,128)S(1)}, u32[]{:S(2)}, u32[]{:S(2)}) async-start(f32[8,10,8,128]{3,2,1,0:T(8,128)} %copy.21), calls=%async_computation.2 | async-start | bytes 655360 | tf_op jit(solution)/shard_map/all_to_all | solution.py:334
  87.2 0.1 copy.22.bias_ref
  87.3 1.7 %copy-done.5 = bf16[16,9,32,256]{3,2,1,0:T(8,128)(2,1)S(1)} copy-done((bf16[16,9,32,256]{3,2,1,0:T(8,128)(2,1)S(1)}, bf16[16,9,32,256]{3,2,1,0:T(8,128)(2,1)}, u32[]{:S(2)}) %copy-start.5) | copy-done | bytes 2359320
  89.0 7.8 %forward.1 = bf16[512,640]{1,0:T(8,128)(2,1)} custom-call(s32[2]{0:T(128)S(1)} %pad_add_fusion.core_ref, bf16[512,640]{1,0:T(8,128)(2,1)S(1)} %bitcast.36, bf16[2,640,128]{2,1,0:T(8,128)(2,1)S(1)} %collective-permute-done.before_ref, bf16[2,640,128]{2,1,0:T(8,128)(2,1)} %collective-permute-done.1.after_ref, bf16[8,2,9,32,256]{4,3,2,1,0:T(8,128)(2,1)S(1)} %bitcast.43, ...), custom_call_target="tpu_custom_call" | custom-call | flops 3019898880 | bytes 7000000 | tf_op jit(solution)/shard_map/forward/pallas_call | solution.py:267
  96.8 0.5 all-to-all-done.2
  97.3 0.9 broadcast_in_dim.2
  98.1 9.9 %all-to-all-start.3 = ((f32[16,10,8,128]{3,2,1,0:T(8,128)}), f32[16,10,8,128]{3,2,1,0:T(8,128)S(1)}, u32[]{:S(2)}, u32[]{:S(2)}) async-start(f32[16,10,8,128]{3,2,1,0:T(8,128)} %broadcast_in_dim.2), calls=%async_computation.3 | async-start | bytes 1310720 | tf_op jit(solution)/shard_map/all_to_all | solution.py:342
  108.0 1.7 %copy-done.6 = bf16[16,9,32,256]{3,2,1,0:T(8,128)(2,1)S(1)} copy-done((bf16[16,9,32,256]{3,2,1,0:T(8,128)(2,1)S(1)}, bf16[16,9,32,256]{3,2,1,0:T(8,128)(2,1)}, u32[]{:S(2)}) %copy-start.6) | copy-done | bytes 2359320
  109.7 8.1 %backward.1 = bf16[512,640]{1,0:T(8,128)(2,1)} custom-call(s32[2]{0:T(128)S(1)} %pad_add_fusion.core_ref, bf16[512,640]{1,0:T(8,128)(2,1)S(1)} %bitcast.41, bf16[2,640,128]{2,1,0:T(8,128)(2,1)S(1)} %collective-permute-done.before_ref, bf16[2,640,128]{2,1,0:T(8,128)(2,1)} %collective-permute-done.1.after_ref, bf16[8,2,9,32,256]{4,3,2,1,0:T(8,128)(2,1)S(1)} %bitcast.44, ...), custom_call_target="tpu_custom_call" | custom-call | flops 3019898880 | bytes 7000000 | tf_op jit(solution)/shard_map/backward/pallas_call | solution.py:267
  117.8 2.9 %all-to-all-done.3 = f32[16,10,8,128]{3,2,1,0:T(8,128)S(1)} async-done(((f32[16,10,8,128]{3,2,1,0:T(8,128)}), f32[16,10,8,128]{3,2,1,0:T(8,128)S(1)}, u32[]{:S(2)}, u32[]{:S(2)}) %all-to-all-start.3) | async-done | bytes 655392 | tf_op jit(solution)/shard_map/all_to_all | solution.py:342
  120.8 0.1 slice_reduce_fusion
  120.9 0.9 copy.23
  121.8 0.6 reshape_squeeze.3
  (28 shorter events, 0.2 us)
Async XLA Ops:
  7.2 15.6 %copy-start = (bf16[32,3,3,512]{3,0,2,1:T(8,128)(2,1)S(1)}, bf16[32,3,3,512]{3,0,2,1:T(8,128)(2,1)}, u32[]{:S(2)}) copy-start(bf16[32,3,3,512]{3,0,2,1:T(8,128)(2,1)} %param.5) | copy-start | bytes 884740
  7.2 64.3 %all-gather.3.cloned.1.call-start = ((), (), s32[]{:S(2)}) async-start(), calls=%async_computation.4 | async-start | bytes 2654208 | tf_op jit(solution)/shard_map/all_gather | solution.py:321
  7.2 15.8 %collective-permute-start.2 = (bf16[512,640]{1,0:T(8,128)(2,1)}, bf16[512,640]{1,0:T(8,128)(2,1)S(1)}, u32[]{:S(2)}, u32[]{:S(2)}) collective-permute-start(bf16[512,640]{1,0:T(8,128)(2,1)} %bitcast.32), channel_id=1, source_target_pairs={{0,16},{16,0},{1,17},{17,1},{2,18},{18,2},{3,19},{19,3},{4,20},{20... | collective-permute-start | bytes 1966088 | tf_op jit(solution)/shard_map/ppermute | solution.py:284
  10.6 12.4 %collective-permute-start.3 = (bf16[512,640]{1,0:T(8,128)(2,1)}, bf16[512,640]{1,0:T(8,128)(2,1)S(1)}, u32[]{:S(2)}, u32[]{:S(2)}) collective-permute-start(bf16[512,640]{1,0:T(8,128)(2,1)} %bitcast.37), channel_id=1, source_target_pairs={{0,16},{16,0},{1,17},{17,1},{2,18},{18,2},{3,19},{19,3},{4,20},{20... | collective-permute-start | bytes 1966088 | tf_op jit(solution)/shard_map/ppermute | solution.py:284
  10.7 1.1 copy-start.1
  11.7 1.1 copy-start.3
  12.8 10.2 %copy-start.2 = (bf16[512,1,640]{2,0,1:T(8,128)(2,1)S(1)}, bf16[512,1,640]{2,0,1:T(8,128)(2,1)}, u32[]{:S(2)}) copy-start(bf16[512,1,640]{2,0,1:T(8,128)(2,1)} %param.4) | copy-start | bytes 1966084
  12.8 10.2 %copy-start.4 = (bf16[512,1,640]{2,0,1:T(8,128)(2,1)S(1)}, bf16[512,1,640]{2,0,1:T(8,128)(2,1)}, u32[]{:S(2)}) copy-start(bf16[512,1,640]{2,0,1:T(8,128)(2,1)} %param.7) | copy-start | bytes 1966084
  13.9 16.3 %collective-permute-start = (bf16[2,640,128]{2,1,0:T(8,128)(2,1)}, bf16[2,640,128]{2,1,0:T(8,128)(2,1)S(1)}, u32[]{:S(2)}, u32[]{:S(2)}) collective-permute-start(bf16[2,640,128]{2,1,0:T(8,128)(2,1)} %get-tuple-element.17), channel_id=1, source_target_pairs={{0,1},{1,2},{2,3},{3,4},{4,5},{5,6},{6,7},{7,8},{8,9},{9,10},{10,1... | collective-permute-start | bytes 983048 | tf_op jit(solution)/shard_map/ppermute | solution.py:308
  15.8 14.3 %collective-permute-start.1 = (bf16[2,640,128]{2,1,0:T(8,128)(2,1)}, bf16[2,640,128]{2,1,0:T(8,128)(2,1)}, u32[]{:S(2)}, u32[]{:S(2)}) collective-permute-start(bf16[2,640,128]{2,1,0:T(8,128)(2,1)} %get-tuple-element.18), channel_id=1, source_target_pairs={{1,0},{2,1},{3,2},{4,3},{5,4},{6,5},{7,6},{8,7},{9,8},{10,9},{11,1... | collective-permute-start | bytes 983048 | tf_op jit(solution)/shard_map/ppermute | solution.py:309
  22.8 7.3 %collective-permute-start.5 = (bf16[9,32,256]{2,1,0:T(8,128)(2,1)S(1)}, bf16[9,32,256]{2,1,0:T(8,128)(2,1)S(1)}, u32[]{:S(2)}, u32[]{:S(2)}) collective-permute-start(bf16[9,32,256]{2,1,0:T(8,128)(2,1)S(1)} %constant_dynamic-slice_fusion), channel_id=1, source_target_pairs={{0,8},{8,0},{1,9},{9,1},{2,10},{10,2},{3,11},{11,3},{4,12},{12,4},... | collective-permute-start | bytes 442376 | tf_op jit(solution)/shard_map/ppermute | solution.py:319
  30.9 22.0 %all-to-all-start.1 = ((f16[16,208,128]{2,1,0:T(8,128)(2,1)}), f16[16,208,128]{2,1,0:T(8,128)(2,1)}, u32[]{:S(2)}, u32[]{:S(2)}) async-start(f16[16,208,128]{2,1,0:T(8,128)(2,1)} %convert_element_type.16), calls=%async_computation.1 | async-start | bytes 1703936 | tf_op jit(solution)/shard_map/all_to_all | solution.py:313
  39.7 2.1 %collective-permute-start.4 = (bf16[2,640,128]{2,1,0:T(8,128)(2,1)S(1)}, bf16[2,640,128]{2,1,0:T(8,128)(2,1)S(1)}, u32[]{:S(2)}, u32[]{:S(2)}) collective-permute-start(bf16[2,640,128]{2,1,0:T(8,128)(2,1)S(1)} %pad_maximum_fusion), channel_id=1, source_target_pairs={{0,16},{16,0},{1,17},{17,1},{2,18},{18,2},{3,19},{19,3},{4,20},{20... | collective-permute-start | bytes 983048 | tf_op jit(solution)/shard_map/ppermute | solution.py:284
  52.9 25.6 %all-to-all-start = ((f16[16,400,128]{2,1,0:T(8,128)(2,1)}), f16[16,400,128]{2,1,0:T(8,128)(2,1)}, u32[]{:S(2)}, u32[]{:S(2)}) async-start(f16[16,400,128]{2,1,0:T(8,128)(2,1)} %convert_element_type.17), calls=%async_computation | async-start | bytes 3276800 | tf_op jit(solution)/shard_map/all_to_all | solution.py:324
  71.5 15.8 %collective-permute-start.6 = (bf16[8,2,9,32,256]{4,3,2,1,0:T(8,128)(2,1)}, bf16[8,2,9,32,256]{4,3,2,1,0:T(8,128)(2,1)}, u32[]{:S(2)}, u32[]{:S(2)}) collective-permute-start(bf16[8,2,9,32,256]{4,3,2,1,0:T(8,128)(2,1)} %bitcast.42), channel_id=1, source_target_pairs={{0,16},{16,0},{1,17},{17,1},{2,18},{18,2},{3,19},{19,3},{4,20},{20... | collective-permute-start | bytes 7077896 | tf_op jit(solution)/shard_map/ppermute | solution.py:284
  79.5 7.6 %copy-start.7 = (f32[512]{0:T(512)S(1)}, f32[512]{0:T(512)}, u32[]{:S(2)}) copy-start(f32[512]{0:T(512)} %param.6) | copy-start | bytes 6148
  82.2 15.0 %all-to-all-start.2 = ((f32[8,10,8,128]{3,2,1,0:T(8,128)}), f32[8,10,8,128]{3,2,1,0:T(8,128)S(1)}, u32[]{:S(2)}, u32[]{:S(2)}) async-start(f32[8,10,8,128]{3,2,1,0:T(8,128)} %copy.21), calls=%async_computation.2 | async-start | bytes 655360 | tf_op jit(solution)/shard_map/all_to_all | solution.py:334
  87.3 1.7 %copy-start.5 = (bf16[16,9,32,256]{3,2,1,0:T(8,128)(2,1)S(1)}, bf16[16,9,32,256]{3,2,1,0:T(8,128)(2,1)}, u32[]{:S(2)}) copy-start(bf16[16,9,32,256]{3,2,1,0:T(8,128)(2,1)} %all-gather.3.cloned.1.call-done) | copy-start | bytes 7077892
  98.1 22.6 %all-to-all-start.3 = ((f32[16,10,8,128]{3,2,1,0:T(8,128)}), f32[16,10,8,128]{3,2,1,0:T(8,128)S(1)}, u32[]{:S(2)}, u32[]{:S(2)}) async-start(f32[16,10,8,128]{3,2,1,0:T(8,128)} %broadcast_in_dim.2), calls=%async_computation.3 | async-start | bytes 1310720 | tf_op jit(solution)/shard_map/all_to_all | solution.py:342
  108.0 1.7 %copy-start.6 = (bf16[16,9,32,256]{3,2,1,0:T(8,128)(2,1)S(1)}, bf16[16,9,32,256]{3,2,1,0:T(8,128)(2,1)}, u32[]{:S(2)}) copy-start(bf16[16,9,32,256]{3,2,1,0:T(8,128)(2,1)} %all-gather.3.cloned.1.call-done) | copy-start | bytes 7077892
Sparse Core Ops, SparseCore 0:
  31.0 40.4 all-gather.2

commit v4 on v3

--- a/solution.py
+++ b/solution.py
@@ -302,26 +302,28 @@
     down = [(i + 1, i) for i in range(63)]
     plane = ("y", "xh", "xl")
 
+    taps = weight.transpose(1, 2, 0, 3).reshape(TAPS, 32, C)
+    half = lax.dynamic_slice_in_dim(taps, core * HALF, HALF, axis=2)
+    beside = lax.ppermute(half, "xl", [(0, 1), (1, 0)])
+
     fx = swap_cores(f)
     gx = swap_cores(g)
     last, first = pack(f, g)
+    half, beside = after((half, beside), last, fx, gx)
+    own = lax.all_gather(jnp.stack((half, beside)), "z", axis=0, tiled=False)
     above = lax.ppermute(last, CELLS, up)
     below = lax.ppermute(first, CELLS, down)
 
     part = middle_taps(place, f, g, fx, gx)
     sent = part.astype(f16)
     got = lax.all_to_all(sent, plane, 0, 0, tiled=True)
-    near = after((above[0], below[0]), sent)
-    halo = swap_cores(jnp.stack(near))
-
-    taps = weight.transpose(1, 2, 0, 3).reshape(TAPS, 32, C)
-    half = lax.dynamic_slice_in_dim(taps, core * HALF, HALF, axis=2)
-    beside = lax.ppermute(half, "xl", [(0, 1), (1, 0)])
-    half, beside = after((half, beside), above, below, sent)
-    own = lax.all_gather(jnp.stack((half, beside)), "z", axis=0, tiled=False)
+    above, below = after((above, below), sent)
+    halo = swap_cores(jnp.stack((above[0], below[0])))
 
     part2 = outer_taps(place, f, g, above, below, fx, gx, halo)
-    got2 = lax.all_to_all(part2.astype(f16), plane, 0, 0, tiled=True)
+    (sent2,) = after((part2.astype(f16),), got)
+    got2 = lax.all_to_all(sent2, plane, 0, 0, tiled=True)
+    (own,) = after((own,), got2)
     other = swap_cores(own)
 
     extra = lax.optimization_barrier(got[:, 192:200]).astype(f32)

time: 130 us -> 131 us (level)
  blocking collectives: 0 us -> 26.9 us
  starting transfers between devices: 44 us -> 29.7 us
  waiting for transfers between devices: 29 us -> 16.3 us
  local copies, waits for them, and re-layouts: 11.6 us -> 13 us
    all_to_all x0 -> x1, blocking collectives: none -> 26.9 us  [local(): got2 = lax.all_to_all(sent2, plane, 0, 0, tiled=True)]
    all_gather x1, waiting for transfers between devices: 14.2 us -> 0.01 us  [local(): own = lax.all_gather(jnp.stack((half, beside)), 'z', axis=0, tiled=False)]
    all_to_all x1, starting transfers between devices: 9.89 us -> 3.82 us  [local(): whole = lax.all_to_all(whole, ('y', 'xh', 'core'), 0, 0, tiled=True)]
    all_to_all x1 -> x0, starting transfers between devices: 4.42 us -> none  [local(): got2 = lax.all_to_all(part2.astype(f16), plane, 0, 0, tiled=True)]
    ppermute x1, waiting for transfers between devices: 3.83 us -> 0.84 us  [local(): beside = lax.ppermute(half, 'xl', [(0, 1), (1, 0)])]
    all_to_all x1, waiting for transfers between devices: 0.46 us -> 3.11 us  [local(): lines = lax.all_to_all(line, 'z', 0, 0, tiled=True)]
    ppermute x4, starting transfers between devices: 7.9 us -> 5.48 us  [swap_cores(): return lax.ppermute(x, 'core', [(0, 1), (1, 0)])]
    all_to_all x1, waiting for transfers between devices: 5.66 us -> 7.7 us  [local(): got = lax.all_to_all(sent, plane, 0, 0, tiled=True)]
  transfers between devices with their start and end apart: 12 -> 11, of which waited for: 7 -> 5; matrix products, arithmetic and copies ran while one was open for 8% -> 8% of each run, Pallas kernels for 18% -> 17%
where the time goes in v4:
time: 131 us; the launch traced here: 130 us
  starting transfers between devices  29.7 us (23%)
  blocking collectives  26.9 us (21%)
  Pallas kernels  22.3 us (17%)
  waiting for transfers between devices  16.3 us (12%)
  between operations  14.3 us (11%)
  local copies, waits for them, and re-layouts  13 us (10%)
  other arithmetic  7.27 us (6%)
    all_to_all x1, blocking collectives, local(): got2 = lax.all_to_all(sent2, plane, 0, 0, tiled=True)  26.9 us
    pallas_call x2, Pallas kernels, convolve(): pl.pallas_call(body, out_shape=jax.ShapeDtypeStruct((C, S), bf16), in_spe...  15.8 us
    ppermute x1, starting transfers between devices, local(): below = lax.ppermute(first, CELLS, down)  7.91 us
    all_to_all x1, waiting for transfers between devices, local(): got = lax.all_to_all(sent, plane, 0, 0, tiled=True)  7.7 us
    unnamed x20, local copies, waits for them, and re-layouts  6.95 us
    all_to_all x1, starting transfers between devices, local(): got = lax.all_to_all(sent, plane, 0, 0, tiled=True)  6.51 us
    ppermute x4, starting transfers between devices, swap_cores(): return lax.ppermute(x, 'core', [(0, 1), (1, 0)])  5.48 us
    pallas_call x1, Pallas kernels, outer_taps(): pl.pallas_call(outer_kernel, out_shape=jax.ShapeDtypeStruct((16, 400, 128...  4 us
  transfers between devices with their start and end apart: 11, of which 5 were waited for; matrix products, arithmetic and copies ran while one was open for 8% of the time, Pallas kernels for 17%

profile of v4, /device:TPU:1, one launch (start us, length us, event | category | flops | bytes accessed | tf_op | source)
XLA Modules:
  0.0 129.7 jit_solution(7354516574565463496)
XLA Ops:
  7.2 0.0 all-gather.3.cloned.1.call-start
  7.2 3.3 %collective-permute-start.2 = (bf16[512,640]{1,0:T(8,128)(2,1)}, bf16[512,640]{1,0:T(8,128)(2,1)S(1)}, u32[]{:S(2)}, u32[]{:S(2)}) collective-permute-start(bf16[512,640]{1,0:T(8,128)(2,1)} %bitcast.26), channel_id=1, source_target_pairs={{0,16},{16,0},{1,17},{17,1},{2,18},{18,2},{3,19},{19,3},{4,20},{20... | collective-permute-start | bytes 1966088 | tf_op jit(solution)/shard_map/ppermute | solution.py:284
  10.6 0.1 collective-permute-start.3
  10.7 0.1 collective-permute-start.5
  10.8 1.1 copy-done.1
  11.9 1.1 copy-done.3
  13.0 0.2 pack.1
  13.1 0.7 copy-done.7
  13.9 0.7 copy-done.8
  14.6 0.8 collective-permute-done.5
  15.4 0.7 pad_maximum_fusion.1
  16.2 2.2 %collective-permute-start = (bf16[2,640,128]{2,1,0:T(8,128)(2,1)}, bf16[2,640,128]{2,1,0:T(8,128)(2,1)S(1)}, u32[]{:S(2)}, u32[]{:S(2)}) collective-permute-start(bf16[2,640,128]{2,1,0:T(8,128)(2,1)} %copy-done.8), channel_id=1, source_target_pairs={{0,1},{1,2},{2,3},{3,4},{4,5},{5,6},{6,7},{7,8},{8,9},{9,10},{10,1... | collective-permute-start | bytes 983048 | tf_op jit(solution)/shard_map/ppermute | solution.py:314
  18.4 7.9 %collective-permute-start.1 = (bf16[2,640,128]{2,1,0:T(8,128)(2,1)}, bf16[2,640,128]{2,1,0:T(8,128)(2,1)}, u32[]{:S(2)}, u32[]{:S(2)}) collective-permute-start(bf16[2,640,128]{2,1,0:T(8,128)(2,1)} %copy-done.7), channel_id=1, source_target_pairs={{1,0},{2,1},{3,2},{4,3},{5,4},{6,5},{7,6},{8,7},{9,8},{10,9},{11,1... | collective-permute-start | bytes 983048 | tf_op jit(solution)/shard_map/ppermute | solution.py:315
  26.3 0.1 pad_add_fusion.core_ref
  26.4 2.2 %middle_taps.1 = f32[16,208,128]{2,1,0:T(8,128)S(1)} custom-call(s32[2]{0:T(128)S(1)} %pad_add_fusion.core_ref, bf16[512,640]{1,0:T(8,128)(2,1)S(1)} %bitcast.28, bf16[512,640]{1,0:T(8,128)(2,1)S(1)} %bitcast.33, bf16[512,640]{1,0:T(8,128)(2,1)S(1)} %collective-permute-done.2.fx_ref, bf16[512,640]{1,0:T(8,128)(2,1)S(1)} %collective-permute-done.3.gx_ref), custom_call_target="tpu_custom_call" | custom-call | flops 1006632960 | bytes 5000000 | tf_op jit(solution)/shard_map/middle_taps/pallas_call | solution.py:159
  28.7 1.0 convert_element_type.16
  29.7 6.5 %all-to-all-start = ((f16[16,208,128]{2,1,0:T(8,128)(2,1)}), f16[16,208,128]{2,1,0:T(8,128)(2,1)}, u32[]{:S(2)}, u32[]{:S(2)}) async-start(f16[16,208,128]{2,1,0:T(8,128)(2,1)} %convert_element_type.16), calls=%async_computation | async-start | bytes 1703936 | tf_op jit(solution)/shard_map/all_to_all | solution.py:319
  36.2 0.9 slice.52
  37.2 0.1 collective-permute-start.4
  37.3 1.6 %collective-permute-done.4.halo_ref = bf16[2,640,128]{2,1,0:T(8,128)(2,1)S(1)} collective-permute-done((bf16[2,640,128]{2,1,0:T(8,128)(2,1)S(1)}, bf16[2,640,128]{2,1,0:T(8,128)(2,1)S(1)}, u32[]{:S(2)}, u32[]{:S(2)}) %collective-permute-start.4) | collective-permute-done | bytes 327712 | tf_op jit(solution)/shard_map/ppermute | solution.py:284
  38.9 4.0 %outer_taps.1 = f32[16,400,128]{2,1,0:T(8,128)S(1)} custom-call(s32[2]{0:T(128)S(1)} %pad_add_fusion.core_ref, bf16[512,640]{1,0:T(8,128)(2,1)S(1)} %bitcast.29, bf16[512,640]{1,0:T(8,128)(2,1)S(1)} %bitcast.34, bf16[2,640,128]{2,1,0:T(8,128)(2,1)S(1)} %collective-permute-done.before_ref, bf16[2,640,128]{2,1,0:T(8,128)(2,1)} %collective-permute-done.1.after_ref, ...), custom_call_target="tpu_custom_call" | custom-call | flops 2013265920 | bytes 7000000 | tf_op jit(solution)/shard_map/outer_taps/pallas_call | solution.py:206
  42.9 1.4 %convert_element_type.17 = f16[16,400,128]{2,1,0:T(8,128)(2,1)} convert(f32[16,400,128]{2,1,0:T(8,128)S(1)} %outer_taps.1) | non-fusion elementwise | flops 819200 | bytes 4915200 | tf_op jit(solution)/shard_map/convert_element_type | solution.py:324
  44.3 7.7 %all-to-all-done = f16[16,208,128]{2,1,0:T(8,128)(2,1)} async-done(((f16[16,208,128]{2,1,0:T(8,128)(2,1)}), f16[16,208,128]{2,1,0:T(8,128)(2,1)}, u32[]{:S(2)}, u32[]{:S(2)}) %all-to-all-start) | async-done | bytes 852000 | tf_op jit(solution)/shard_map/all_to_all | solution.py:319
  52.0 26.9 %all_to_all.20 = f16[16,400,128]{2,1,0:T(8,128)(2,1)} all-to-all(f16[16,400,128]{2,1,0:T(8,128)(2,1)} %convert_element_type.17), channel_id=1, replica_groups=mesh['y'=4,'xh'=2,'core'=2,'xl'=2,'z'=8] {'y','xh','xl'}, dimensions={0} | all-to-all | bytes 3276800 | tf_op jit(solution)/shard_map/all_to_all | solution.py:325
  78.9 1.9 %collective-permute-start.6 = (bf16[8,2,9,32,256]{4,3,2,1,0:T(8,128)(2,1)}, bf16[8,2,9,32,256]{4,3,2,1,0:T(8,128)(2,1)}, u32[]{:S(2)}, u32[]{:S(2)}) collective-permute-start(bf16[8,2,9,32,256]{4,3,2,1,0:T(8,128)(2,1)} %bitcast.36), channel_id=1, source_target_pairs={{0,16},{16,0},{1,17},{17,1},{2,18},{18,2},{3,19},{19,3},{4,20},{20... | collective-permute-start | bytes 7077896 | tf_op jit(solution)/shard_map/ppermute | solution.py:284
  80.8 0.8 slice.73
  81.6 0.4 fusion.8
  82.0 0.1 multiply_reduce_fusion.2
  82.1 0.1 copy.20
  82.2 1.4 %multiply_reduce_fusion.1 = f32[192,128]{1,0:T(8,128)S(1)} fusion(f16[16,208,128]{2,1,0:T(8,128)(2,1)} %all-to-all-done, f32[16]{0:T(128)S(1)} %get-tuple-element.34), kind=kLoop, calls=%fused_computation.1 | loop fusion | flops 1155072 | bytes 884800 | tf_op jit(solution)/shard_map/reduce_sum | solution.py:289
  83.6 0.8 slice.69
  84.3 0.3 fusion.7
  84.6 1.8 %multiply_reduce_fusion = f32[384,128]{1,0:T(8,128)S(1)} fusion(f16[16,400,128]{2,1,0:T(8,128)(2,1)} %all_to_all.20, f32[16]{0:T(128)S(1)} %fusion.7), kind=kLoop, calls=%fused_computation | loop fusion | flops 2310144 | bytes 1769536 | tf_op jit(solution)/shard_map/reduce_sum | solution.py:289
  86.5 0.1 broadcast_in_dim_broadcast_in_dim.2
  86.6 0.7 copy.21
  87.3 3.6 %all-to-all-start.2 = ((f32[8,10,8,128]{3,2,1,0:T(8,128)}), f32[8,10,8,128]{3,2,1,0:T(8,128)S(1)}, u32[]{:S(2)}, u32[]{:S(2)}) async-start(f32[8,10,8,128]{3,2,1,0:T(8,128)} %copy.21), calls=%async_computation.2 | async-start | bytes 655360 | tf_op jit(solution)/shard_map/all_to_all | solution.py:336
  91.0 0.1 copy.22.bias_ref
  91.1 1.7 %copy-done.5 = bf16[16,9,32,256]{3,2,1,0:T(8,128)(2,1)S(1)} copy-done((bf16[16,9,32,256]{3,2,1,0:T(8,128)(2,1)S(1)}, bf16[16,9,32,256]{3,2,1,0:T(8,128)(2,1)}, u32[]{:S(2)}) %copy-start.5) | copy-done | bytes 2359320
  92.8 7.8 %forward.1 = bf16[512,640]{1,0:T(8,128)(2,1)} custom-call(s32[2]{0:T(128)S(1)} %pad_add_fusion.core_ref, bf16[512,640]{1,0:T(8,128)(2,1)S(1)} %bitcast.30, bf16[2,640,128]{2,1,0:T(8,128)(2,1)S(1)} %collective-permute-done.before_ref, bf16[2,640,128]{2,1,0:T(8,128)(2,1)} %collective-permute-done.1.after_ref, bf16[8,2,9,32,256]{4,3,2,1,0:T(8,128)(2,1)S(1)} %bitcast.37, ...), custom_call_target="tpu_custom_call" | custom-call | flops 3019898880 | bytes 7000000 | tf_op jit(solution)/shard_map/forward/pallas_call | solution.py:267
  100.6 3.1 %all-to-all-done.2 = f32[8,10,8,128]{3,2,1,0:T(8,128)S(1)} async-done(((f32[8,10,8,128]{3,2,1,0:T(8,128)}), f32[8,10,8,128]{3,2,1,0:T(8,128)S(1)}, u32[]{:S(2)}, u32[]{:S(2)}) %all-to-all-start.2) | async-done | bytes 327712 | tf_op jit(solution)/shard_map/all_to_all | solution.py:336
  103.7 0.9 broadcast_in_dim.2
  104.6 3.8 %all-to-all-start.3 = ((f32[16,10,8,128]{3,2,1,0:T(8,128)}), f32[16,10,8,128]{3,2,1,0:T(8,128)S(1)}, u32[]{:S(2)}, u32[]{:S(2)}) async-start(f32[16,10,8,128]{3,2,1,0:T(8,128)} %broadcast_in_dim.2), calls=%async_computation.3 | async-start | bytes 1310720 | tf_op jit(solution)/shard_map/all_to_all | solution.py:344
  108.4 1.7 %copy-done.6 = bf16[16,9,32,256]{3,2,1,0:T(8,128)(2,1)S(1)} copy-done((bf16[16,9,32,256]{3,2,1,0:T(8,128)(2,1)S(1)}, bf16[16,9,32,256]{3,2,1,0:T(8,128)(2,1)}, u32[]{:S(2)}) %copy-start.6) | copy-done | bytes 2359320
  110.1 8.1 %backward.1 = bf16[512,640]{1,0:T(8,128)(2,1)} custom-call(s32[2]{0:T(128)S(1)} %pad_add_fusion.core_ref, bf16[512,640]{1,0:T(8,128)(2,1)S(1)} %bitcast.35, bf16[2,640,128]{2,1,0:T(8,128)(2,1)S(1)} %collective-permute-done.before_ref, bf16[2,640,128]{2,1,0:T(8,128)(2,1)} %collective-permute-done.1.after_ref, bf16[8,2,9,32,256]{4,3,2,1,0:T(8,128)(2,1)S(1)} %bitcast.38, ...), custom_call_target="tpu_custom_call" | custom-call | flops 3019898880 | bytes 7000000 | tf_op jit(solution)/shard_map/backward/pallas_call | solution.py:267
  118.2 3.0 %all-to-all-done.3 = f32[16,10,8,128]{3,2,1,0:T(8,128)S(1)} async-done(((f32[16,10,8,128]{3,2,1,0:T(8,128)}), f32[16,10,8,128]{3,2,1,0:T(8,128)S(1)}, u32[]{:S(2)}, u32[]{:S(2)}) %all-to-all-start.3) | async-done | bytes 655392 | tf_op jit(solution)/shard_map/all_to_all | solution.py:344
  121.2 0.1 slice_reduce_fusion
  121.3 0.9 copy.23
  122.2 0.6 reshape_squeeze.3
  (31 shorter events, 0.2 us)
Async XLA Ops:
  7.2 3.5 %copy-start = (bf16[32,3,3,512]{3,0,2,1:T(8,128)(2,1)S(1)}, bf16[32,3,3,512]{3,0,2,1:T(8,128)(2,1)}, u32[]{:S(2)}) copy-start(bf16[32,3,3,512]{3,0,2,1:T(8,128)(2,1)} %param.5) | copy-start | bytes 884740
  7.2 71.7 %all-gather.3.cloned.1.call-start = ((), (), s32[]{:S(2)}) async-start(), calls=%async_computation.4 | async-start | bytes 2654208 | tf_op jit(solution)/shard_map/all_gather | solution.py:313
  7.2 8.2 %collective-permute-start.2 = (bf16[512,640]{1,0:T(8,128)(2,1)}, bf16[512,640]{1,0:T(8,128)(2,1)S(1)}, u32[]{:S(2)}, u32[]{:S(2)}) collective-permute-start(bf16[512,640]{1,0:T(8,128)(2,1)} %bitcast.26), channel_id=1, source_target_pairs={{0,16},{16,0},{1,17},{17,1},{2,18},{18,2},{3,19},{19,3},{4,20},{20... | collective-permute-start | bytes 1966088 | tf_op jit(solution)/shard_map/ppermute | solution.py:284
  10.6 4.9 %collective-permute-start.3 = (bf16[512,640]{1,0:T(8,128)(2,1)}, bf16[512,640]{1,0:T(8,128)(2,1)S(1)}, u32[]{:S(2)}, u32[]{:S(2)}) collective-permute-start(bf16[512,640]{1,0:T(8,128)(2,1)} %bitcast.31), channel_id=1, source_target_pairs={{0,16},{16,0},{1,17},{17,1},{2,18},{18,2},{3,19},{19,3},{4,20},{20... | collective-permute-start | bytes 1966088 | tf_op jit(solution)/shard_map/ppermute | solution.py:284
  10.7 4.8 %collective-permute-start.5 = (bf16[9,32,256]{2,1,0:T(8,128)(2,1)S(1)}, bf16[9,32,256]{2,1,0:T(8,128)(2,1)S(1)}, u32[]{:S(2)}, u32[]{:S(2)}) collective-permute-start(bf16[9,32,256]{2,1,0:T(8,128)(2,1)S(1)} %constant_dynamic-slice_fusion), channel_id=1, source_target_pairs={{0,8},{8,0},{1,9},{9,1},{2,10},{10,2},{3,11},{11,3},{4,12},{12,4},... | collective-permute-start | bytes 442376 | tf_op jit(solution)/shard_map/ppermute | solution.py:307
  10.8 1.1 copy-start.1
  11.9 1.1 copy-start.3
  13.0 13.5 %copy-start.2 = (bf16[512,1,640]{2,0,1:T(8,128)(2,1)S(1)}, bf16[512,1,640]{2,0,1:T(8,128)(2,1)}, u32[]{:S(2)}) copy-start(bf16[512,1,640]{2,0,1:T(8,128)(2,1)} %param.4) | copy-start | bytes 1966084
  13.0 13.5 %copy-start.4 = (bf16[512,1,640]{2,0,1:T(8,128)(2,1)S(1)}, bf16[512,1,640]{2,0,1:T(8,128)(2,1)}, u32[]{:S(2)}) copy-start(bf16[512,1,640]{2,0,1:T(8,128)(2,1)} %param.7) | copy-start | bytes 1966084
  13.1 0.7 copy-start.7
  13.9 0.7 copy-start.8
  16.2 20.0 %collective-permute-start = (bf16[2,640,128]{2,1,0:T(8,128)(2,1)}, bf16[2,640,128]{2,1,0:T(8,128)(2,1)S(1)}, u32[]{:S(2)}, u32[]{:S(2)}) collective-permute-start(bf16[2,640,128]{2,1,0:T(8,128)(2,1)} %copy-done.8), channel_id=1, source_target_pairs={{0,1},{1,2},{2,3},{3,4},{4,5},{5,6},{6,7},{7,8},{8,9},{9,10},{10,1... | collective-permute-start | bytes 983048 | tf_op jit(solution)/shard_map/ppermute | solution.py:314
  18.4 17.8 %collective-permute-start.1 = (bf16[2,640,128]{2,1,0:T(8,128)(2,1)}, bf16[2,640,128]{2,1,0:T(8,128)(2,1)}, u32[]{:S(2)}, u32[]{:S(2)}) collective-permute-start(bf16[2,640,128]{2,1,0:T(8,128)(2,1)} %copy-done.7), channel_id=1, source_target_pairs={{1,0},{2,1},{3,2},{4,3},{5,4},{6,5},{7,6},{8,7},{9,8},{10,9},{11,1... | collective-permute-start | bytes 983048 | tf_op jit(solution)/shard_map/ppermute | solution.py:315
  29.7 22.3 %all-to-all-start = ((f16[16,208,128]{2,1,0:T(8,128)(2,1)}), f16[16,208,128]{2,1,0:T(8,128)(2,1)}, u32[]{:S(2)}, u32[]{:S(2)}) async-start(f16[16,208,128]{2,1,0:T(8,128)(2,1)} %convert_element_type.16), calls=%async_computation | async-start | bytes 1703936 | tf_op jit(solution)/shard_map/all_to_all | solution.py:319
  37.2 1.7 %collective-permute-start.4 = (bf16[2,640,128]{2,1,0:T(8,128)(2,1)S(1)}, bf16[2,640,128]{2,1,0:T(8,128)(2,1)S(1)}, u32[]{:S(2)}, u32[]{:S(2)}) collective-permute-start(bf16[2,640,128]{2,1,0:T(8,128)(2,1)S(1)} %pad_maximum_fusion), channel_id=1, source_target_pairs={{0,16},{16,0},{1,17},{17,1},{2,18},{18,2},{3,19},{19,3},{4,20},{20... | collective-permute-start | bytes 983048 | tf_op jit(solution)/shard_map/ppermute | solution.py:284
  78.9 12.2 %collective-permute-start.6 = (bf16[8,2,9,32,256]{4,3,2,1,0:T(8,128)(2,1)}, bf16[8,2,9,32,256]{4,3,2,1,0:T(8,128)(2,1)}, u32[]{:S(2)}, u32[]{:S(2)}) collective-permute-start(bf16[8,2,9,32,256]{4,3,2,1,0:T(8,128)(2,1)} %bitcast.36), channel_id=1, source_target_pairs={{0,16},{16,0},{1,17},{17,1},{2,18},{18,2},{3,19},{19,3},{4,20},{20... | collective-permute-start | bytes 7077896 | tf_op jit(solution)/shard_map/ppermute | solution.py:284
  84.6 6.3 %copy-start.9 = (f32[512]{0:T(512)S(1)}, f32[512]{0:T(512)}, u32[]{:S(2)}) copy-start(f32[512]{0:T(512)} %param.6) | copy-start | bytes 6148
  87.3 16.3 %all-to-all-start.2 = ((f32[8,10,8,128]{3,2,1,0:T(8,128)}), f32[8,10,8,128]{3,2,1,0:T(8,128)S(1)}, u32[]{:S(2)}, u32[]{:S(2)}) async-start(f32[8,10,8,128]{3,2,1,0:T(8,128)} %copy.21), calls=%async_computation.2 | async-start | bytes 655360 | tf_op jit(solution)/shard_map/all_to_all | solution.py:336
  91.1 1.7 %copy-start.5 = (bf16[16,9,32,256]{3,2,1,0:T(8,128)(2,1)S(1)}, bf16[16,9,32,256]{3,2,1,0:T(8,128)(2,1)}, u32[]{:S(2)}) copy-start(bf16[16,9,32,256]{3,2,1,0:T(8,128)(2,1)} %all-gather.3.cloned.1.call-done) | copy-start | bytes 7077892
  104.6 16.6 %all-to-all-start.3 = ((f32[16,10,8,128]{3,2,1,0:T(8,128)}), f32[16,10,8,128]{3,2,1,0:T(8,128)S(1)}, u32[]{:S(2)}, u32[]{:S(2)}) async-start(f32[16,10,8,128]{3,2,1,0:T(8,128)} %broadcast_in_dim.2), calls=%async_computation.3 | async-start | bytes 1310720 | tf_op jit(solution)/shard_map/all_to_all | solution.py:344
  108.4 1.7 %copy-start.6 = (bf16[16,9,32,256]{3,2,1,0:T(8,128)(2,1)S(1)}, bf16[16,9,32,256]{3,2,1,0:T(8,128)(2,1)}, u32[]{:S(2)}) copy-start(bf16[16,9,32,256]{3,2,1,0:T(8,128)(2,1)} %all-gather.3.cloned.1.call-done) | copy-start | bytes 7077892
Sparse Core Ops, SparseCore 0:
  16.3 41.4 all-gather.2

commit v5 on v4

--- a/solution.py
+++ b/solution.py
@@ -219,18 +219,20 @@
     )(core, f, g, before, after, fx, gx, halo)
 
 
-def load_kernel(place_ref, own_ref, other_ref, kern):
+def load_kernel(place_ref, own_ref, other_refs, kern):
     core, low = place_ref[0], place_ref[1]
-    for half, ref in ((core, own_ref), (1 - core, other_ref)):
+    for half, refs in ((core, (own_ref,)), (1 - core, other_refs)):
+        size = HALF // len(refs)
         for t in range(TAPS):
             lanes = pl.ds(pl.multiple_of(t * C + half * HALF, HALF), HALF)
             for k in range(2):
-                first = pl.multiple_of(HALF * (low if k == 0 else 1 - low), HALF)
-                kern[pl.ds(first, HALF), lanes] = ref[:, k, t].reshape(HALF, HALF)
-
-
-def forward_kernel(core_ref, f_ref, before_ref, after_ref, own_ref, other_ref, bias_ref, out_ref, ext, win, kern):
-    load_kernel(core_ref, own_ref, other_ref, kern)
+                for j, ref in enumerate(refs):
+                    first = HALF * (low if k == 0 else 1 - low) + j * size
+                    kern[pl.ds(pl.multiple_of(first, size), size), lanes] = ref[:, k, t].reshape(size, HALF)
+
+
+def forward_kernel(core_ref, f_ref, before_ref, after_ref, own_ref, o0_ref, o1_ref, o2_ref, o3_ref, bias_ref, out_ref, ext, win, kern):
+    load_kernel(core_ref, own_ref, (o0_ref, o1_ref, o2_ref, o3_ref), kern)
     masks = column_masks(C)
     fill(ext, C, f_ref[...], (before_ref[0, :C, :], before_ref[0, C:, :]), (after_ref[0, :C, :], after_ref[0, C:, :]), GROUPS)
     for a in range(3):
@@ -243,8 +245,8 @@
         out_ref[rows, :] = (total + bias_ref[rows, :]).astype(bf16)
 
 
-def backward_kernel(core_ref, g_ref, before_ref, after_ref, own_ref, other_ref, grad_ref, ext, win, kern):
-    load_kernel(core_ref, own_ref, other_ref, kern)
+def backward_kernel(core_ref, g_ref, before_ref, after_ref, own_ref, o0_ref, o1_ref, o2_ref, o3_ref, grad_ref, ext, win, kern):
+    load_kernel(core_ref, own_ref, (o0_ref, o1_ref, o2_ref, o3_ref), kern)
     masks = column_masks(C)
     fill(ext, C, g_ref[...], (before_ref[1, :C, :], before_ref[1, C:, :]), (after_ref[1, :C, :], after_ref[1, C:, :]), GROUPS)
     for a in range(3):
@@ -275,7 +277,7 @@
             pltpu.VMEM((C, TAPS * C), bf16),
         ],
         compiler_params=params(32),
-        cost_estimate=pl.CostEstimate(flops=2 * TAPS * C * C * S, bytes_accessed=7_000_000, transcendentals=0),
+        cost_estimate=pl.CostEstimate(flops=1_000_000, bytes_accessed=1_000_000, transcendentals=0),
         name=name,
     )(*args)
 
@@ -323,8 +325,10 @@
     part2 = outer_taps(place, f, g, above, below, fx, gx, halo)
     (sent2,) = after((part2.astype(f16),), got)
     got2 = lax.all_to_all(sent2, plane, 0, 0, tiled=True)
-    (own,) = after((own,), got2)
-    other = swap_cores(own)
+    (own,) = after((own,), got)
+    other = tuple(swap_cores(own[2 * k:2 * k + 2]) for k in range(4))
+    outputs = convolve(forward_kernel, "forward", place, f, above, below, own, *other, bias.reshape(C, 1))
+    got2, outputs = lax.optimization_barrier((got2, outputs))
 
     extra = lax.optimization_barrier(got[:, 192:200]).astype(f32)
     extra2 = lax.optimization_barrier(got2[:, 384:392]).astype(f32)
@@ -334,15 +338,12 @@
     ends = jnp.broadcast_to(ends[:, :8].T[:, :, None], (8, 8, 128))[None]
     line = jnp.concatenate((outer[:3], middle, outer[3:], ends), axis=0).transpose(1, 0, 2, 3)
     lines = lax.all_to_all(line, "z", 0, 0, tiled=True)
-    (f,) = after((f,), line)
-    outputs = convolve(forward_kernel, "forward", place, f, above, below, own, other, bias.reshape(C, 1))
-    lines, outputs = lax.optimization_barrier((lines, outputs))
     scale = 1.0 / math.sqrt(4 * 256 * 160)
     done = jnp.sum(lines, axis=0) * scale
     whole = jnp.broadcast_to(done, (16, 10, 8, 128))
     whole, g = lax.optimization_barrier((whole, g))
     whole = lax.all_to_all(whole, ("y", "xh", "core"), 0, 0, tiled=True)
-    grad_frames = convolve(backward_kernel, "backward", place, g, above, below, own, other)
+    grad_frames = convolve(backward_kernel, "backward", place, g, above, below, own, *other)
     whole, grad_frames = lax.optimization_barrier((whole, grad_frames))
     whole = whole.reshape(4, 2, 2, 10, 8, 128)
     grad_weight = whole[:, :, :, :9].reshape(4, 2, 2, 3, 3, 8, 128)

time: 131 us -> 134 us (1.023)
  blocking collectives: 26.9 us -> 13.8 us
  local copies, waits for them, and re-layouts: 13 us -> 20.9 us
  starting transfers between devices: 29.7 us -> 35.4 us
  waiting for transfers between devices: 16.3 us -> 18.9 us
    all_to_all x1, blocking collectives: 26.9 us -> 13.8 us  [local(): lines = lax.all_to_all(line, 'z', 0, 0, tiled=True)]
    all_to_all x1, starting transfers between devices: 3.82 us -> 8.55 us  [local(): whole = lax.all_to_all(whole, ('y', 'xh', 'core'), 0, 0, tiled=True)]
    unnamed x20 -> x38, local copies, waits for them, and re-layouts: 6.95 us -> 10.8 us
    slice x0 -> x1, local copies, waits for them, and re-layouts: none -> 3.2 us  [local(): other = tuple((swap_cores(own[2 * k:2 * k + 2]) for k in range(4)))]
    ppermute x4 -> x7, waiting for transfers between devices: 1.6 us -> 3.63 us  [swap_cores(): return lax.ppermute(x, 'core', [(0, 1), (1, 0)])]
    ppermute x4 -> x7, starting transfers between devices: 5.48 us -> 5.66 us  [swap_cores(): return lax.ppermute(x, 'core', [(0, 1), (1, 0)])]
  transfers between devices with their start and end apart: 11 -> 14, of which waited for: 5 -> 8; matrix products, arithmetic and copies ran while one was open for 8% -> 7% of each run, Pallas kernels for 17% -> 16%
where the time goes in v5:
time: 134 us; the launch traced here: 133 us
  starting transfers between devices  35.4 us (26%)
  Pallas kernels  21.5 us (16%)
  local copies, waits for them, and re-layouts  20.9 us (16%)
  waiting for transfers between devices  18.9 us (14%)
  between operations  14.3 us (11%)
  blocking collectives  13.8 us (10%)
  other arithmetic  8.25 us (6%)
    pallas_call x2, Pallas kernels, convolve(): pl.pallas_call(body, out_shape=jax.ShapeDtypeStruct((C, S), bf16), in_spe...  15.5 us
    all_to_all x1, blocking collectives, local(): lines = lax.all_to_all(line, 'z', 0, 0, tiled=True)  13.8 us
    unnamed x38, local copies, waits for them, and re-layouts  10.8 us
    all_to_all x1, starting transfers between devices, local(): whole = lax.all_to_all(whole, ('y', 'xh', 'core'), 0, 0, tiled=True)  8.55 us
    ppermute x1, starting transfers between devices, local(): below = lax.ppermute(first, CELLS, down)  8.2 us
    all_to_all x1, waiting for transfers between devices, local(): got = lax.all_to_all(sent, plane, 0, 0, tiled=True)  7.89 us
    all_to_all x1, starting transfers between devices, local(): got = lax.all_to_all(sent, plane, 0, 0, tiled=True)  6.51 us
    ppermute x7, starting transfers between devices, swap_cores(): return lax.ppermute(x, 'core', [(0, 1), (1, 0)])  5.66 us
  transfers between devices with their start and end apart: 14, of which 8 were waited for; matrix products, arithmetic and copies ran while one was open for 7% of the time, Pallas kernels for 16%

profile of v5, /device:TPU:1, one launch (start us, length us, event | category | flops | bytes accessed | tf_op | source)
XLA Modules:
  0.0 133.1 jit_solution(15273381673105162344)
XLA Ops:
  7.2 3.3 %collective-permute-start.2 = (bf16[512,640]{1,0:T(8,128)(2,1)}, bf16[512,640]{1,0:T(8,128)(2,1)S(1)}, u32[]{:S(2)}, u32[]{:S(2)}) collective-permute-start(bf16[512,640]{1,0:T(8,128)(2,1)} %bitcast.29), channel_id=1, source_target_pairs={{0,16},{16,0},{1,17},{17,1},{2,18},{18,2},{3,19},{19,3},{4,20},{20... | collective-permute-start | bytes 1966088 | tf_op jit(solution)/shard_map/ppermute | solution.py:286
  10.8 1.1 copy-done.2
  11.9 1.1 copy-done.4
  13.1 0.7 copy-done.17
  13.9 1.6 %collective-permute-done.5 = bf16[9,32,256]{2,1,0:T(8,128)(2,1)S(1)} collective-permute-done((bf16[9,32,256]{2,1,0:T(8,128)(2,1)S(1)}, bf16[9,32,256]{2,1,0:T(8,128)(2,1)S(1)}, u32[]{:S(2)}, u32[]{:S(2)}) %collective-permute-start.5) | collective-permute-done | bytes 147488 | tf_op jit(solution)/shard_map/ppermute | solution.py:309
  15.4 0.8 copy-done.14
  16.3 0.7 pad_maximum_fusion.1
  17.0 1.9 %collective-permute-start = (bf16[2,640,128]{2,1,0:T(8,128)(2,1)}, bf16[2,640,128]{2,1,0:T(8,128)(2,1)S(1)}, u32[]{:S(2)}, u32[]{:S(2)}) collective-permute-start(bf16[2,640,128]{2,1,0:T(8,128)(2,1)} %copy-done.17), channel_id=1, source_target_pairs={{0,1},{1,2},{2,3},{3,4},{4,5},{5,6},{6,7},{7,8},{8,9},{9,10},{10,1... | collective-permute-start | bytes 983048 | tf_op jit(solution)/shard_map/ppermute | solution.py:316
  19.0 8.2 %collective-permute-start.1 = (bf16[2,640,128]{2,1,0:T(8,128)(2,1)S(1)}, bf16[2,640,128]{2,1,0:T(8,128)(2,1)S(1)}, u32[]{:S(2)}, u32[]{:S(2)}) collective-permute-start(bf16[2,640,128]{2,1,0:T(8,128)(2,1)S(1)} %get-tuple-element.19), channel_id=1, source_target_pairs={{1,0},{2,1},{3,2},{4,3},{5,4},{6,5},{7,6},{8,7},{9,8},{10,9},{11,1... | collective-permute-start | bytes 983048 | tf_op jit(solution)/shard_map/ppermute | solution.py:317
  27.3 1.1 copy-done.15
  28.3 2.2 %middle_taps.1 = f32[16,208,128]{2,1,0:T(8,128)S(1)} custom-call(s32[2]{0:T(128)S(1)} %pad_add_fusion.core_ref, bf16[512,640]{1,0:T(8,128)(2,1)S(1)} %bitcast.31, bf16[512,640]{1,0:T(8,128)(2,1)S(1)} %bitcast.36, bf16[512,640]{1,0:T(8,128)(2,1)S(1)} %collective-permute-done.2.fx_ref, bf16[512,640]{1,0:T(8,128)(2,1)S(1)} %copy-done.15), custom_call_target="tpu_custom_call" | custom-call | flops 1006632960 | bytes 5000000 | tf_op jit(solution)/shard_map/middle_taps/pallas_call | solution.py:159
  30.6 1.0 convert_element_type.16
  31.6 6.5 %all-to-all-start = ((f16[16,208,128]{2,1,0:T(8,128)(2,1)}), f16[16,208,128]{2,1,0:T(8,128)(2,1)}, u32[]{:S(2)}, u32[]{:S(2)}) async-start(f16[16,208,128]{2,1,0:T(8,128)(2,1)} %convert_element_type.16), calls=%async_computation | async-start | bytes 1703936 | tf_op jit(solution)/shard_map/all_to_all | solution.py:321
  38.4 1.6 %collective-permute-done.4.halo_ref = bf16[2,640,128]{2,1,0:T(8,128)(2,1)S(1)} collective-permute-done((bf16[2,640,128]{2,1,0:T(8,128)(2,1)S(1)}, bf16[2,640,128]{2,1,0:T(8,128)(2,1)S(1)}, u32[]{:S(2)}, u32[]{:S(2)}) %collective-permute-start.4) | collective-permute-done | bytes 327712 | tf_op jit(solution)/shard_map/ppermute | solution.py:286
  40.0 1.1 copy-done.16
  41.1 3.6 %outer_taps.1 = f32[16,400,128]{2,1,0:T(8,128)S(1)} custom-call(s32[2]{0:T(128)S(1)} %pad_add_fusion.core_ref, bf16[512,640]{1,0:T(8,128)(2,1)S(1)} %bitcast.32, bf16[512,640]{1,0:T(8,128)(2,1)S(1)} %bitcast.37, bf16[2,640,128]{2,1,0:T(8,128)(2,1)S(1)} %collective-permute-done.before_ref, bf16[2,640,128]{2,1,0:T(8,128)(2,1)S(1)} %collective-permute-done.1.after_ref, ...), custom_call_target="tpu_custom_call" | custom-call | flops 2013265920 | bytes 7000000 | tf_op jit(solution)/shard_map/outer_taps/pallas_call | solution.py:206
  44.7 1.4 %convert_element_type.17 = f16[16,400,128]{2,1,0:T(8,128)(2,1)} convert(f32[16,400,128]{2,1,0:T(8,128)S(1)} %outer_taps.1) | non-fusion elementwise | flops 819200 | bytes 4915200 | tf_op jit(solution)/shard_map/convert_element_type | solution.py:326
  46.0 7.9 %all-to-all-done = f16[16,208,128]{2,1,0:T(8,128)(2,1)} async-done(((f16[16,208,128]{2,1,0:T(8,128)(2,1)}), f16[16,208,128]{2,1,0:T(8,128)(2,1)}, u32[]{:S(2)}, u32[]{:S(2)}) %all-to-all-start) | async-done | bytes 852000 | tf_op jit(solution)/shard_map/all_to_all | solution.py:321
  53.9 4.4 %all-to-all-start.1 = ((f16[16,400,128]{2,1,0:T(8,128)(2,1)}), f16[16,400,128]{2,1,0:T(8,128)(2,1)}, u32[]{:S(2)}, u32[]{:S(2)}) async-start(f16[16,400,128]{2,1,0:T(8,128)(2,1)} %convert_element_type.17), calls=%async_computation.1 | async-start | bytes 3276800 | tf_op jit(solution)/shard_map/all_to_all | solution.py:327
  58.3 0.9 copy.20.bias_ref
  59.2 0.8 slice.87
  60.1 3.2 %fusion.10 = (bf16[2,2,9,32,256]{4,3,2,1,0:T(8,128)(2,1)}, bf16[2,2,9,32,256]{4,3,2,1,0:T(8,128)(2,1)}, bf16[2,2,9,32,256]{4,3,2,1,0:T(8,128)(2,1)}, bf16[2,2,9,32,256]{4,3,2,1,0:T(8,128)(2,1)}) fusion(bf16[8,2,9,32,256]{4,3,2,1,0:T(8,128)(2,1)} %bitcast.26), kind=kLoop, calls=%fused_computation.24 | loop fusion | bytes 4718592 | tf_op jit(solution)/shard_map/slice | solution.py:329
  63.3 1.6 %collective-permute-start.6 = (bf16[2,2,9,32,256]{4,3,2,1,0:T(8,128)(2,1)}, bf16[2,2,9,32,256]{4,3,2,1,0:T(8,128)(2,1)}, u32[]{:S(2)}, u32[]{:S(2)}) collective-permute-start(bf16[2,2,9,32,256]{4,3,2,1,0:T(8,128)(2,1)} %get-tuple-element.37), channel_id=1, source_target_pairs={{0,16},{16,0},{1,17},{17,1},{2,18},{18,2},{3,19},{19,3},{4,20},{20... | collective-permute-start | bytes 1769480 | tf_op jit(solution)/shard_map/ppermute | solution.py:286
  64.9 0.5 collective-permute-start.8
  65.4 0.4 fusion.8
  65.9 1.4 %multiply_reduce_fusion.1 = f32[192,128]{1,0:T(8,128)S(1)} fusion(f16[16,208,128]{2,1,0:T(8,128)(2,1)} %all-to-all-done, f32[16]{0:T(128)S(1)} %get-tuple-element.32), kind=kLoop, calls=%fused_computation.1 | loop fusion | flops 1155072 | bytes 884800 | tf_op jit(solution)/shard_map/reduce_sum | solution.py:291
  67.3 0.3 collective-permute-done.7.o1_ref
  67.7 0.8 collective-permute-done.8.o2_ref
  68.5 0.8 collective-permute-done.9.o3_ref
  69.4 1.0 copy-done.8
  70.3 1.0 copy-done.11
  71.3 0.9 copy-done.13
  72.3 7.6 %forward.1 = bf16[512,640]{1,0:T(8,128)(2,1)} custom-call(s32[2]{0:T(128)S(1)} %pad_add_fusion.core_ref, bf16[512,640]{1,0:T(8,128)(2,1)S(1)} %bitcast.33, bf16[2,640,128]{2,1,0:T(8,128)(2,1)S(1)} %copy-done.8, bf16[2,640,128]{2,1,0:T(8,128)(2,1)S(1)} %copy-done.11, bf16[8,2,9,32,256]{4,3,2,1,0:T(8,128)(2,1)S(1)} %bitcast.27, ...), custom_call_target="tpu_custom_call" | custom-call | flops 1000000 | bytes 1000000 | tf_op jit(solution)/shard_map/forward/pallas_call | solution.py:269
  79.8 2.9 %all-to-all-done.1 = f16[16,400,128]{2,1,0:T(8,128)(2,1)} async-done(((f16[16,400,128]{2,1,0:T(8,128)(2,1)}), f16[16,400,128]{2,1,0:T(8,128)(2,1)}, u32[]{:S(2)}, u32[]{:S(2)}) %all-to-all-start.1) | async-done | bytes 1638432 | tf_op jit(solution)/shard_map/all_to_all | solution.py:327
  82.7 0.8 slice.70
  83.7 1.8 %multiply_reduce_fusion = f32[384,128]{1,0:T(8,128)S(1)} fusion(f32[16]{0:T(128)S(1)} %fusion.7, f16[16,400,128]{2,1,0:T(8,128)(2,1)} %all-to-all-done.1), kind=kLoop, calls=%fused_computation | loop fusion | flops 2310144 | bytes 1769536 | tf_op jit(solution)/shard_map/reduce_sum | solution.py:291
  85.7 13.8 %all_to_all.20 = f32[8,10,8,128]{3,2,1,0:T(8,128)} all-to-all(f32[8,10,8,128]{3,2,1,0:T(8,128)S(1)} %copy.22), channel_id=1, replica_groups=mesh['y'=4,'xh'=2,'core'=2,'xl'=2,'z'=8] {'z'}, dimensions={0} | all-to-all | bytes 655360 | tf_op jit(solution)/shard_map/all_to_all | solution.py:340
  99.6 1.0 reduce_sum.39
  100.6 0.9 broadcast_in_dim.2
  101.5 8.5 %all-to-all-start.3 = ((f32[16,10,8,128]{3,2,1,0:T(8,128)}), f32[16,10,8,128]{3,2,1,0:T(8,128)}, u32[]{:S(2)}, u32[]{:S(2)}) async-start(f32[16,10,8,128]{3,2,1,0:T(8,128)} %broadcast_in_dim.2), calls=%async_computation.3 | async-start | bytes 1310720 | tf_op jit(solution)/shard_map/all_to_all | solution.py:345
  110.1 1.0 copy-done.9
  111.0 1.0 copy-done.12
  112.0 7.9 %backward.1 = bf16[512,640]{1,0:T(8,128)(2,1)} custom-call(s32[2]{0:T(128)S(1)} %pad_add_fusion.core_ref, bf16[512,640]{1,0:T(8,128)(2,1)S(1)} %bitcast.38, bf16[2,640,128]{2,1,0:T(8,128)(2,1)S(1)} %copy-done.9, bf16[2,640,128]{2,1,0:T(8,128)(2,1)S(1)} %copy-done.12, bf16[8,2,9,32,256]{4,3,2,1,0:T(8,128)(2,1)S(1)} %bitcast.28, ...), custom_call_target="tpu_custom_call" | custom-call | flops 1000000 | bytes 1000000 | tf_op jit(solution)/shard_map/backward/pallas_call | solution.py:269
  119.9 2.9 %all-to-all-done.3 = f32[16,10,8,128]{3,2,1,0:T(8,128)} async-done(((f32[16,10,8,128]{3,2,1,0:T(8,128)}), f32[16,10,8,128]{3,2,1,0:T(8,128)}, u32[]{:S(2)}, u32[]{:S(2)}) %all-to-all-start.3) | async-done | bytes 655392 | tf_op jit(solution)/shard_map/all_to_all | solution.py:345
  122.8 1.1 slice.91
  124.0 0.8 slice_reduce_fusion
  124.8 0.9 copy.23
  125.7 0.6 reshape_squeeze.3
  (56 shorter events, 1.4 us)
Async XLA Ops:
  7.2 3.5 %copy-start = (bf16[32,3,3,512]{3,0,2,1:T(8,128)(2,1)S(1)}, bf16[32,3,3,512]{3,0,2,1:T(8,128)(2,1)}, u32[]{:S(2)}) copy-start(bf16[32,3,3,512]{3,0,2,1:T(8,128)(2,1)} %param.5) | copy-start | bytes 884740
  7.2 52.9 %all-gather.3.cloned.1.call-start = ((), (), s32[]{:S(2)}) async-start(), calls=%async_computation.4 | async-start | bytes 2654208 | tf_op jit(solution)/shard_map/all_gather | solution.py:315
  7.2 8.2 %collective-permute-start.2 = (bf16[512,640]{1,0:T(8,128)(2,1)}, bf16[512,640]{1,0:T(8,128)(2,1)S(1)}, u32[]{:S(2)}, u32[]{:S(2)}) collective-permute-start(bf16[512,640]{1,0:T(8,128)(2,1)} %bitcast.29), channel_id=1, source_target_pairs={{0,16},{16,0},{1,17},{17,1},{2,18},{18,2},{3,19},{19,3},{4,20},{20... | collective-permute-start | bytes 1966088 | tf_op jit(solution)/shard_map/ppermute | solution.py:286
  10.6 4.9 %collective-permute-start.3 = (bf16[512,640]{1,0:T(8,128)(2,1)}, bf16[512,640]{1,0:T(8,128)(2,1)S(1)}, u32[]{:S(2)}, u32[]{:S(2)}) collective-permute-start(bf16[512,640]{1,0:T(8,128)(2,1)} %bitcast.34), channel_id=1, source_target_pairs={{0,16},{16,0},{1,17},{17,1},{2,18},{18,2},{3,19},{19,3},{4,20},{20... | collective-permute-start | bytes 1966088 | tf_op jit(solution)/shard_map/ppermute | solution.py:286
  10.7 4.8 %collective-permute-start.5 = (bf16[9,32,256]{2,1,0:T(8,128)(2,1)S(1)}, bf16[9,32,256]{2,1,0:T(8,128)(2,1)S(1)}, u32[]{:S(2)}, u32[]{:S(2)}) collective-permute-start(bf16[9,32,256]{2,1,0:T(8,128)(2,1)S(1)} %constant_dynamic-slice_fusion), channel_id=1, source_target_pairs={{0,8},{8,0},{1,9},{9,1},{2,10},{10,2},{3,11},{11,3},{4,12},{12,4},... | collective-permute-start | bytes 442376 | tf_op jit(solution)/shard_map/ppermute | solution.py:309
  10.8 1.1 copy-start.2
  11.9 1.1 copy-start.4
  13.0 14.3 %copy-start.3 = (bf16[512,1,640]{2,0,1:T(8,128)(2,1)S(1)}, bf16[512,1,640]{2,0,1:T(8,128)(2,1)}, u32[]{:S(2)}) copy-start(bf16[512,1,640]{2,0,1:T(8,128)(2,1)} %param.4) | copy-start | bytes 1966084
  13.0 14.3 %copy-start.5 = (bf16[512,1,640]{2,0,1:T(8,128)(2,1)S(1)}, bf16[512,1,640]{2,0,1:T(8,128)(2,1)}, u32[]{:S(2)}) copy-start(bf16[512,1,640]{2,0,1:T(8,128)(2,1)} %param.7) | copy-start | bytes 1966084
  13.1 0.7 copy-start.17
  15.4 0.8 copy-start.14
  17.0 21.1 %collective-permute-start = (bf16[2,640,128]{2,1,0:T(8,128)(2,1)}, bf16[2,640,128]{2,1,0:T(8,128)(2,1)S(1)}, u32[]{:S(2)}, u32[]{:S(2)}) collective-permute-start(bf16[2,640,128]{2,1,0:T(8,128)(2,1)} %copy-done.17), channel_id=1, source_target_pairs={{0,1},{1,2},{2,3},{3,4},{4,5},{5,6},{6,7},{7,8},{8,9},{9,10},{10,1... | collective-permute-start | bytes 983048 | tf_op jit(solution)/shard_map/ppermute | solution.py:316
  19.0 19.2 %collective-permute-start.1 = (bf16[2,640,128]{2,1,0:T(8,128)(2,1)S(1)}, bf16[2,640,128]{2,1,0:T(8,128)(2,1)S(1)}, u32[]{:S(2)}, u32[]{:S(2)}) collective-permute-start(bf16[2,640,128]{2,1,0:T(8,128)(2,1)S(1)} %get-tuple-element.19), channel_id=1, source_target_pairs={{1,0},{2,1},{3,2},{4,3},{5,4},{6,5},{7,6},{8,7},{9,8},{10,9},{11,1... | collective-permute-start | bytes 983048 | tf_op jit(solution)/shard_map/ppermute | solution.py:317
  27.3 1.1 copy-start.15
  31.6 22.3 %all-to-all-start = ((f16[16,208,128]{2,1,0:T(8,128)(2,1)}), f16[16,208,128]{2,1,0:T(8,128)(2,1)}, u32[]{:S(2)}, u32[]{:S(2)}) async-start(f16[16,208,128]{2,1,0:T(8,128)(2,1)} %convert_element_type.16), calls=%async_computation | async-start | bytes 1703936 | tf_op jit(solution)/shard_map/all_to_all | solution.py:321
  38.1 6.5 %copy-start.7 = (bf16[2,640,128]{2,1,0:T(8,128)(2,1)}, bf16[2,640,128]{2,1,0:T(8,128)(2,1)S(1)}, u32[]{:S(2)}) copy-start(bf16[2,640,128]{2,1,0:T(8,128)(2,1)S(1)} %collective-permute-done.before_ref) | copy-start | bytes 983044
  38.2 6.5 %copy-start.10 = (bf16[2,640,128]{2,1,0:T(8,128)(2,1)}, bf16[2,640,128]{2,1,0:T(8,128)(2,1)S(1)}, u32[]{:S(2)}) copy-start(bf16[2,640,128]{2,1,0:T(8,128)(2,1)S(1)} %collective-permute-done.1.after_ref) | copy-start | bytes 983044
  38.2 1.7 %collective-permute-start.4 = (bf16[2,640,128]{2,1,0:T(8,128)(2,1)S(1)}, bf16[2,640,128]{2,1,0:T(8,128)(2,1)S(1)}, u32[]{:S(2)}, u32[]{:S(2)}) collective-permute-start(bf16[2,640,128]{2,1,0:T(8,128)(2,1)S(1)} %pad_maximum_fusion), channel_id=1, source_target_pairs={{0,16},{16,0},{1,17},{17,1},{2,18},{18,2},{3,19},{19,3},{4,20},{20... | collective-permute-start | bytes 983048 | tf_op jit(solution)/shard_map/ppermute | solution.py:286
  40.0 1.1 copy-start.16
  46.0 12.3 %copy-start.18 = (f32[512]{0:T(512)S(1)}, f32[512]{0:T(512)}, u32[]{:S(2)}) copy-start(f32[512]{0:T(512)} %param.6) | copy-start | bytes 6148
  53.9 28.7 %all-to-all-start.1 = ((f16[16,400,128]{2,1,0:T(8,128)(2,1)}), f16[16,400,128]{2,1,0:T(8,128)(2,1)}, u32[]{:S(2)}, u32[]{:S(2)}) async-start(f16[16,400,128]{2,1,0:T(8,128)(2,1)} %convert_element_type.17), calls=%async_computation.1 | async-start | bytes 3276800 | tf_op jit(solution)/shard_map/all_to_all | solution.py:327
  60.0 9.3 %copy-start.1 = (bf16[16,9,32,256]{3,2,1,0:T(8,128)(2,1)S(1)}, bf16[16,9,32,256]{3,2,1,0:T(8,128)(2,1)}, u32[]{:S(2)}) copy-start(bf16[16,9,32,256]{3,2,1,0:T(8,128)(2,1)} %all-gather.3.cloned.1.call-done) | copy-start | bytes 7077892
  63.3 4.1 %collective-permute-start.6 = (bf16[2,2,9,32,256]{4,3,2,1,0:T(8,128)(2,1)}, bf16[2,2,9,32,256]{4,3,2,1,0:T(8,128)(2,1)}, u32[]{:S(2)}, u32[]{:S(2)}) collective-permute-start(bf16[2,2,9,32,256]{4,3,2,1,0:T(8,128)(2,1)} %get-tuple-element.37), channel_id=1, source_target_pairs={{0,16},{16,0},{1,17},{17,1},{2,18},{18,2},{3,19},{19,3},{4,20},{20... | collective-permute-start | bytes 1769480 | tf_op jit(solution)/shard_map/ppermute | solution.py:286
  64.8 2.8 %collective-permute-start.7 = (bf16[2,2,9,32,256]{4,3,2,1,0:T(8,128)(2,1)}, bf16[2,2,9,32,256]{4,3,2,1,0:T(8,128)(2,1)}, u32[]{:S(2)}, u32[]{:S(2)}) collective-permute-start(bf16[2,2,9,32,256]{4,3,2,1,0:T(8,128)(2,1)} %get-tuple-element.36), channel_id=1, source_target_pairs={{0,16},{16,0},{1,17},{17,1},{2,18},{18,2},{3,19},{19,3},{4,20},{20... | collective-permute-start | bytes 1769480 | tf_op jit(solution)/shard_map/ppermute | solution.py:286
  64.9 3.7 %collective-permute-start.8 = (bf16[2,2,9,32,256]{4,3,2,1,0:T(8,128)(2,1)}, bf16[2,2,9,32,256]{4,3,2,1,0:T(8,128)(2,1)}, u32[]{:S(2)}, u32[]{:S(2)}) collective-permute-start(bf16[2,2,9,32,256]{4,3,2,1,0:T(8,128)(2,1)} %get-tuple-element.35), channel_id=1, source_target_pairs={{0,16},{16,0},{1,17},{17,1},{2,18},{18,2},{3,19},{19,3},{4,20},{20... | collective-permute-start | bytes 1769480 | tf_op jit(solution)/shard_map/ppermute | solution.py:286
  65.4 4.0 %collective-permute-start.9 = (bf16[2,2,9,32,256]{4,3,2,1,0:T(8,128)(2,1)}, bf16[2,2,9,32,256]{4,3,2,1,0:T(8,128)(2,1)}, u32[]{:S(2)}, u32[]{:S(2)}) collective-permute-start(bf16[2,2,9,32,256]{4,3,2,1,0:T(8,128)(2,1)} %get-tuple-element.34), channel_id=1, source_target_pairs={{0,16},{16,0},{1,17},{17,1},{2,18},{18,2},{3,19},{19,3},{4,20},{20... | collective-permute-start | bytes 1769480 | tf_op jit(solution)/shard_map/ppermute | solution.py:286
  69.4 1.0 copy-start.8
  70.3 1.0 copy-start.11
  71.3 0.9 copy-start.13
  85.7 24.3 %copy-start.6 = (bf16[512,1,640]{2,0,1:T(8,128)(2,1)S(1)}, bf16[512,1,640]{2,0,1:T(8,128)(2,1)}, u32[]{:S(2)}) copy-start(bf16[512,1,640]{2,0,1:T(8,128)(2,1)} %param.7) | copy-start | bytes 1966084
  101.5 21.4 %all-to-all-start.3 = ((f32[16,10,8,128]{3,2,1,0:T(8,128)}), f32[16,10,8,128]{3,2,1,0:T(8,128)}, u32[]{:S(2)}, u32[]{:S(2)}) async-start(f32[16,10,8,128]{3,2,1,0:T(8,128)} %broadcast_in_dim.2), calls=%async_computation.3 | async-start | bytes 1310720 | tf_op jit(solution)/shard_map/all_to_all | solution.py:345
  110.0 1.0 copy-start.9
  111.0 1.0 copy-start.12
Sparse Core Ops, SparseCore 0:
  17.2 40.5 all-gather.2

commit v6 on v5

--- a/solution.py
+++ b/solution.py
@@ -277,7 +277,7 @@
             pltpu.VMEM((C, TAPS * C), bf16),
         ],
         compiler_params=params(32),
-        cost_estimate=pl.CostEstimate(flops=1_000_000, bytes_accessed=1_000_000, transcendentals=0),
+        cost_estimate=pl.CostEstimate(flops=2 * TAPS * C * C * S, bytes_accessed=7_000_000, transcendentals=0),
         name=name,
     )(*args)
 
@@ -338,13 +338,13 @@
     ends = jnp.broadcast_to(ends[:, :8].T[:, :, None], (8, 8, 128))[None]
     line = jnp.concatenate((outer[:3], middle, outer[3:], ends), axis=0).transpose(1, 0, 2, 3)
     lines = lax.all_to_all(line, "z", 0, 0, tiled=True)
+    (g,) = after((g,), line)
+    grad_frames = convolve(backward_kernel, "backward", place, g, above, below, own, *other)
+    lines, grad_frames = lax.optimization_barrier((lines, grad_frames))
     scale = 1.0 / math.sqrt(4 * 256 * 160)
     done = jnp.sum(lines, axis=0) * scale
     whole = jnp.broadcast_to(done, (16, 10, 8, 128))
-    whole, g = lax.optimization_barrier((whole, g))
     whole = lax.all_to_all(whole, ("y", "xh", "core"), 0, 0, tiled=True)
-    grad_frames = convolve(backward_kernel, "backward", place, g, above, below, own, *other)
-    whole, grad_frames = lax.optimization_barrier((whole, grad_frames))
     whole = whole.reshape(4, 2, 2, 10, 8, 128)
     grad_weight = whole[:, :, :, :9].reshape(4, 2, 2, 3, 3, 8, 128)
     grad_weight = grad_weight.transpose(0, 5, 3, 4, 2, 1, 6).reshape(32, 3, 3, C)

time: 134 us -> 129 us (0.963)
  blocking collectives: 13.8 us -> 20.7 us
  local copies, waits for them, and re-layouts: 20.9 us -> 15 us
  starting transfers between devices: 35.4 us -> 31.9 us
  waiting for transfers between devices: 18.9 us -> 17.4 us
    all_to_all x1, blocking collectives: 13.8 us -> 20.7 us  [local(): whole = lax.all_to_all(whole, ('y', 'xh', 'core'), 0, 0, tiled=True)]
    all_to_all x1, starting transfers between devices: 8.55 us -> 3.43 us  [local(): lines = lax.all_to_all(line, 'z', 0, 0, tiled=True)]
    unnamed x38 -> x20, local copies, waits for them, and re-layouts: 10.8 us -> 6.96 us
    ppermute x7, starting transfers between devices: 5.66 us -> 7.33 us  [swap_cores(): return lax.ppermute(x, 'core', [(0, 1), (1, 0)])]
    all_to_all x1, waiting for transfers between devices: 2.94 us -> 1.55 us  [local(): lines = lax.all_to_all(line, 'z', 0, 0, tiled=True)]
  transfers between devices with their start and end apart: 14 -> 14, of which waited for: 8 -> 9; matrix products, arithmetic and copies ran while one was open for 7% -> 7% of each run, Pallas kernels for 16% -> 17%
where the time goes in v6:
time: 129 us; the launch traced here: 128 us
  starting transfers between devices  31.9 us (25%)
  Pallas kernels  21.7 us (17%)
  blocking collectives  20.7 us (16%)
  waiting for transfers between devices  17.4 us (13%)
  local copies, waits for them, and re-layouts  15 us (12%)
  between operations  14.3 us (11%)
  other arithmetic  7.28 us (6%)
    all_to_all x1, blocking collectives, local(): whole = lax.all_to_all(whole, ('y', 'xh', 'core'), 0, 0, tiled=True)  20.7 us
    pallas_call x2, Pallas kernels, convolve(): pl.pallas_call(body, out_shape=jax.ShapeDtypeStruct((C, S), bf16), in_spe...  15.3 us
    ppermute x1, starting transfers between devices, local(): below = lax.ppermute(first, CELLS, down)  7.91 us
    all_to_all x1, waiting for transfers between devices, local(): got = lax.all_to_all(sent, plane, 0, 0, tiled=True)  7.71 us
    ppermute x7, starting transfers between devices, swap_cores(): return lax.ppermute(x, 'core', [(0, 1), (1, 0)])  7.33 us
    unnamed x20, local copies, waits for them, and re-layouts  6.96 us
    all_to_all x1, starting transfers between devices, local(): got = lax.all_to_all(sent, plane, 0, 0, tiled=True)  6.51 us
    all_to_all x1, starting transfers between devices, local(): got2 = lax.all_to_all(sent2, plane, 0, 0, tiled=True)  4.42 us
  transfers between devices with their start and end apart: 14, of which 9 were waited for; matrix products, arithmetic and copies ran while one was open for 7% of the time, Pallas kernels for 17%

profile of v6, /device:TPU:1, one launch (start us, length us, event | category | flops | bytes accessed | tf_op | source)
XLA Modules:
  0.0 128.3 jit_solution(4886856506881361935)
XLA Ops:
  7.2 3.3 %collective-permute-start.2 = (bf16[512,640]{1,0:T(8,128)(2,1)}, bf16[512,640]{1,0:T(8,128)(2,1)S(1)}, u32[]{:S(2)}, u32[]{:S(2)}) collective-permute-start(bf16[512,640]{1,0:T(8,128)(2,1)} %bitcast.26), channel_id=1, source_target_pairs={{0,16},{16,0},{1,17},{17,1},{2,18},{18,2},{3,19},{19,3},{4,20},{20... | collective-permute-start | bytes 1966088 | tf_op jit(solution)/shard_map/ppermute | solution.py:286
  10.6 0.1 collective-permute-start.3
  10.7 0.1 collective-permute-start.5
  10.8 1.1 copy-done.1
  11.9 1.1 copy-done.3
  13.0 0.2 pack.1
  13.1 0.7 copy-done.7
  13.9 0.7 copy-done.8
  14.6 0.8 collective-permute-done.5
  15.4 0.7 pad_maximum_fusion.1
  16.2 2.2 %collective-permute-start = (bf16[2,640,128]{2,1,0:T(8,128)(2,1)}, bf16[2,640,128]{2,1,0:T(8,128)(2,1)S(1)}, u32[]{:S(2)}, u32[]{:S(2)}) collective-permute-start(bf16[2,640,128]{2,1,0:T(8,128)(2,1)} %copy-done.8), channel_id=1, source_target_pairs={{0,1},{1,2},{2,3},{3,4},{4,5},{5,6},{6,7},{7,8},{8,9},{9,10},{10,1... | collective-permute-start | bytes 983048 | tf_op jit(solution)/shard_map/ppermute | solution.py:316
  18.4 7.9 %collective-permute-start.1 = (bf16[2,640,128]{2,1,0:T(8,128)(2,1)}, bf16[2,640,128]{2,1,0:T(8,128)(2,1)}, u32[]{:S(2)}, u32[]{:S(2)}) collective-permute-start(bf16[2,640,128]{2,1,0:T(8,128)(2,1)} %copy-done.7), channel_id=1, source_target_pairs={{1,0},{2,1},{3,2},{4,3},{5,4},{6,5},{7,6},{8,7},{9,8},{10,9},{11,1... | collective-permute-start | bytes 983048 | tf_op jit(solution)/shard_map/ppermute | solution.py:317
  26.4 2.2 %middle_taps.1 = f32[16,208,128]{2,1,0:T(8,128)S(1)} custom-call(s32[2]{0:T(128)S(1)} %pad_add_fusion.core_ref, bf16[512,640]{1,0:T(8,128)(2,1)S(1)} %bitcast.28, bf16[512,640]{1,0:T(8,128)(2,1)S(1)} %bitcast.33, bf16[512,640]{1,0:T(8,128)(2,1)S(1)} %collective-permute-done.2.fx_ref, bf16[512,640]{1,0:T(8,128)(2,1)S(1)} %collective-permute-done.3.gx_ref), custom_call_target="tpu_custom_call" | custom-call | flops 1006632960 | bytes 5000000 | tf_op jit(solution)/shard_map/middle_taps/pallas_call | solution.py:159
  28.7 1.0 convert_element_type.16
  29.7 6.5 %all-to-all-start = ((f16[16,208,128]{2,1,0:T(8,128)(2,1)}), f16[16,208,128]{2,1,0:T(8,128)(2,1)}, u32[]{:S(2)}, u32[]{:S(2)}) async-start(f16[16,208,128]{2,1,0:T(8,128)(2,1)} %convert_element_type.16), calls=%async_computation | async-start | bytes 1703936 | tf_op jit(solution)/shard_map/all_to_all | solution.py:321
  36.2 0.9 slice.64
  37.2 0.1 collective-permute-start.4
  37.3 1.6 %collective-permute-done.4.halo_ref = bf16[2,640,128]{2,1,0:T(8,128)(2,1)S(1)} collective-permute-done((bf16[2,640,128]{2,1,0:T(8,128)(2,1)S(1)}, bf16[2,640,128]{2,1,0:T(8,128)(2,1)S(1)}, u32[]{:S(2)}, u32[]{:S(2)}) %collective-permute-start.4) | collective-permute-done | bytes 327712 | tf_op jit(solution)/shard_map/ppermute | solution.py:286
  38.9 4.0 %outer_taps.1 = f32[16,400,128]{2,1,0:T(8,128)S(1)} custom-call(s32[2]{0:T(128)S(1)} %pad_add_fusion.core_ref, bf16[512,640]{1,0:T(8,128)(2,1)S(1)} %bitcast.29, bf16[512,640]{1,0:T(8,128)(2,1)S(1)} %bitcast.34, bf16[2,640,128]{2,1,0:T(8,128)(2,1)S(1)} %collective-permute-done.before_ref, bf16[2,640,128]{2,1,0:T(8,128)(2,1)} %collective-permute-done.1.after_ref, ...), custom_call_target="tpu_custom_call" | custom-call | flops 2013265920 | bytes 7000000 | tf_op jit(solution)/shard_map/outer_taps/pallas_call | solution.py:206
  42.9 1.4 %convert_element_type.17 = f16[16,400,128]{2,1,0:T(8,128)(2,1)} convert(f32[16,400,128]{2,1,0:T(8,128)S(1)} %outer_taps.1) | non-fusion elementwise | flops 819200 | bytes 4915200 | tf_op jit(solution)/shard_map/convert_element_type | solution.py:326
  44.3 7.7 %all-to-all-done = f16[16,208,128]{2,1,0:T(8,128)(2,1)} async-done(((f16[16,208,128]{2,1,0:T(8,128)(2,1)}), f16[16,208,128]{2,1,0:T(8,128)(2,1)}, u32[]{:S(2)}, u32[]{:S(2)}) %all-to-all-start) | async-done | bytes 852000 | tf_op jit(solution)/shard_map/all_to_all | solution.py:321
  52.0 4.4 %all-to-all-start.1 = ((f16[16,400,128]{2,1,0:T(8,128)(2,1)}), f16[16,400,128]{2,1,0:T(8,128)(2,1)}, u32[]{:S(2)}, u32[]{:S(2)}) async-start(f16[16,400,128]{2,1,0:T(8,128)(2,1)} %convert_element_type.17), calls=%async_computation.1 | async-start | bytes 3276800 | tf_op jit(solution)/shard_map/all_to_all | solution.py:327
  56.5 0.1 copy.20.bias_ref
  56.6 0.8 slice.87
  57.4 0.2 all-gather.3.cloned.1.call-done
  57.6 2.8 %fusion.10 = (bf16[2,2,9,32,256]{4,3,2,1,0:T(8,128)(2,1)S(1)}, bf16[2,2,9,32,256]{4,3,2,1,0:T(8,128)(2,1)}, bf16[2,2,9,32,256]{4,3,2,1,0:T(8,128)(2,1)}, bf16[2,2,9,32,256]{4,3,2,1,0:T(8,128)(2,1)}) fusion(bf16[8,2,9,32,256]{4,3,2,1,0:T(8,128)(2,1)} %bitcast.36), kind=kLoop, calls=%fused_computation.24 | loop fusion | bytes 4718592 | tf_op jit(solution)/shard_map/slice | solution.py:329
  60.5 3.3 %collective-permute-start.6 = (bf16[2,2,9,32,256]{4,3,2,1,0:T(8,128)(2,1)}, bf16[2,2,9,32,256]{4,3,2,1,0:T(8,128)(2,1)S(1)}, u32[]{:S(2)}, u32[]{:S(2)}) collective-permute-start(bf16[2,2,9,32,256]{4,3,2,1,0:T(8,128)(2,1)} %get-tuple-element.35), channel_id=1, source_target_pairs={{0,16},{16,0},{1,17},{17,1},{2,18},{18,2},{3,19},{19,3},{4,20},{20... | collective-permute-start | bytes 1769480 | tf_op jit(solution)/shard_map/ppermute | solution.py:286
  63.7 0.5 collective-permute-start.8
  64.2 0.4 fusion.8
  64.6 0.1 multiply_reduce_fusion.2
  64.8 1.4 %multiply_reduce_fusion.1 = f32[192,128]{1,0:T(8,128)S(1)} fusion(f16[16,208,128]{2,1,0:T(8,128)(2,1)} %all-to-all-done, f32[16]{0:T(128)S(1)} %get-tuple-element.30), kind=kLoop, calls=%fused_computation.1 | loop fusion | flops 1155072 | bytes 884800 | tf_op jit(solution)/shard_map/reduce_sum | solution.py:291
  66.2 0.2 collective-permute-done.6.o0_ref
  66.4 0.2 collective-permute-done.7.o1_ref
  66.6 1.7 %collective-permute-done.8.o2_ref = bf16[2,2,9,32,256]{4,3,2,1,0:T(8,128)(2,1)} collective-permute-done((bf16[2,2,9,32,256]{4,3,2,1,0:T(8,128)(2,1)}, bf16[2,2,9,32,256]{4,3,2,1,0:T(8,128)(2,1)}, u32[]{:S(2)}, u32[]{:S(2)}) %collective-permute-start.8) | collective-permute-done | bytes 589856 | tf_op jit(solution)/shard_map/ppermute | solution.py:286
  68.2 1.7 %copy-done.5 = bf16[16,9,32,256]{3,2,1,0:T(8,128)(2,1)S(1)} copy-done((bf16[16,9,32,256]{3,2,1,0:T(8,128)(2,1)S(1)}, bf16[16,9,32,256]{3,2,1,0:T(8,128)(2,1)}, u32[]{:S(2)}) %copy-start.5) | copy-done | bytes 2359320
  69.9 7.5 %forward.1 = bf16[512,640]{1,0:T(8,128)(2,1)} custom-call(s32[2]{0:T(128)S(1)} %pad_add_fusion.core_ref, bf16[512,640]{1,0:T(8,128)(2,1)S(1)} %bitcast.30, bf16[2,640,128]{2,1,0:T(8,128)(2,1)S(1)} %collective-permute-done.before_ref, bf16[2,640,128]{2,1,0:T(8,128)(2,1)} %collective-permute-done.1.after_ref, bf16[8,2,9,32,256]{4,3,2,1,0:T(8,128)(2,1)S(1)} %bitcast.37, ...), custom_call_target="tpu_custom_call" | custom-call | flops 3019898880 | bytes 7000000 | tf_op jit(solution)/shard_map/forward/pallas_call | solution.py:269
  77.4 3.4 %all-to-all-done.1 = f16[16,400,128]{2,1,0:T(8,128)(2,1)} async-done(((f16[16,400,128]{2,1,0:T(8,128)(2,1)}), f16[16,400,128]{2,1,0:T(8,128)(2,1)}, u32[]{:S(2)}, u32[]{:S(2)}) %all-to-all-start.1) | async-done | bytes 1638432 | tf_op jit(solution)/shard_map/all_to_all | solution.py:327
  80.8 0.8 slice.70
  81.6 0.3 fusion.7
  81.9 1.8 %multiply_reduce_fusion = f32[384,128]{1,0:T(8,128)S(1)} fusion(f32[16]{0:T(128)S(1)} %fusion.7, f16[16,400,128]{2,1,0:T(8,128)(2,1)} %all-to-all-done.1), kind=kLoop, calls=%fused_computation | loop fusion | flops 2310144 | bytes 1769536 | tf_op jit(solution)/shard_map/reduce_sum | solution.py:291
  83.8 0.7 copy.22
  84.6 3.4 %all-to-all-start.2 = ((f32[8,10,8,128]{3,2,1,0:T(8,128)}), f32[8,10,8,128]{3,2,1,0:T(8,128)S(1)}, u32[]{:S(2)}, u32[]{:S(2)}) async-start(f32[8,10,8,128]{3,2,1,0:T(8,128)} %copy.22), calls=%async_computation.2 | async-start | bytes 655360 | tf_op jit(solution)/shard_map/all_to_all | solution.py:340
  88.0 1.7 %copy-done.6 = bf16[16,9,32,256]{3,2,1,0:T(8,128)(2,1)S(1)} copy-done((bf16[16,9,32,256]{3,2,1,0:T(8,128)(2,1)S(1)}, bf16[16,9,32,256]{3,2,1,0:T(8,128)(2,1)}, u32[]{:S(2)}) %copy-start.6) | copy-done | bytes 2359320
  89.7 7.8 %backward.1 = bf16[512,640]{1,0:T(8,128)(2,1)} custom-call(s32[2]{0:T(128)S(1)} %pad_add_fusion.core_ref, bf16[512,640]{1,0:T(8,128)(2,1)S(1)} %bitcast.35, bf16[2,640,128]{2,1,0:T(8,128)(2,1)S(1)} %collective-permute-done.before_ref, bf16[2,640,128]{2,1,0:T(8,128)(2,1)} %collective-permute-done.1.after_ref, bf16[8,2,9,32,256]{4,3,2,1,0:T(8,128)(2,1)S(1)} %bitcast.38, ...), custom_call_target="tpu_custom_call" | custom-call | flops 3019898880 | bytes 7000000 | tf_op jit(solution)/shard_map/backward/pallas_call | solution.py:269
  97.5 1.5 %all-to-all-done.2 = f32[8,10,8,128]{3,2,1,0:T(8,128)S(1)} async-done(((f32[8,10,8,128]{3,2,1,0:T(8,128)}), f32[8,10,8,128]{3,2,1,0:T(8,128)S(1)}, u32[]{:S(2)}, u32[]{:S(2)}) %all-to-all-start.2) | async-done | bytes 327712 | tf_op jit(solution)/shard_map/all_to_all | solution.py:340
  99.1 20.7 %all_to_all.20 = f32[16,10,8,128]{3,2,1,0:T(8,128)S(1)} all-to-all(f32[16,10,8,128]{3,2,1,0:T(8,128)S(1)} %broadcast_in_dim.2), channel_id=1, replica_groups=mesh['y'=4,'xh'=2,'core'=2,'xl'=2,'z'=8] {'y','xh','core'}, dimensions={0} | all-to-all | bytes 1310720 | tf_op jit(solution)/shard_map/all_to_all | solution.py:347
  119.9 0.9 copy.23
  120.8 0.6 reshape_squeeze.3
  (38 shorter events, 0.6 us)
Async XLA Ops:
  7.2 3.5 %copy-start = (bf16[32,3,3,512]{3,0,2,1:T(8,128)(2,1)S(1)}, bf16[32,3,3,512]{3,0,2,1:T(8,128)(2,1)}, u32[]{:S(2)}) copy-start(bf16[32,3,3,512]{3,0,2,1:T(8,128)(2,1)} %param.5) | copy-start | bytes 884740
  7.2 50.4 %all-gather.3.cloned.1.call-start = ((), (), s32[]{:S(2)}) async-start(), calls=%async_computation.4 | async-start | bytes 2654208 | tf_op jit(solution)/shard_map/all_gather | solution.py:315
  7.2 8.2 %collective-permute-start.2 = (bf16[512,640]{1,0:T(8,128)(2,1)}, bf16[512,640]{1,0:T(8,128)(2,1)S(1)}, u32[]{:S(2)}, u32[]{:S(2)}) collective-permute-start(bf16[512,640]{1,0:T(8,128)(2,1)} %bitcast.26), channel_id=1, source_target_pairs={{0,16},{16,0},{1,17},{17,1},{2,18},{18,2},{3,19},{19,3},{4,20},{20... | collective-permute-start | bytes 1966088 | tf_op jit(solution)/shard_map/ppermute | solution.py:286
  10.6 4.9 %collective-permute-start.3 = (bf16[512,640]{1,0:T(8,128)(2,1)}, bf16[512,640]{1,0:T(8,128)(2,1)S(1)}, u32[]{:S(2)}, u32[]{:S(2)}) collective-permute-start(bf16[512,640]{1,0:T(8,128)(2,1)} %bitcast.31), channel_id=1, source_target_pairs={{0,16},{16,0},{1,17},{17,1},{2,18},{18,2},{3,19},{19,3},{4,20},{20... | collective-permute-start | bytes 1966088 | tf_op jit(solution)/shard_map/ppermute | solution.py:286
  10.7 4.8 %collective-permute-start.5 = (bf16[9,32,256]{2,1,0:T(8,128)(2,1)S(1)}, bf16[9,32,256]{2,1,0:T(8,128)(2,1)S(1)}, u32[]{:S(2)}, u32[]{:S(2)}) collective-permute-start(bf16[9,32,256]{2,1,0:T(8,128)(2,1)S(1)} %constant_dynamic-slice_fusion), channel_id=1, source_target_pairs={{0,8},{8,0},{1,9},{9,1},{2,10},{10,2},{3,11},{11,3},{4,12},{12,4},... | collective-permute-start | bytes 442376 | tf_op jit(solution)/shard_map/ppermute | solution.py:309
  10.8 1.1 copy-start.1
  11.9 1.1 copy-start.3
  13.0 13.5 %copy-start.2 = (bf16[512,1,640]{2,0,1:T(8,128)(2,1)S(1)}, bf16[512,1,640]{2,0,1:T(8,128)(2,1)}, u32[]{:S(2)}) copy-start(bf16[512,1,640]{2,0,1:T(8,128)(2,1)} %param.4) | copy-start | bytes 1966084
  13.0 13.5 %copy-start.4 = (bf16[512,1,640]{2,0,1:T(8,128)(2,1)S(1)}, bf16[512,1,640]{2,0,1:T(8,128)(2,1)}, u32[]{:S(2)}) copy-start(bf16[512,1,640]{2,0,1:T(8,128)(2,1)} %param.7) | copy-start | bytes 1966084
  13.1 0.7 copy-start.7
  13.9 0.7 copy-start.8
  16.2 20.0 %collective-permute-start = (bf16[2,640,128]{2,1,0:T(8,128)(2,1)}, bf16[2,640,128]{2,1,0:T(8,128)(2,1)S(1)}, u32[]{:S(2)}, u32[]{:S(2)}) collective-permute-start(bf16[2,640,128]{2,1,0:T(8,128)(2,1)} %copy-done.8), channel_id=1, source_target_pairs={{0,1},{1,2},{2,3},{3,4},{4,5},{5,6},{6,7},{7,8},{8,9},{9,10},{10,1... | collective-permute-start | bytes 983048 | tf_op jit(solution)/shard_map/ppermute | solution.py:316
  18.4 17.8 %collective-permute-start.1 = (bf16[2,640,128]{2,1,0:T(8,128)(2,1)}, bf16[2,640,128]{2,1,0:T(8,128)(2,1)}, u32[]{:S(2)}, u32[]{:S(2)}) collective-permute-start(bf16[2,640,128]{2,1,0:T(8,128)(2,1)} %copy-done.7), channel_id=1, source_target_pairs={{1,0},{2,1},{3,2},{4,3},{5,4},{6,5},{7,6},{8,7},{9,8},{10,9},{11,1... | collective-permute-start | bytes 983048 | tf_op jit(solution)/shard_map/ppermute | solution.py:317
  29.7 22.3 %all-to-all-start = ((f16[16,208,128]{2,1,0:T(8,128)(2,1)}), f16[16,208,128]{2,1,0:T(8,128)(2,1)}, u32[]{:S(2)}, u32[]{:S(2)}) async-start(f16[16,208,128]{2,1,0:T(8,128)(2,1)} %convert_element_type.16), calls=%async_computation | async-start | bytes 1703936 | tf_op jit(solution)/shard_map/all_to_all | solution.py:321
  37.2 1.7 %collective-permute-start.4 = (bf16[2,640,128]{2,1,0:T(8,128)(2,1)S(1)}, bf16[2,640,128]{2,1,0:T(8,128)(2,1)S(1)}, u32[]{:S(2)}, u32[]{:S(2)}) collective-permute-start(bf16[2,640,128]{2,1,0:T(8,128)(2,1)S(1)} %pad_maximum_fusion), channel_id=1, source_target_pairs={{0,16},{16,0},{1,17},{17,1},{2,18},{18,2},{3,19},{19,3},{4,20},{20... | collective-permute-start | bytes 983048 | tf_op jit(solution)/shard_map/ppermute | solution.py:286
  44.3 12.1 %copy-start.9 = (f32[512]{0:T(512)S(1)}, f32[512]{0:T(512)}, u32[]{:S(2)}) copy-start(f32[512]{0:T(512)} %param.6) | copy-start | bytes 6148
  52.0 28.8 %all-to-all-start.1 = ((f16[16,400,128]{2,1,0:T(8,128)(2,1)}), f16[16,400,128]{2,1,0:T(8,128)(2,1)}, u32[]{:S(2)}, u32[]{:S(2)}) async-start(f16[16,400,128]{2,1,0:T(8,128)(2,1)} %convert_element_type.17), calls=%async_computation.1 | async-start | bytes 3276800 | tf_op jit(solution)/shard_map/all_to_all | solution.py:327
  60.5 5.9 %collective-permute-start.6 = (bf16[2,2,9,32,256]{4,3,2,1,0:T(8,128)(2,1)}, bf16[2,2,9,32,256]{4,3,2,1,0:T(8,128)(2,1)S(1)}, u32[]{:S(2)}, u32[]{:S(2)}) collective-permute-start(bf16[2,2,9,32,256]{4,3,2,1,0:T(8,128)(2,1)} %get-tuple-element.35), channel_id=1, source_target_pairs={{0,16},{16,0},{1,17},{17,1},{2,18},{18,2},{3,19},{19,3},{4,20},{20... | collective-permute-start | bytes 1769480 | tf_op jit(solution)/shard_map/ppermute | solution.py:286
  63.7 2.8 %collective-permute-start.7 = (bf16[2,2,9,32,256]{4,3,2,1,0:T(8,128)(2,1)}, bf16[2,2,9,32,256]{4,3,2,1,0:T(8,128)(2,1)}, u32[]{:S(2)}, u32[]{:S(2)}) collective-permute-start(bf16[2,2,9,32,256]{4,3,2,1,0:T(8,128)(2,1)} %get-tuple-element.34), channel_id=1, source_target_pairs={{0,16},{16,0},{1,17},{17,1},{2,18},{18,2},{3,19},{19,3},{4,20},{20... | collective-permute-start | bytes 1769480 | tf_op jit(solution)/shard_map/ppermute | solution.py:286
  63.7 4.5 %collective-permute-start.8 = (bf16[2,2,9,32,256]{4,3,2,1,0:T(8,128)(2,1)}, bf16[2,2,9,32,256]{4,3,2,1,0:T(8,128)(2,1)}, u32[]{:S(2)}, u32[]{:S(2)}) collective-permute-start(bf16[2,2,9,32,256]{4,3,2,1,0:T(8,128)(2,1)} %get-tuple-element.33), channel_id=1, source_target_pairs={{0,16},{16,0},{1,17},{17,1},{2,18},{18,2},{3,19},{19,3},{4,20},{20... | collective-permute-start | bytes 1769480 | tf_op jit(solution)/shard_map/ppermute | solution.py:286
  64.2 4.0 %collective-permute-start.9 = (bf16[2,2,9,32,256]{4,3,2,1,0:T(8,128)(2,1)S(1)}, bf16[2,2,9,32,256]{4,3,2,1,0:T(8,128)(2,1)}, u32[]{:S(2)}, u32[]{:S(2)}) collective-permute-start(bf16[2,2,9,32,256]{4,3,2,1,0:T(8,128)(2,1)S(1)} %get-tuple-element.32), channel_id=1, source_target_pairs={{0,16},{16,0},{1,17},{17,1},{2,18},{18,2},{3,19},{19,3},{4,20},{20... | collective-permute-start | bytes 1769480 | tf_op jit(solution)/shard_map/ppermute | solution.py:286
  68.2 1.7 %copy-start.5 = (bf16[16,9,32,256]{3,2,1,0:T(8,128)(2,1)S(1)}, bf16[16,9,32,256]{3,2,1,0:T(8,128)(2,1)}, u32[]{:S(2)}) copy-start(bf16[16,9,32,256]{3,2,1,0:T(8,128)(2,1)} %all-gather.3.cloned.1.call-done) | copy-start | bytes 7077892
  84.6 14.5 %all-to-all-start.2 = ((f32[8,10,8,128]{3,2,1,0:T(8,128)}), f32[8,10,8,128]{3,2,1,0:T(8,128)S(1)}, u32[]{:S(2)}, u32[]{:S(2)}) async-start(f32[8,10,8,128]{3,2,1,0:T(8,128)} %copy.22), calls=%async_computation.2 | async-start | bytes 655360 | tf_op jit(solution)/shard_map/all_to_all | solution.py:340
  88.0 1.7 %copy-start.6 = (bf16[16,9,32,256]{3,2,1,0:T(8,128)(2,1)S(1)}, bf16[16,9,32,256]{3,2,1,0:T(8,128)(2,1)}, u32[]{:S(2)}) copy-start(bf16[16,9,32,256]{3,2,1,0:T(8,128)(2,1)} %all-gather.3.cloned.1.call-done) | copy-start | bytes 7077892
Sparse Core Ops, SparseCore 0:
  16.3 41.2 all-gather.2

commit v7 on v6

--- a/solution.py
+++ b/solution.py
@@ -49,19 +49,19 @@
     return jnp.concatenate([wide, total.astype(bf16)], axis=0)
 
 
-def pack_kernel(f_ref, g_ref, last_ref, first_ref):
-    for k, x in enumerate((f_ref, g_ref)):
-        last_ref[k] = pack_row(x[:, 512:640], x[:, 384:512], 96)
-        first_ref[k] = pack_row(x[:, 0:128], x[:, 128:256], 0)
+def pack_kernel(f_ref, g_ref, fl_ref, ff_ref, gl_ref, gf_ref):
+    for x, last, first in ((f_ref, fl_ref, ff_ref), (g_ref, gl_ref, gf_ref)):
+        last[...] = pack_row(x[:, 512:640], x[:, 384:512], 96)
+        first[...] = pack_row(x[:, 0:128], x[:, 128:256], 0)
 
 
 def pack(f, g):
-    rows = jax.ShapeDtypeStruct((2, 640, 128), bf16)
+    row = jax.ShapeDtypeStruct((640, 128), bf16)
     return pl.pallas_call(
         pack_kernel,
-        out_shape=(rows, rows),
+        out_shape=(row,) * 4,
         in_specs=[vmem(), vmem()],
-        out_specs=(vmem(), vmem()),
+        out_specs=(vmem(),) * 4,
         compiler_params=params(12),
         name="pack",
     )(f, g)
@@ -182,8 +182,8 @@
     for seg in range(2):
         if seg == 0:
             cells = f_ref[pl.ds(mine, HALF), :]
-            before = (before_ref[0, pl.ds(mine, HALF), :], before_ref[0, C:, :])
-            after = (after_ref[0, pl.ds(mine, HALF), :], after_ref[0, C:, :])
+            before = (before_ref[pl.ds(mine, HALF), :], before_ref[C:, :])
+            after = (after_ref[pl.ds(mine, HALF), :], after_ref[C:, :])
         else:
             cells = fx_ref[pl.ds(mine, HALF), :]
             before = (halo_ref[0, pl.ds(mine, HALF), :], halo_ref[0, C:, :])
@@ -234,7 +234,7 @@
 def forward_kernel(core_ref, f_ref, before_ref, after_ref, own_ref, o0_ref, o1_ref, o2_ref, o3_ref, bias_ref, out_ref, ext, win, kern):
     load_kernel(core_ref, own_ref, (o0_ref, o1_ref, o2_ref, o3_ref), kern)
     masks = column_masks(C)
-    fill(ext, C, f_ref[...], (before_ref[0, :C, :], before_ref[0, C:, :]), (after_ref[0, :C, :], after_ref[0, C:, :]), GROUPS)
+    fill(ext, C, f_ref[...], (before_ref[:C, :], before_ref[C:, :]), (after_ref[:C, :], after_ref[C:, :]), GROUPS)
     for a in range(3):
         for b in range(3):
             t = 3 * a + b
@@ -248,7 +248,7 @@
 def backward_kernel(core_ref, g_ref, before_ref, after_ref, own_ref, o0_ref, o1_ref, o2_ref, o3_ref, grad_ref, ext, win, kern):
     load_kernel(core_ref, own_ref, (o0_ref, o1_ref, o2_ref, o3_ref), kern)
     masks = column_masks(C)
-    fill(ext, C, g_ref[...], (before_ref[1, :C, :], before_ref[1, C:, :]), (after_ref[1, :C, :], after_ref[1, C:, :]), GROUPS)
+    fill(ext, C, g_ref[...], (before_ref[:C, :], before_ref[C:, :]), (after_ref[:C, :], after_ref[C:, :]), GROUPS)
     for a in range(3):
         for b in range(3):
             t = 3 * a + b
@@ -310,17 +310,17 @@
 
     fx = swap_cores(f)
     gx = swap_cores(g)
-    last, first = pack(f, g)
-    half, beside = after((half, beside), last, fx, gx)
+    fl, ff, gl, gf = pack(f, g)
+    half, beside = after((half, beside), fl, fx, gx)
     own = lax.all_gather(jnp.stack((half, beside)), "z", axis=0, tiled=False)
-    above = lax.ppermute(last, CELLS, up)
-    below = lax.ppermute(first, CELLS, down)
+    above = lax.ppermute(fl, CELLS, up)
+    below = lax.ppermute(ff, CELLS, down)
 
     part = middle_taps(place, f, g, fx, gx)
     sent = part.astype(f16)
     got = lax.all_to_all(sent, plane, 0, 0, tiled=True)
     above, below = after((above, below), sent)
-    halo = swap_cores(jnp.stack((above[0], below[0])))
+    halo = swap_cores(jnp.stack((above, below)))
 
     part2 = outer_taps(place, f, g, above, below, fx, gx, halo)
     (sent2,) = after((part2.astype(f16),), got)
@@ -328,7 +328,10 @@
     (own,) = after((own,), got)
     other = tuple(swap_cores(own[2 * k:2 * k + 2]) for k in range(4))
     outputs = convolve(forward_kernel, "forward", place, f, above, below, own, *other, bias.reshape(C, 1))
-    got2, outputs = lax.optimization_barrier((got2, outputs))
+    gl, gf = after((gl, gf), *other)
+    above_g = lax.ppermute(gl, CELLS, up)
+    below_g = lax.ppermute(gf, CELLS, down)
+    got2, outputs, above_g, below_g = lax.optimization_barrier((got2, outputs, above_g, below_g))
 
     extra = lax.optimization_barrier(got[:, 192:200]).astype(f32)
     extra2 = lax.optimization_barrier(got2[:, 384:392]).astype(f32)
@@ -339,7 +342,7 @@
     line = jnp.concatenate((outer[:3], middle, outer[3:], ends), axis=0).transpose(1, 0, 2, 3)
     lines = lax.all_to_all(line, "z", 0, 0, tiled=True)
     (g,) = after((g,), line)
-    grad_frames = convolve(backward_kernel, "backward", place, g, above, below, own, *other)
+    grad_frames = convolve(backward_kernel, "backward", place, g, above_g, below_g, own, *other)
     lines, grad_frames = lax.optimization_barrier((lines, grad_frames))
     scale = 1.0 / math.sqrt(4 * 256 * 160)
     done = jnp.sum(lines, axis=0) * scale

time: 129 us -> 136 us (1.054)
  starting transfers between devices: 31.9 us -> 39.9 us
  local copies, waits for them, and re-layouts: 15 us -> 13.6 us
    ppermute x2 -> x4, starting transfers between devices: 10.1 us -> 18 us  [the longest x1 8 us: local(): below = lax.ppermute(ff, CELLS, down)]
    all_to_all x1, waiting for transfers between devices: 3.41 us -> 0.01 us  [local(): got2 = lax.all_to_all(sent2, plane, 0, 0, tiled=True)]
    all_to_all x1, waiting for transfers between devices: 1.55 us -> 3.48 us  [local(): lines = lax.all_to_all(line, 'z', 0, 0, tiled=True)]
    all_to_all x1, waiting for transfers between devices: 7.71 us -> 9.08 us  [local(): got = lax.all_to_all(sent, plane, 0, 0, tiled=True)]
    unnamed x20 -> x22, local copies, waits for them, and re-layouts: 6.96 us -> 6.18 us
  transfers between devices with their start and end apart: 14 -> 16, of which waited for: 9 -> 8; matrix products, arithmetic and copies ran while one was open for 7% -> 6% of each run, Pallas kernels for 17% -> 16%
where the time goes in v7:
time: 136 us; the launch traced here: 135 us
  starting transfers between devices  39.9 us (29%)
  Pallas kernels  21.8 us (16%)
  blocking collectives  21 us (15%)
  waiting for transfers between devices  17.2 us (13%)
  between operations  14.3 us (11%)
  local copies, waits for them, and re-layouts  13.6 us (10%)
  other arithmetic  7.29 us (5%)
    all_to_all x1, blocking collectives, local(): whole = lax.all_to_all(whole, ('y', 'xh', 'core'), 0, 0, tiled=True)  21 us
    pallas_call x2, Pallas kernels, convolve(): pl.pallas_call(body, out_shape=jax.ShapeDtypeStruct((C, S), bf16), in_spe...  15.1 us
    all_to_all x1, waiting for transfers between devices, local(): got = lax.all_to_all(sent, plane, 0, 0, tiled=True)  9.08 us
    ppermute x1, starting transfers between devices, local(): below = lax.ppermute(ff, CELLS, down)  8 us
    ppermute x7, starting transfers between devices, swap_cores(): return lax.ppermute(x, 'core', [(0, 1), (1, 0)])  7.44 us
    all_to_all x1, starting transfers between devices, local(): got = lax.all_to_all(sent, plane, 0, 0, tiled=True)  6.51 us
    unnamed x22, local copies, waits for them, and re-layouts  6.18 us
    ppermute x1, starting transfers between devices, local(): below_g = lax.ppermute(gf, CELLS, down)  5.07 us
  transfers between devices with their start and end apart: 16, of which 8 were waited for; matrix products, arithmetic and copies ran while one was open for 6% of the time, Pallas kernels for 16%

profile of v7, /device:TPU:1, one launch (start us, length us, event | category | flops | bytes accessed | tf_op | source)
XLA Modules:
  0.0 135.1 jit_solution(14703730852666547217)
XLA Ops:
  7.2 3.3 %collective-permute-start.2 = (bf16[512,640]{1,0:T(8,128)(2,1)}, bf16[512,640]{1,0:T(8,128)(2,1)S(1)}, u32[]{:S(2)}, u32[]{:S(2)}) collective-permute-start(bf16[512,640]{1,0:T(8,128)(2,1)} %bitcast.28), channel_id=1, source_target_pairs={{0,16},{16,0},{1,17},{17,1},{2,18},{18,2},{3,19},{19,3},{4,20},{20... | collective-permute-start | bytes 1966088 | tf_op jit(solution)/shard_map/ppermute | solution.py:286
  10.6 0.1 collective-permute-start.3
  10.7 0.1 collective-permute-start.5
  10.8 1.1 copy-done.1
  11.9 1.1 copy-done.3
  13.0 0.9 pack.1
  13.8 0.7 copy-done.9
  14.5 0.9 collective-permute-done.5
  15.4 0.7 pad_maximum_fusion.1
  16.2 2.1 %collective-permute-start = (bf16[640,128]{1,0:T(8,128)(2,1)}, bf16[640,128]{1,0:T(8,128)(2,1)S(1)}, u32[]{:S(2)}, u32[]{:S(2)}) collective-permute-start(bf16[640,128]{1,0:T(8,128)(2,1)} %get-tuple-element.23), channel_id=1, source_target_pairs={{0,1},{1,2},{2,3},{3,4},{4,5},{5,6},{6,7},{7,8},{8,9},{9,10},{10,1... | collective-permute-start | bytes 491528 | tf_op jit(solution)/shard_map/ppermute | solution.py:316
  18.3 8.0 %collective-permute-start.1 = (bf16[640,128]{1,0:T(8,128)(2,1)}, bf16[640,128]{1,0:T(8,128)(2,1)S(1)}, u32[]{:S(2)}, u32[]{:S(2)}) collective-permute-start(bf16[640,128]{1,0:T(8,128)(2,1)} %copy-done.9), channel_id=1, source_target_pairs={{1,0},{2,1},{3,2},{4,3},{5,4},{6,5},{7,6},{8,7},{9,8},{10,9},{11,1... | collective-permute-start | bytes 491528 | tf_op jit(solution)/shard_map/ppermute | solution.py:317
  26.4 2.2 %middle_taps.1 = f32[16,208,128]{2,1,0:T(8,128)S(1)} custom-call(s32[2]{0:T(128)S(1)} %pad_add_fusion.core_ref, bf16[512,640]{1,0:T(8,128)(2,1)S(1)} %bitcast.30, bf16[512,640]{1,0:T(8,128)(2,1)S(1)} %bitcast.35, bf16[512,640]{1,0:T(8,128)(2,1)S(1)} %collective-permute-done.2.fx_ref, bf16[512,640]{1,0:T(8,128)(2,1)S(1)} %collective-permute-done.3.gx_ref), custom_call_target="tpu_custom_call" | custom-call | flops 1006632960 | bytes 5000000 | tf_op jit(solution)/shard_map/middle_taps/pallas_call | solution.py:159
  28.7 1.0 convert_element_type.16
  29.7 6.5 %all-to-all-start = ((f16[16,208,128]{2,1,0:T(8,128)(2,1)}), f16[16,208,128]{2,1,0:T(8,128)(2,1)}, u32[]{:S(2)}, u32[]{:S(2)}) async-start(f16[16,208,128]{2,1,0:T(8,128)(2,1)} %convert_element_type.16), calls=%async_computation | async-start | bytes 1703936 | tf_op jit(solution)/shard_map/all_to_all | solution.py:321
  36.3 0.1 collective-permute-start.4
  36.4 1.6 %collective-permute-done.4.halo_ref = bf16[2,640,128]{2,1,0:T(8,128)(2,1)S(1)} collective-permute-done((bf16[2,640,128]{2,1,0:T(8,128)(2,1)S(1)}, bf16[2,640,128]{2,1,0:T(8,128)(2,1)S(1)}, u32[]{:S(2)}, u32[]{:S(2)}) %collective-permute-start.4) | collective-permute-done | bytes 327712 | tf_op jit(solution)/shard_map/ppermute | solution.py:286
  38.0 3.6 %outer_taps.1 = f32[16,400,128]{2,1,0:T(8,128)S(1)} custom-call(s32[2]{0:T(128)S(1)} %pad_add_fusion.core_ref, bf16[512,640]{1,0:T(8,128)(2,1)S(1)} %bitcast.31, bf16[512,640]{1,0:T(8,128)(2,1)S(1)} %bitcast.36, bf16[640,128]{1,0:T(8,128)(2,1)S(1)} %collective-permute-done.before_ref, bf16[640,128]{1,0:T(8,128)(2,1)S(1)} %collective-permute-done.1.after_ref, ...), custom_call_target="tpu_custom_call" | custom-call | flops 2013265920 | bytes 7000000 | tf_op jit(solution)/shard_map/outer_taps/pallas_call | solution.py:206
  41.5 1.4 %convert_element_type.17 = f16[16,400,128]{2,1,0:T(8,128)(2,1)} convert(f32[16,400,128]{2,1,0:T(8,128)S(1)} %outer_taps.1) | non-fusion elementwise | flops 819200 | bytes 4915200 | tf_op jit(solution)/shard_map/convert_element_type | solution.py:326
  42.9 9.1 %all-to-all-done = f16[16,208,128]{2,1,0:T(8,128)(2,1)} async-done(((f16[16,208,128]{2,1,0:T(8,128)(2,1)}), f16[16,208,128]{2,1,0:T(8,128)(2,1)}, u32[]{:S(2)}, u32[]{:S(2)}) %all-to-all-start) | async-done | bytes 852000 | tf_op jit(solution)/shard_map/all_to_all | solution.py:321
  52.0 4.4 %all-to-all-start.1 = ((f16[16,400,128]{2,1,0:T(8,128)(2,1)}), f16[16,400,128]{2,1,0:T(8,128)(2,1)}, u32[]{:S(2)}, u32[]{:S(2)}) async-start(f16[16,400,128]{2,1,0:T(8,128)(2,1)} %convert_element_type.17), calls=%async_computation.1 | async-start | bytes 3276800 | tf_op jit(solution)/shard_map/all_to_all | solution.py:327
  56.4 0.1 copy.20.bias_ref
  56.6 0.8 slice.79
  57.4 3.1 %fusion.10 = (bf16[2,2,9,32,256]{4,3,2,1,0:T(8,128)(2,1)}, bf16[2,2,9,32,256]{4,3,2,1,0:T(8,128)(2,1)}, bf16[2,2,9,32,256]{4,3,2,1,0:T(8,128)(2,1)}, bf16[2,2,9,32,256]{4,3,2,1,0:T(8,128)(2,1)}) fusion(bf16[8,2,9,32,256]{4,3,2,1,0:T(8,128)(2,1)} %bitcast.38), kind=kLoop, calls=%fused_computation.24 | loop fusion | bytes 4718592 | tf_op jit(solution)/shard_map/slice | solution.py:329
  60.6 3.4 %collective-permute-start.6 = (bf16[2,2,9,32,256]{4,3,2,1,0:T(8,128)(2,1)}, bf16[2,2,9,32,256]{4,3,2,1,0:T(8,128)(2,1)S(1)}, u32[]{:S(2)}, u32[]{:S(2)}) collective-permute-start(bf16[2,2,9,32,256]{4,3,2,1,0:T(8,128)(2,1)} %get-tuple-element.47), channel_id=1, source_target_pairs={{0,16},{16,0},{1,17},{17,1},{2,18},{18,2},{3,19},{19,3},{4,20},{20... | collective-permute-start | bytes 1769480 | tf_op jit(solution)/shard_map/ppermute | solution.py:286
  63.9 0.5 collective-permute-start.8
  64.4 0.4 fusion.8
  64.8 0.1 multiply_reduce_fusion.2
  65.0 1.4 %multiply_reduce_fusion.1 = f32[192,128]{1,0:T(8,128)S(1)} fusion(f16[16,208,128]{2,1,0:T(8,128)(2,1)} %all-to-all-done, f32[16]{0:T(128)S(1)} %get-tuple-element.42), kind=kLoop, calls=%fused_computation.1 | loop fusion | flops 1155072 | bytes 884800 | tf_op jit(solution)/shard_map/reduce_sum | solution.py:291
  66.4 0.2 collective-permute-done.6.o0_ref
  66.6 0.2 collective-permute-done.7.o1_ref
  66.7 0.8 collective-permute-done.8.o2_ref
  67.6 0.8 collective-permute-done.9.o3_ref
  68.4 2.8 %collective-permute-start.10 = (bf16[640,128]{1,0:T(8,128)(2,1)S(1)}, bf16[640,128]{1,0:T(8,128)(2,1)S(1)}, u32[]{:S(2)}, u32[]{:S(2)}) collective-permute-start(bf16[640,128]{1,0:T(8,128)(2,1)S(1)} %copy-done.8), channel_id=1, source_target_pairs={{0,1},{1,2},{2,3},{3,4},{4,5},{5,6},{6,7},{7,8},{8,9},{9,10},{10,1... | collective-permute-start | bytes 491528 | tf_op jit(solution)/shard_map/ppermute | solution.py:332
  71.2 5.1 %collective-permute-start.11 = (bf16[640,128]{1,0:T(8,128)(2,1)S(1)}, bf16[640,128]{1,0:T(8,128)(2,1)S(1)}, u32[]{:S(2)}, u32[]{:S(2)}) collective-permute-start(bf16[640,128]{1,0:T(8,128)(2,1)S(1)} %get-tuple-element.34), channel_id=1, source_target_pairs={{1,0},{2,1},{3,2},{4,3},{5,4},{6,5},{7,6},{8,7},{9,8},{10,9},{11,1... | collective-permute-start | bytes 491528 | tf_op jit(solution)/shard_map/ppermute | solution.py:333
  76.3 1.7 %copy-done.5 = bf16[16,9,32,256]{3,2,1,0:T(8,128)(2,1)S(1)} copy-done((bf16[16,9,32,256]{3,2,1,0:T(8,128)(2,1)S(1)}, bf16[16,9,32,256]{3,2,1,0:T(8,128)(2,1)}, u32[]{:S(2)}) %copy-start.5) | copy-done | bytes 2359320
  78.0 7.4 %forward.1 = bf16[512,640]{1,0:T(8,128)(2,1)} custom-call(s32[2]{0:T(128)S(1)} %pad_add_fusion.core_ref, bf16[512,640]{1,0:T(8,128)(2,1)S(1)} %bitcast.32, bf16[640,128]{1,0:T(8,128)(2,1)S(1)} %collective-permute-done.before_ref, bf16[640,128]{1,0:T(8,128)(2,1)S(1)} %collective-permute-done.1.after_ref, bf16[8,2,9,32,256]{4,3,2,1,0:T(8,128)(2,1)S(1)} %bitcast.39, ...), custom_call_target="tpu_custom_call" | custom-call | flops 3019898880 | bytes 7000000 | tf_op jit(solution)/shard_map/forward/pallas_call | solution.py:269
  85.4 0.8 slice.62
  86.1 0.3 fusion.7
  86.4 1.8 %multiply_reduce_fusion = f32[384,128]{1,0:T(8,128)S(1)} fusion(f32[16]{0:T(128)S(1)} %fusion.7, f16[16,400,128]{2,1,0:T(8,128)(2,1)} %all-to-all-done.1), kind=kLoop, calls=%fused_computation | loop fusion | flops 2310144 | bytes 1769536 | tf_op jit(solution)/shard_map/reduce_sum | solution.py:291
  88.4 0.7 copy.22
  89.1 3.4 %all-to-all-start.2 = ((f32[8,10,8,128]{3,2,1,0:T(8,128)}), f32[8,10,8,128]{3,2,1,0:T(8,128)S(1)}, u32[]{:S(2)}, u32[]{:S(2)}) async-start(f32[8,10,8,128]{3,2,1,0:T(8,128)} %copy.22), calls=%async_computation.2 | async-start | bytes 655360 | tf_op jit(solution)/shard_map/all_to_all | solution.py:343
  92.6 1.7 %copy-done.6 = bf16[16,9,32,256]{3,2,1,0:T(8,128)(2,1)S(1)} copy-done((bf16[16,9,32,256]{3,2,1,0:T(8,128)(2,1)S(1)}, bf16[16,9,32,256]{3,2,1,0:T(8,128)(2,1)}, u32[]{:S(2)}) %copy-start.6) | copy-done | bytes 2359320
  94.3 7.8 %backward.1 = bf16[512,640]{1,0:T(8,128)(2,1)} custom-call(s32[2]{0:T(128)S(1)} %pad_add_fusion.core_ref, bf16[512,640]{1,0:T(8,128)(2,1)S(1)} %bitcast.37, bf16[640,128]{1,0:T(8,128)(2,1)S(1)} %collective-permute-done.10.before_ref, bf16[640,128]{1,0:T(8,128)(2,1)S(1)} %collective-permute-done.11.after_ref, bf16[8,2,9,32,256]{4,3,2,1,0:T(8,128)(2,1)S(1)} %bitcast.40, ...), custom_call_target="tpu_custom_call" | custom-call | flops 3019898880 | bytes 7000000 | tf_op jit(solution)/shard_map/backward/pallas_call | solution.py:269
  102.0 3.5 %all-to-all-done.2 = f32[8,10,8,128]{3,2,1,0:T(8,128)S(1)} async-done(((f32[8,10,8,128]{3,2,1,0:T(8,128)}), f32[8,10,8,128]{3,2,1,0:T(8,128)S(1)}, u32[]{:S(2)}, u32[]{:S(2)}) %all-to-all-start.2) | async-done | bytes 327712 | tf_op jit(solution)/shard_map/all_to_all | solution.py:343
  105.6 21.0 %all_to_all.20 = f32[16,10,8,128]{3,2,1,0:T(8,128)S(1)} all-to-all(f32[16,10,8,128]{3,2,1,0:T(8,128)S(1)} %broadcast_in_dim.2), channel_id=1, replica_groups=mesh['y'=4,'xh'=2,'core'=2,'xl'=2,'z'=8] {'y','xh','core'}, dimensions={0} | all-to-all | bytes 1310720 | tf_op jit(solution)/shard_map/all_to_all | solution.py:350
  126.7 0.1 slice_reduce_fusion
  126.7 0.9 copy.23
  127.6 0.6 reshape_squeeze.3
  (42 shorter events, 0.6 us)
Async XLA Ops:
  7.2 3.5 %copy-start = (bf16[32,3,3,512]{3,0,2,1:T(8,128)(2,1)S(1)}, bf16[32,3,3,512]{3,0,2,1:T(8,128)(2,1)}, u32[]{:S(2)}) copy-start(bf16[32,3,3,512]{3,0,2,1:T(8,128)(2,1)} %param.5) | copy-start | bytes 884740
  7.2 50.2 %all-gather.3.cloned.1.call-start = ((), (), s32[]{:S(2)}) async-start(), calls=%async_computation.4 | async-start | bytes 2654208 | tf_op jit(solution)/shard_map/all_gather | solution.py:315
  7.2 8.2 %collective-permute-start.2 = (bf16[512,640]{1,0:T(8,128)(2,1)}, bf16[512,640]{1,0:T(8,128)(2,1)S(1)}, u32[]{:S(2)}, u32[]{:S(2)}) collective-permute-start(bf16[512,640]{1,0:T(8,128)(2,1)} %bitcast.28), channel_id=1, source_target_pairs={{0,16},{16,0},{1,17},{17,1},{2,18},{18,2},{3,19},{19,3},{4,20},{20... | collective-permute-start | bytes 1966088 | tf_op jit(solution)/shard_map/ppermute | solution.py:286
  10.6 4.9 %collective-permute-start.3 = (bf16[512,640]{1,0:T(8,128)(2,1)}, bf16[512,640]{1,0:T(8,128)(2,1)S(1)}, u32[]{:S(2)}, u32[]{:S(2)}) collective-permute-start(bf16[512,640]{1,0:T(8,128)(2,1)} %bitcast.33), channel_id=1, source_target_pairs={{0,16},{16,0},{1,17},{17,1},{2,18},{18,2},{3,19},{19,3},{4,20},{20... | collective-permute-start | bytes 1966088 | tf_op jit(solution)/shard_map/ppermute | solution.py:286
  10.7 4.8 %collective-permute-start.5 = (bf16[9,32,256]{2,1,0:T(8,128)(2,1)S(1)}, bf16[9,32,256]{2,1,0:T(8,128)(2,1)S(1)}, u32[]{:S(2)}, u32[]{:S(2)}) collective-permute-start(bf16[9,32,256]{2,1,0:T(8,128)(2,1)S(1)} %constant_dynamic-slice_fusion), channel_id=1, source_target_pairs={{0,8},{8,0},{1,9},{9,1},{2,10},{10,2},{3,11},{11,3},{4,12},{12,4},... | collective-permute-start | bytes 442376 | tf_op jit(solution)/shard_map/ppermute | solution.py:309
  10.8 1.1 copy-start.1
  11.9 1.1 copy-start.3
  13.0 13.5 %copy-start.2 = (bf16[512,1,640]{2,0,1:T(8,128)(2,1)S(1)}, bf16[512,1,640]{2,0,1:T(8,128)(2,1)}, u32[]{:S(2)}) copy-start(bf16[512,1,640]{2,0,1:T(8,128)(2,1)} %param.4) | copy-start | bytes 1966084
  13.0 13.5 %copy-start.4 = (bf16[512,1,640]{2,0,1:T(8,128)(2,1)S(1)}, bf16[512,1,640]{2,0,1:T(8,128)(2,1)}, u32[]{:S(2)}) copy-start(bf16[512,1,640]{2,0,1:T(8,128)(2,1)} %param.7) | copy-start | bytes 1966084
  13.8 0.7 copy-start.9
  14.5 1.7 %copy-start.7 = (bf16[640,128]{1,0:T(8,128)(2,1)}, bf16[640,128]{1,0:T(8,128)(2,1)S(1)}, u32[]{:S(2)}) copy-start(bf16[640,128]{1,0:T(8,128)(2,1)S(1)} %get-tuple-element.33) | copy-start | bytes 491524
  16.2 20.0 %collective-permute-start = (bf16[640,128]{1,0:T(8,128)(2,1)}, bf16[640,128]{1,0:T(8,128)(2,1)S(1)}, u32[]{:S(2)}, u32[]{:S(2)}) collective-permute-start(bf16[640,128]{1,0:T(8,128)(2,1)} %get-tuple-element.23), channel_id=1, source_target_pairs={{0,1},{1,2},{2,3},{3,4},{4,5},{5,6},{6,7},{7,8},{8,9},{9,10},{10,1... | collective-permute-start | bytes 491528 | tf_op jit(solution)/shard_map/ppermute | solution.py:316
  18.3 17.9 %collective-permute-start.1 = (bf16[640,128]{1,0:T(8,128)(2,1)}, bf16[640,128]{1,0:T(8,128)(2,1)S(1)}, u32[]{:S(2)}, u32[]{:S(2)}) collective-permute-start(bf16[640,128]{1,0:T(8,128)(2,1)} %copy-done.9), channel_id=1, source_target_pairs={{1,0},{2,1},{3,2},{4,3},{5,4},{6,5},{7,6},{8,7},{9,8},{10,9},{11,1... | collective-permute-start | bytes 491528 | tf_op jit(solution)/shard_map/ppermute | solution.py:317
  29.7 22.3 %all-to-all-start = ((f16[16,208,128]{2,1,0:T(8,128)(2,1)}), f16[16,208,128]{2,1,0:T(8,128)(2,1)}, u32[]{:S(2)}, u32[]{:S(2)}) async-start(f16[16,208,128]{2,1,0:T(8,128)(2,1)} %convert_element_type.16), calls=%async_computation | async-start | bytes 1703936 | tf_op jit(solution)/shard_map/all_to_all | solution.py:321
  36.3 1.7 %collective-permute-start.4 = (bf16[2,640,128]{2,1,0:T(8,128)(2,1)S(1)}, bf16[2,640,128]{2,1,0:T(8,128)(2,1)S(1)}, u32[]{:S(2)}, u32[]{:S(2)}) collective-permute-start(bf16[2,640,128]{2,1,0:T(8,128)(2,1)S(1)} %pad_maximum_fusion), channel_id=1, source_target_pairs={{0,16},{16,0},{1,17},{17,1},{2,18},{18,2},{3,19},{19,3},{4,20},{20... | collective-permute-start | bytes 983048 | tf_op jit(solution)/shard_map/ppermute | solution.py:286
  42.9 13.5 %copy-start.10 = (f32[512]{0:T(512)S(1)}, f32[512]{0:T(512)}, u32[]{:S(2)}) copy-start(f32[512]{0:T(512)} %param.6) | copy-start | bytes 6148
  52.0 33.3 %all-to-all-start.1 = ((f16[16,400,128]{2,1,0:T(8,128)(2,1)}), f16[16,400,128]{2,1,0:T(8,128)(2,1)}, u32[]{:S(2)}, u32[]{:S(2)}) async-start(f16[16,400,128]{2,1,0:T(8,128)(2,1)} %convert_element_type.17), calls=%async_computation.1 | async-start | bytes 3276800 | tf_op jit(solution)/shard_map/all_to_all | solution.py:327
  57.4 11.0 %copy-start.8 = (bf16[640,128]{1,0:T(8,128)(2,1)S(1)}, bf16[640,128]{1,0:T(8,128)(2,1)}, u32[]{:S(2)}) copy-start(bf16[640,128]{1,0:T(8,128)(2,1)} %copy-done.7) | copy-start | bytes 491524
  60.6 6.0 %collective-permute-start.6 = (bf16[2,2,9,32,256]{4,3,2,1,0:T(8,128)(2,1)}, bf16[2,2,9,32,256]{4,3,2,1,0:T(8,128)(2,1)S(1)}, u32[]{:S(2)}, u32[]{:S(2)}) collective-permute-start(bf16[2,2,9,32,256]{4,3,2,1,0:T(8,128)(2,1)} %get-tuple-element.47), channel_id=1, source_target_pairs={{0,16},{16,0},{1,17},{17,1},{2,18},{18,2},{3,19},{19,3},{4,20},{20... | collective-permute-start | bytes 1769480 | tf_op jit(solution)/shard_map/ppermute | solution.py:286
  63.9 2.8 %collective-permute-start.7 = (bf16[2,2,9,32,256]{4,3,2,1,0:T(8,128)(2,1)}, bf16[2,2,9,32,256]{4,3,2,1,0:T(8,128)(2,1)}, u32[]{:S(2)}, u32[]{:S(2)}) collective-permute-start(bf16[2,2,9,32,256]{4,3,2,1,0:T(8,128)(2,1)} %get-tuple-element.46), channel_id=1, source_target_pairs={{0,16},{16,0},{1,17},{17,1},{2,18},{18,2},{3,19},{19,3},{4,20},{20... | collective-permute-start | bytes 1769480 | tf_op jit(solution)/shard_map/ppermute | solution.py:286
  63.9 3.7 %collective-permute-start.8 = (bf16[2,2,9,32,256]{4,3,2,1,0:T(8,128)(2,1)}, bf16[2,2,9,32,256]{4,3,2,1,0:T(8,128)(2,1)}, u32[]{:S(2)}, u32[]{:S(2)}) collective-permute-start(bf16[2,2,9,32,256]{4,3,2,1,0:T(8,128)(2,1)} %get-tuple-element.45), channel_id=1, source_target_pairs={{0,16},{16,0},{1,17},{17,1},{2,18},{18,2},{3,19},{19,3},{4,20},{20... | collective-permute-start | bytes 1769480 | tf_op jit(solution)/shard_map/ppermute | solution.py:286
  64.4 4.0 %collective-permute-start.9 = (bf16[2,2,9,32,256]{4,3,2,1,0:T(8,128)(2,1)}, bf16[2,2,9,32,256]{4,3,2,1,0:T(8,128)(2,1)}, u32[]{:S(2)}, u32[]{:S(2)}) collective-permute-start(bf16[2,2,9,32,256]{4,3,2,1,0:T(8,128)(2,1)} %get-tuple-element.44), channel_id=1, source_target_pairs={{0,16},{16,0},{1,17},{17,1},{2,18},{18,2},{3,19},{19,3},{4,20},{20... | collective-permute-start | bytes 1769480 | tf_op jit(solution)/shard_map/ppermute | solution.py:286
  68.4 16.9 %collective-permute-start.10 = (bf16[640,128]{1,0:T(8,128)(2,1)S(1)}, bf16[640,128]{1,0:T(8,128)(2,1)S(1)}, u32[]{:S(2)}, u32[]{:S(2)}) collective-permute-start(bf16[640,128]{1,0:T(8,128)(2,1)S(1)} %copy-done.8), channel_id=1, source_target_pairs={{0,1},{1,2},{2,3},{3,4},{4,5},{5,6},{6,7},{7,8},{8,9},{9,10},{10,1... | collective-permute-start | bytes 491528 | tf_op jit(solution)/shard_map/ppermute | solution.py:332
  71.2 14.2 %collective-permute-start.11 = (bf16[640,128]{1,0:T(8,128)(2,1)S(1)}, bf16[640,128]{1,0:T(8,128)(2,1)S(1)}, u32[]{:S(2)}, u32[]{:S(2)}) collective-permute-start(bf16[640,128]{1,0:T(8,128)(2,1)S(1)} %get-tuple-element.34), channel_id=1, source_target_pairs={{1,0},{2,1},{3,2},{4,3},{5,4},{6,5},{7,6},{8,7},{9,8},{10,9},{11,1... | collective-permute-start | bytes 491528 | tf_op jit(solution)/shard_map/ppermute | solution.py:333
  76.3 1.7 %copy-start.5 = (bf16[16,9,32,256]{3,2,1,0:T(8,128)(2,1)S(1)}, bf16[16,9,32,256]{3,2,1,0:T(8,128)(2,1)}, u32[]{:S(2)}) copy-start(bf16[16,9,32,256]{3,2,1,0:T(8,128)(2,1)} %all-gather.3.cloned.1.call-done) | copy-start | bytes 7077892
  89.1 16.3 %all-to-all-start.2 = ((f32[8,10,8,128]{3,2,1,0:T(8,128)}), f32[8,10,8,128]{3,2,1,0:T(8,128)S(1)}, u32[]{:S(2)}, u32[]{:S(2)}) async-start(f32[8,10,8,128]{3,2,1,0:T(8,128)} %copy.22), calls=%async_computation.2 | async-start | bytes 655360 | tf_op jit(solution)/shard_map/all_to_all | solution.py:343
  92.6 1.7 %copy-start.6 = (bf16[16,9,32,256]{3,2,1,0:T(8,128)(2,1)S(1)}, bf16[16,9,32,256]{3,2,1,0:T(8,128)(2,1)}, u32[]{:S(2)}) copy-start(bf16[16,9,32,256]{3,2,1,0:T(8,128)(2,1)} %all-gather.3.cloned.1.call-done) | copy-start | bytes 7077892
Sparse Core Ops, SparseCore 0:
  16.3 40.8 all-gather.2
